TPU v7x, 512 devices: a whole 4x8x8 slice. The times are simulated.
512 devices in a mesh: seq: 64 (over x, z, core), grp: 2 (over y_hi), rep: 4 (over y_lo).
Axes of the slice: x: 4, y: 8 (y_hi: 2, y_lo: 4; y = y_hi * 4 + y_lo), z: 8, core: 2. Of those that a mesh axis runs over, the one named last changes fastest.
Arguments:
- queries: bfloat16 [8192, 4096], P(('rep', 'seq'), 'grp'), parts along dimension 0, may hold values from -6 to 6
- keys: bfloat16 [8192, 4096], P(('rep', 'seq'), 'grp'), parts along dimension 0, may hold values from -6 to 6
- values: bfloat16 [8192, 4096], P(('rep', 'seq'), 'grp'), parts along dimension 0, may hold values from -6 to 6
- q_gain: float32 [4096], P('grp'), may hold values from 0.1 to 1.9
- k_gain: float32 [4096], P('grp'), may hold values from 0.1 to 1.9
- clip_ids: int32 [8192], P(('rep', 'seq')), parts along dimension 0, may hold values from 0 to 3, never falling along the last dimension, each value on 1 to 1024 neighbouring positions
- features: bfloat16 [4, 128, 128, 384], P('rep', 'seq', 'grp'), parts along dimension 0, may hold values from -6 to 6
- frame_cache: bfloat16 [8, 128, 128, 384], P('rep', 'seq', 'grp'), parts along dimension 0, may hold values from -4 to 4
- feat_gain: float32 [384], replicated, may hold values from 0.1 to 1.9
- conv_weight: bfloat16 [10368, 384], P('seq'), may hold values from -0.0625 to 0.0625
Outputs:
- attended: bfloat16 [8192, 4096], P(('rep', 'seq'), 'grp'), parts along dimension 0
- decoded: bfloat16 [4, 128, 128, 384], P('rep', 'seq', 'grp'), parts along dimension 0
There are 4 independent parts, one for each index of `rep`. A program takes and returns all parts, laid end to end along the dimension named above; an argument that names none is the same for every part. Nothing has to cross between parts.
All inputs are finite; a program needn't handle non-finite values.
Results may differ from a plain program's by a relative error of at most 0.0084.
Values may be sent and summed in bfloat16 or wider, within the bound.
No kernel may reach another device: no remote copies, remote signals or barrier semaphores. Data moves between devices by JAX's collectives and lax.ppermute only.
A program may use at most 64 MiB of HBM per device.

v0:
```python
import math

import jax
import jax.numpy as jnp
from jax import lax
from jax.sharding import PartitionSpec as P

HEADS = 32
HEAD_DIM = 128


epsilon = 1e-06


def with_halo(cells, sides, width):
    for axis, dim in sides:
        count = lax.axis_size(axis)
        ends = count - 1
        head = lax.slice_in_dim(cells, 0, width, axis=dim)
        tail = lax.slice_in_dim(cells, cells.shape[dim] - width, cells.shape[dim], axis=dim)
        cells = jnp.concatenate(
            [
                lax.ppermute(tail, axis, [(i, (i + 1) % count) for i in range(ends)]),
                cells,
                lax.ppermute(head, axis, [((i + 1) % count, i) for i in range(ends)]),
            ],
            axis=dim,
        )
    return cells


def attend(query_rows, key_rows, value_rows, query_ids, key_ids, head_count):
    row_count = query_rows.shape[0]
    block_rows = math.gcd(row_count, 256)
    head_width = query_rows.shape[1] // head_count
    score_scale = 1.0 / math.sqrt(head_width)
    key_heads = key_rows.reshape(-1, head_count, head_width)
    value_heads = value_rows.reshape(-1, head_count, head_width)
    query_blocks = query_rows.reshape(row_count // block_rows, block_rows, head_count, head_width)
    id_blocks = query_ids.reshape(row_count // block_rows, block_rows)

    def one_block(pair_item):
        query_block, id_block = pair_item
        scores = (
            jnp.einsum("qhd,khd->hqk", query_block, key_heads, preferred_element_type=jnp.float32)
            * score_scale
        )
        same_clip = id_block[:, None] == key_ids[None, :]
        scores = jnp.where(same_clip[None], scores, -1e30)
        row_max = jnp.max(scores, axis=-1, keepdims=True)
        probs = jnp.exp(scores - row_max)
        row_total = jnp.sum(probs, axis=-1)
        mixed_out = jnp.einsum(
            "hqk,khd->qhd",
            probs.astype(jnp.bfloat16),
            value_heads,
            preferred_element_type=jnp.float32,
        )
        normed = mixed_out / jnp.transpose(row_total)[:, :, None]
        return normed.astype(jnp.bfloat16).reshape(block_rows, head_count * head_width)

    return lax.map(one_block, (query_blocks, id_blocks)).reshape(row_count, head_count * head_width)


def shards(
    queries, keys, values, q_gain, k_gain, clip_ids, features, frame_cache, feat_gain, conv_weight
):
    tok_rows = queries.shape[0]
    local_cols = queries.shape[1]
    full_width = HEADS * HEAD_DIM
    q_float = queries.astype(jnp.float32)
    k_float = keys.astype(jnp.float32)
    q_total, k_total = lax.psum(
        (jnp.sum(q_float * q_float, axis=-1), jnp.sum(k_float * k_float, axis=-1)), "grp"
    )
    q_norm = (q_float * lax.rsqrt(q_total[:, None] / full_width + epsilon) * q_gain).astype(
        jnp.bfloat16
    )
    k_norm = (k_float * lax.rsqrt(k_total[:, None] / full_width + epsilon) * k_gain).astype(
        jnp.bfloat16
    )
    devices = lax.axis_size("seq")
    local_heads = local_cols // HEAD_DIM
    heads_here = max(local_heads // devices, 1)
    head_groups = local_heads // heads_here
    copy_count = devices // head_groups
    span_cols = heads_here * HEAD_DIM
    part_rows = tok_rows // copy_count
    my_part = lax.axis_index("seq") % copy_count
    all_ids = lax.all_gather(clip_ids, "seq", axis=0, tiled=True)
    id_grid = all_ids.reshape(devices, copy_count, part_rows)
    query_ids = lax.dynamic_index_in_dim(id_grid, my_part, 1, keepdims=False).reshape(-1)
    split_queries = (
        q_norm.reshape(copy_count, part_rows, head_groups, span_cols)
        .transpose(2, 0, 1, 3)
        .reshape(devices, part_rows, span_cols)
    )

    def full_rows(data):
        spread = data.reshape(tok_rows, head_groups, span_cols).transpose(1, 0, 2)
        return jnp.repeat(spread, copy_count, axis=0)

    got_q, got_k, got_v = (
        lax.all_to_all(split_queries, "seq", split_axis=0, concat_axis=1, tiled=True),
        lax.all_to_all(full_rows(k_norm), "seq", split_axis=0, concat_axis=1, tiled=True),
        lax.all_to_all(full_rows(values), "seq", split_axis=0, concat_axis=1, tiled=True),
    )
    head_out = attend(got_q[0], got_k[0], got_v[0], query_ids, all_ids, heads_here)
    outgoing = head_out.reshape(devices, 1, part_rows, span_cols)
    returned = lax.all_to_all(outgoing, "seq", split_axis=0, concat_axis=1, tiled=True)
    attended = (
        returned.reshape(head_groups, copy_count, part_rows, span_cols)
        .transpose(1, 2, 0, 3)
        .reshape(tok_rows, local_cols)
    )
    frame_count, tile_rows, tile_cols, channels = features.shape
    feat_float = features.astype(jnp.float32)
    scaled = (
        feat_float
        * lax.rsqrt(jnp.mean(feat_float * feat_float, axis=-1, keepdims=True) + epsilon)
        * feat_gain
    )
    activated = jax.nn.silu(scaled).astype(jnp.bfloat16)
    stacked = jnp.concatenate([frame_cache, activated], axis=0)
    padded = with_halo(stacked, (("seq", 1), ("grp", 2)), 1)
    shifted = []
    for time_off in range(3):
        for row_off in range(3):
            for col_off in range(3):
                shifted.append(
                    padded[
                        time_off : time_off + frame_count,
                        row_off : row_off + tile_rows,
                        col_off : col_off + tile_cols,
                    ]
                )
    cell_count = frame_count * tile_rows * tile_cols
    patches = jnp.stack(shifted, axis=3).reshape(cell_count, 27 * channels)
    convolved = jnp.dot(
        patches,
        lax.all_gather(conv_weight, "seq", axis=0, tiled=True),
        preferred_element_type=jnp.float32,
    )
    decoded = (feat_float + convolved.reshape(features.shape)).astype(jnp.bfloat16)
    return (attended, decoded)


def solution(mesh):
    placed = (
        P(("rep", "seq"), "grp"),
        P(("rep", "seq"), "grp"),
        P(("rep", "seq"), "grp"),
        P("grp"),
        P("grp"),
        P(("rep", "seq")),
        P("rep", "seq", "grp", None),
        P("rep", "seq", "grp", None),
        P(),
        P("seq", None),
    )
    return jax.shard_map(
        shards,
        mesh=mesh,
        in_specs=placed,
        out_specs=(P(("rep", "seq"), "grp"), P("rep", "seq", "grp", None)),
        check_vma=False,
    )
```

profile of v0, /device:TPU:1, one launch (start us, length us, event | category | flops | bytes accessed | tf_op | source)
XLA Modules:
  0.0 186.8 jit_solution(8120972171622714617)
XLA Ops:
  7.9 1.0 fusion.16
  9.0 1.0 fusion.19
  10.0 8.7 %all-reduce.1 = (f32[32]{0:T(128)S(1)}, f32[32]{0:T(128)S(1)}) all-reduce(f32[32]{0:T(128)S(1)} %fusion.16, f32[32]{0:T(128)S(1)} %fusion.19), channel_id=1, replica_groups=mesh['seq'=64,'grp'=2,'rep'=4] {'grp'}, use_global_device_ids=true, to_apply=%region_1.0 | all-reduce | flops 64 | bytes 512 | tf_op jit(solution)/shard_map/psum | solution.py:73
  20.4 15.0 %all-to-all-start = ((bf16[64,8,128]{2,1,0:T(8,128)(2,1)}), bf16[64,8,128]{2,1,0:T(8,128)(2,1)S(1)}, u32[]{:S(2)}, u32[]{:S(2)}) async-start(bf16[64,8,128]{2,1,0:T(8,128)(2,1)} %bitcast.11), calls=%async_computation | async-start | bytes 262144 | tf_op jit(solution)/shard_map/all_to_all | solution.py:104
  36.4 1.0 fusion.29
  38.5 3.5 %collective-permute-start = (bf16[3,1,64,384]{3,2,1,0:T(8,128)(2,1)S(1)}, bf16[3,1,64,384]{3,2,1,0:T(8,128)(2,1)S(1)}, u32[]{:S(2)}, u32[]{:S(2)}) collective-permute-start(bf16[3,1,64,384]{3,2,1,0:T(8,128)(2,1)S(1)} %get-tuple-element.83), channel_id=1, source_target_pairs={{0,8},{8,16},{16,24},{24,32},{32,40},{40,48},{48,56},{56,64},{64,7... | collective-permute-start | bytes 442376 | tf_op jit(solution)/shard_map/ppermute | solution.py:23
  42.0 1.9 %collective-permute-start.1 = (bf16[3,1,64,384]{3,2,1,0:T(8,128)(2,1)S(1)}, bf16[3,1,64,384]{3,2,1,0:T(8,128)(2,1)S(1)}, u32[]{:S(2)}, u32[]{:S(2)}) collective-permute-start(bf16[3,1,64,384]{3,2,1,0:T(8,128)(2,1)S(1)} %get-tuple-element.84), channel_id=1, source_target_pairs={{8,0},{16,8},{24,16},{32,24},{40,32},{48,40},{56,48},{64,56},{72,6... | collective-permute-start | bytes 442376 | tf_op jit(solution)/shard_map/ppermute | solution.py:25
  45.0 4.1 %collective-permute-done.1 = bf16[3,1,64,384]{3,2,1,0:T(8,128)(2,1)S(1)} collective-permute-done((bf16[3,1,64,384]{3,2,1,0:T(8,128)(2,1)S(1)}, bf16[3,1,64,384]{3,2,1,0:T(8,128)(2,1)S(1)}, u32[]{:S(2)}, u32[]{:S(2)}) %collective-permute-start.1) | collective-permute-done | bytes 147488 | tf_op jit(solution)/shard_map/ppermute | solution.py:25
  49.9 1.3 collective-permute-start.3
  51.2 7.9 %collective-permute-start.2 = (bf16[3,4,1,384]{3,2,1,0:T(2,128)(2,1)S(1)}, bf16[3,4,1,384]{3,2,1,0:T(2,128)(2,1)S(1)}, u32[]{:S(2)}, u32[]{:S(2)}) collective-permute-start(bf16[3,4,1,384]{3,2,1,0:T(2,128)(2,1)S(1)} %get-tuple-element.82), channel_id=1, source_target_pairs={{0,4},{1,5},{2,6},{3,7},{8,12},{9,13},{10,14},{11,15},{16,20},{17,... | collective-permute-start | bytes 27656 | tf_op jit(solution)/shard_map/ppermute | solution.py:23
  59.2 1.2 dynamic-slice
  61.3 16.5 %all-reduce = s32[2048]{0:T(1024)S(1)} all-reduce(s32[2048]{0:T(1024)S(1)} %dynamic-update-slice), channel_id=1, replica_groups=mesh['seq'=64,'grp'=2,'rep'=4] {'seq'}, use_global_device_ids=true, to_apply=%add | all-reduce | flops 2048 | bytes 16384
  88.6 12.5 %all-to-all-start.2 = ((bf16[64,32,128]{2,1,0:T(8,128)(2,1)}), bf16[64,32,128]{2,1,0:T(8,128)(2,1)S(1)}, u32[]{:S(2)}, u32[]{:S(2)}) async-start(bf16[64,32,128]{2,1,0:T(8,128)(2,1)} %bitcast.18), calls=%async_computation.2 | async-start | bytes 1048576 | tf_op jit(solution)/shard_map/all_to_all | solution.py:106
  105.1 13.4 %all-to-all-done.2 = bf16[64,32,128]{2,1,0:T(8,128)(2,1)S(1)} async-done(((bf16[64,32,128]{2,1,0:T(8,128)(2,1)}), bf16[64,32,128]{2,1,0:T(8,128)(2,1)S(1)}, u32[]{:S(2)}, u32[]{:S(2)}) %all-to-all-start.2) | async-done | bytes 524320 | tf_op jit(solution)/shard_map/all_to_all | solution.py:106
  119.4 6.3 %all-to-all-start.1 = ((bf16[64,32,128]{2,1,0:T(8,128)(2,1)}), bf16[64,32,128]{2,1,0:T(8,128)(2,1)S(1)}, u32[]{:S(2)}, u32[]{:S(2)}) async-start(bf16[64,32,128]{2,1,0:T(8,128)(2,1)} %bitcast.15), calls=%async_computation.1 | async-start | bytes 1048576 | tf_op jit(solution)/shard_map/all_to_all | solution.py:105
  129.1 13.9 %all-to-all-done.1 = bf16[64,32,128]{2,1,0:T(8,128)(2,1)S(1)} async-done(((bf16[64,32,128]{2,1,0:T(8,128)(2,1)}), bf16[64,32,128]{2,1,0:T(8,128)(2,1)S(1)}, u32[]{:S(2)}, u32[]{:S(2)}) %all-to-all-start.1) | async-done | bytes 524320 | tf_op jit(solution)/shard_map/all_to_all | solution.py:105
  143.0 4.3 %while.10 = (s32[]{:T(128)}, bf16[2,256,128]{2,1,0:T(8,128)(2,1)}, s32[2,256]{1,0:T(2,128)S(1)}, s32[2048]{0:T(1024)S(1)}, bf16[2,256,1,128]{3,1,2,0:T(8,128)(2,...) while((s32[]{:T(128)}, bf16[2,256,128]{2,1,0:T(8,128)(2,1)}, ...), condition=%wide.region_7.8_spmd, body=%wide.region_4.7_spmd.sunk | while | flops 272694784 | bytes 7487593 | solution.py:62
  144.0 1.2 fusion.71
  146.1 1.2 fusion.71
  147.3 6.3 %all-to-all-start.3 = ((bf16[64,1,8,128]{3,2,1,0:T(8,128)(2,1)}), bf16[64,1,8,128]{3,2,1,0:T(8,128)(2,1)S(1)}, u32[]{:S(2)}, u32[]{:S(2)}) async-start(bf16[64,1,8,128]{3,2,1,0:T(8,128)(2,1)} %bitcast.20), calls=%async_computation.3 | async-start | bytes 262144 | tf_op jit(solution)/shard_map/all_to_all | solution.py:110
  154.9 5.1 %copy.32 = bf16[1,2,64,27,384]{4,3,2,1,0:T(8,128)(2,1)} copy(bf16[1,2,64,27,384]{4,2,1,3,0:T(8,128)(2,1)} %fusion.33) | data formatting | bytes 5308416 | tf_op jit(solution)/shard_map/stack | solution.py:138
  160.0 4.2 %reshape.126 = bf16[2,64,10368]{2,1,0:T(8,128)(2,1)S(1)} reshape(bf16[1,2,64,27,384]{4,3,2,1,0:T(8,128)(2,1)} %copy.32) | data formatting | bytes 5308416 | tf_op jit(solution)/shard_map/reshape.82
  165.0 9.5 %reshape.134 = bf16[10368,384,1]{1,0,2:T(8,128)(2,1)} reshape(bf16[64,162,384]{2,1,0:T(8,128)(2,1)} %all-gather.3.cloned.1.call-done) | data formatting | bytes 15925248
  174.5 5.5 %fusion.15 = bf16[1,2,64,384]{3,2,1,0:T(8,128)(2,1)} fusion(bf16[2,64,10368]{2,1,0:T(8,128)(2,1)S(1)} %reshape.126, bf16[10368,384,1]{1,0,2:T(8,128)(2,1)} %reshape.134, bf16[1,2,64,384]{3,2,1,0:T(8,128)(2,1)S(1)} %copy-done.1), kind=kOutput, calls=%fused_computation.19 | convolution fusion | flops 1019363328 | bytes 10813440 | tf_op jit(solution)/shard_map/dot_general | solution.py:139
  (74 shorter events, 29.6 us)
Async XLA Ops:
  7.2 71.2 %copy-start = (bf16[2,2,64,384]{3,2,1,0:T(8,128)(2,1)S(1)}, bf16[2,2,64,384]{3,2,1,0:T(8,128)(2,1)}, u32[]{:S(2)}) copy-start(bf16[2,2,64,384]{3,2,1,0:T(8,128)(2,1)} %param.19) | copy-start | bytes 589828
  7.2 53.8 %copy-start.4 = (s32[32]{0:T(128)S(1)}, s32[32]{0:T(128)}, u32[]{:S(2)}) copy-start(s32[32]{0:T(128)} %param.17) | copy-start | bytes 388
  7.2 71.0 %copy-start.2 = (bf16[32,2048]{1,0:T(8,128)(2,1)S(1)}, bf16[32,2048]{1,0:T(8,128)(2,1)}, u32[]{:S(2)}) copy-start(bf16[32,2048]{1,0:T(8,128)(2,1)} %param.14) | copy-start | bytes 393220
  7.2 157.8 %all-gather.3.cloned.1.call-start = ((), (), s32[]{:S(2)}) async-start(), calls=%async_computation.4 | async-start | bytes 8386560 | tf_op jit(solution)/shard_map/all_gather | solution.py:141
  20.4 67.3 %all-to-all-start = ((bf16[64,8,128]{2,1,0:T(8,128)(2,1)}), bf16[64,8,128]{2,1,0:T(8,128)(2,1)S(1)}, u32[]{:S(2)}, u32[]{:S(2)}) async-start(bf16[64,8,128]{2,1,0:T(8,128)(2,1)} %bitcast.11), calls=%async_computation | async-start | bytes 262144 | tf_op jit(solution)/shard_map/all_to_all | solution.py:104
  38.5 6.5 %collective-permute-start = (bf16[3,1,64,384]{3,2,1,0:T(8,128)(2,1)S(1)}, bf16[3,1,64,384]{3,2,1,0:T(8,128)(2,1)S(1)}, u32[]{:S(2)}, u32[]{:S(2)}) collective-permute-start(bf16[3,1,64,384]{3,2,1,0:T(8,128)(2,1)S(1)} %get-tuple-element.83), channel_id=1, source_target_pairs={{0,8},{8,16},{16,24},{24,32},{32,40},{40,48},{48,56},{56,64},{64,7... | collective-permute-start | bytes 442376 | tf_op jit(solution)/shard_map/ppermute | solution.py:23
  42.0 7.1 %collective-permute-start.1 = (bf16[3,1,64,384]{3,2,1,0:T(8,128)(2,1)S(1)}, bf16[3,1,64,384]{3,2,1,0:T(8,128)(2,1)S(1)}, u32[]{:S(2)}, u32[]{:S(2)}) collective-permute-start(bf16[3,1,64,384]{3,2,1,0:T(8,128)(2,1)S(1)} %get-tuple-element.84), channel_id=1, source_target_pairs={{8,0},{16,8},{24,16},{32,24},{40,32},{48,40},{56,48},{64,56},{72,6... | collective-permute-start | bytes 442376 | tf_op jit(solution)/shard_map/ppermute | solution.py:25
  49.9 28.4 %collective-permute-start.3 = (bf16[3,4,1,384]{3,2,1,0:T(2,128)(2,1)S(1)}, bf16[3,4,1,384]{3,2,1,0:T(2,128)(2,1)S(1)}, u32[]{:S(2)}, u32[]{:S(2)}) collective-permute-start(bf16[3,4,1,384]{3,2,1,0:T(2,128)(2,1)S(1)} %get-tuple-element.81), channel_id=1, source_target_pairs={{4,0},{5,1},{6,2},{7,3},{12,8},{13,9},{14,10},{15,11},{20,16},{21,... | collective-permute-start | bytes 27656 | tf_op jit(solution)/shard_map/ppermute | solution.py:25
  51.2 27.1 %collective-permute-start.2 = (bf16[3,4,1,384]{3,2,1,0:T(2,128)(2,1)S(1)}, bf16[3,4,1,384]{3,2,1,0:T(2,128)(2,1)S(1)}, u32[]{:S(2)}, u32[]{:S(2)}) collective-permute-start(bf16[3,4,1,384]{3,2,1,0:T(2,128)(2,1)S(1)} %get-tuple-element.82), channel_id=1, source_target_pairs={{0,4},{1,5},{2,6},{3,7},{8,12},{9,13},{10,14},{11,15},{16,20},{17,... | collective-permute-start | bytes 27656 | tf_op jit(solution)/shard_map/ppermute | solution.py:23
  88.6 38.3 %copy-start.1 = (bf16[1,2,64,384]{3,2,1,0:T(8,128)(2,1)S(1)}, bf16[1,2,64,384]{3,2,1,0:T(8,128)(2,1)}, u32[]{:S(2)}) copy-start(bf16[1,2,64,384]{3,2,1,0:T(8,128)(2,1)} %param.18) | copy-start | bytes 294916
  88.6 38.3 %copy-start.3 = (f32[384]{0:T(512)S(1)}, f32[384]{0:T(512)}, u32[]{:S(2)}) copy-start(f32[384]{0:T(512)} %param.20) | copy-start | bytes 4612
  88.6 29.8 %all-to-all-start.2 = ((bf16[64,32,128]{2,1,0:T(8,128)(2,1)}), bf16[64,32,128]{2,1,0:T(8,128)(2,1)S(1)}, u32[]{:S(2)}, u32[]{:S(2)}) async-start(bf16[64,32,128]{2,1,0:T(8,128)(2,1)} %bitcast.18), calls=%async_computation.2 | async-start | bytes 1048576 | tf_op jit(solution)/shard_map/all_to_all | solution.py:106
  119.4 23.6 %all-to-all-start.1 = ((bf16[64,32,128]{2,1,0:T(8,128)(2,1)}), bf16[64,32,128]{2,1,0:T(8,128)(2,1)S(1)}, u32[]{:S(2)}, u32[]{:S(2)}) async-start(bf16[64,32,128]{2,1,0:T(8,128)(2,1)} %bitcast.15), calls=%async_computation.1 | async-start | bytes 1048576 | tf_op jit(solution)/shard_map/all_to_all | solution.py:105
  147.3 16.9 %all-to-all-start.3 = ((bf16[64,1,8,128]{3,2,1,0:T(8,128)(2,1)}), bf16[64,1,8,128]{3,2,1,0:T(8,128)(2,1)S(1)}, u32[]{:S(2)}, u32[]{:S(2)}) async-start(bf16[64,1,8,128]{3,2,1,0:T(8,128)(2,1)} %bitcast.20), calls=%async_computation.3 | async-start | bytes 262144 | tf_op jit(solution)/shard_map/all_to_all | solution.py:110
Sparse Core Ops, SparseCore 0:
  11.3 96.0 all-gather.2
where the time goes:
time: 188 us; the launch traced here: 187 us
  starting transfers between devices  54.7 us (29%)
  local copies, waits for them, and re-layouts  37.2 us (20%)
  waiting for transfers between devices  32.1 us (17%)
  blocking collectives  25.2 us (13%)
  between operations  14.9 us (8%)
  other arithmetic  13.7 us (7%)
  matrix products  8.88 us (5%)
    unnamed x36, local copies, waits for them, and re-layouts  24.1 us
    unnamed x1, blocking collectives  16.5 us
    all_to_all x1, starting transfers between devices, shards(): lax.all_to_all(split_queries, 'seq', split_axis=0, concat_axis=1, tiled=T...  15 us
    all_to_all x1, waiting for transfers between devices, shards(): lax.all_to_all(full_rows(k_norm), 'seq', split_axis=0, concat_axis=1, til...  13.9 us
    all_to_all x1, waiting for transfers between devices, shards(): lax.all_to_all(full_rows(values), 'seq', split_axis=0, concat_axis=1, til...  13.4 us
    all_to_all x1, starting transfers between devices, shards(): lax.all_to_all(full_rows(values), 'seq', split_axis=0, concat_axis=1, til...  12.5 us
    ppermute x2, starting transfers between devices, with_halo(): lax.ppermute(tail, axis, [(i, (i + 1) % count) for i in range(ends)])  11.4 us
    psum x1, blocking collectives, shards(): lax.psum((jnp.sum(q_float * q_float, axis=-1), jnp.sum(k_float * k_float,...  8.68 us
  transfers between devices with their start and end apart: 9, of which 3 were waited for; matrix products, arithmetic and copies ran while one was open for 24% of the time, Pallas kernels for 0%

commit v1 on v0

v1 whole, which is shorter than its diff:
```python
import functools
import math

import jax
import jax.numpy as jnp
from jax import lax
from jax.experimental import pallas as pl
from jax.experimental.pallas import tpu as pltpu
from jax.sharding import Mesh
from jax.sharding import PartitionSpec as P

HEADS = 32
HEAD_DIM = 128
CH = 384
WIDTH = HEADS * HEAD_DIM
EPS = 1e-06
SEQ = ("x", "z", "core")
HEAD_AXES = ("z", "core")
BF = jnp.bfloat16
F32 = jnp.float32
VMEM = pl.BlockSpec(memory_space=pltpu.VMEM)


def attention_kernel(tok, q_ref, own_ref, b_ref, c_ref, d_ref, qid_ref, out_ref):
    groups = q_ref.shape[0]
    count = groups * tok
    scale = 1.0 / math.sqrt(HEAD_DIM)
    q = q_ref[:, :tok, :].reshape(count, HEAD_DIM)
    keys, vals, ids = [], [], []
    for ref in (own_ref, b_ref, c_ref, d_ref):
        pairs = ref[: 2 * count, :].reshape(groups, 2 * tok, HEAD_DIM)
        keys.append(pairs[:, :tok].reshape(count, HEAD_DIM))
        vals.append(pairs[:, tok:].reshape(count, HEAD_DIM))
        rows = ref[2 * count : 2 * count + 16, :].astype(F32)
        ids.append(jnp.concatenate([rows[i : i + 1] for i in range(count // HEAD_DIM)], axis=1))
    step = 128
    for lo in range(0, count, step):
        q_id = qid_ref[lo : lo + step, :]
        scores = []
        for key, key_id in zip(keys, ids):
            s = lax.dot_general(
                q[lo : lo + step], key, (((1,), (1,)), ((), ())), preferred_element_type=F32
            )
            scores.append(jnp.where(q_id == key_id, s * scale, -1e30))
        top = functools.reduce(
            jnp.maximum, [jnp.max(s, axis=-1, keepdims=True) for s in scores]
        )
        total = jnp.zeros((step, 1), F32)
        mixed = jnp.zeros((step, HEAD_DIM), F32)
        for s, val in zip(scores, vals):
            probs = jnp.exp(s - top)
            total = total + jnp.sum(probs, axis=-1, keepdims=True)
            mixed = mixed + jnp.dot(probs.astype(BF), val, preferred_element_type=F32)
        out_ref[lo : lo + step, :] = (mixed / total).astype(BF)


SLOTS = 8


def conv_kernel(share, base_ref, slab_ref, own_ref, b_ref, c_ref, d_ref, out_ref, pad_ref, low_ref, high_ref):
    _, parts, _, high, cols, lanes = slab_ref.shape
    rows = high - 2
    cells = rows * cols
    half = SLOTS // 2
    pad_ref[...] = jnp.zeros_like(pad_ref)
    for p, ref in enumerate((own_ref, b_ref, c_ref, d_ref)):
        for j in range(SLOTS):
            pad_ref[j, :share, :128] = ref[j * share : (j + 1) * share, :]
            start = SLOTS * share + (j % half) * share
            pad_ref[j, :share, 128:] = ref[start : start + share, :]
        for part in range(parts):
            for side, total_ref in ((0, low_ref), (1, high_ref)):
                pieces = []
                for j in range(half):
                    tap = jnp.minimum(base_ref[p] + side * half + j, 26)
                    t, r, c = tap // 9, (tap // 3) % 3, tap % 3
                    pieces.append(
                        slab_ref[c, part, t, pl.ds(r, rows), :, :].reshape(cells, lanes)
                    )
                patches = jnp.concatenate(pieces, axis=1)
                weight = pad_ref[side * half : (side + 1) * half].reshape(half * lanes, 256)
                product = jnp.dot(patches, weight, preferred_element_type=F32)
                if p == 0:
                    total_ref[part] = product
                else:
                    total_ref[part] += product
    lane = lax.broadcasted_iota(jnp.int32, (cells // 2, 128), 1)
    for part in range(parts):
        low, top = low_ref[part], high_ref[part]
        out_ref[part, :cells, :] = (low[:, :128] + top[:, :128]).astype(BF)
        rest = low[:, 128:] + pltpu.roll(top[:, 128:], 64, axis=1)
        rest = jnp.where(lane < 64, rest[: cells // 2], pltpu.roll(rest[cells // 2 :], 64, axis=1))
        out_ref[part, cells:, :] = rest.astype(BF)


def ring(data, axis, by):
    count = lax.axis_size(axis)
    return lax.ppermute(data, axis, [(i, (i + by) % count) for i in range(count)])


def planes_of(data):
    count = lax.axis_size("x")
    return ring(data, "x", 1), ring(data, "x", count - 1), ring(data, "x", 2)


def exchange(data, axes):
    return lax.all_to_all(data, axes, split_axis=0, concat_axis=0, tiled=True)


def shards(
    queries, keys, values, q_gain, k_gain, clip_ids, features, frame_cache, feat_gain, conv_weight
):
    tok, local_cols = queries.shape
    heads = local_cols // HEAD_DIM
    planes = lax.axis_size("x")
    plane_tok = heads * tok
    deep, cores = lax.axis_size("z"), lax.axis_size("core")
    seq_count = planes * deep * cores
    me_x, me_core = lax.axis_index("x"), lax.axis_index("core")
    me_grp, me_rep = lax.axis_index("grp"), lax.axis_index("rep")
    parts = lax.axis_size("rep")
    order = jnp.stack([me_x, me_x - 1, me_x + 1, me_x + 2]) % planes

    q_f, k_f = queries.astype(F32), keys.astype(F32)
    sums = jnp.stack([jnp.sum(q_f * q_f, axis=-1), jnp.sum(k_f * k_f, axis=-1)])
    sums = sums + ring(sums, "grp", 1)

    lanes = 128
    share = CH // parts
    weight_rows = conv_weight.shape[0]
    first = (me_rep + 2 * me_core) % parts
    held = jnp.arange(48)[:, None]
    late = (me_core == 1) & (me_rep >= 2)
    source = jnp.where(
        held < 40,
        4 * (held + late.astype(jnp.int32)) + first,
        jnp.where((held == 40) & (first < 2), jnp.where(me_core == 1, first, 160 + first), -1),
    )
    pick = (source == jnp.arange(weight_rows)[None, :]).astype(BF)
    chosen = jnp.dot(pick, conv_weight, preferred_element_type=F32).astype(BF)
    halves = chosen.reshape(48, cores, CH // cores).transpose(1, 0, 2)
    last = halves[:, :, 128:]
    halves = jnp.concatenate(
        [halves[:, :, :128], jnp.concatenate([last[:, :24], last[:, 24:]], axis=2)], axis=1
    )
    sent_weight = jnp.broadcast_to(halves[None], (deep,) + halves.shape).reshape(-1, 72, 128)
    plane_weight = exchange(sent_weight, HEAD_AXES)

    scales = lax.rsqrt(sums / WIDTH + EPS)
    q_norm = (q_f * scales[0][:, None] * q_gain).astype(BF)
    k_norm = (k_f * scales[1][:, None] * k_gain).astype(BF)
    id_row = jnp.pad(clip_ids.astype(BF)[None, :], ((0, 7), (0, HEAD_DIM - tok)))

    def by_head(data):
        return data.reshape(tok, heads, HEAD_DIM).transpose(1, 0, 2)

    payload = jnp.concatenate(
        [
            by_head(q_norm),
            by_head(k_norm),
            by_head(values),
            jnp.broadcast_to(id_row[None], (heads,) + id_row.shape),
        ],
        axis=1,
    )
    got = exchange(payload, HEAD_AXES)
    ids_got = got[:, 3 * tok, :tok].reshape(-1)
    id_block = jnp.pad(ids_got.reshape(-1, HEAD_DIM), ((0, 16 - plane_tok // HEAD_DIM), (0, 0)))
    key_vals = jnp.concatenate(
        [got[:, tok : 3 * tok, :].reshape(2 * plane_tok, HEAD_DIM), id_block], axis=0
    )

    slot = jnp.arange(deep * cores * 48)
    spot, item = slot // 48, slot % 48
    target = 81 * (spot // cores) + jnp.where(item == 40, 40, item + 41 * (spot % cores))
    target = jnp.where(item > 40, -1, target + (648 * me_x) % share)
    place = (jnp.arange(SLOTS * share)[:, None] == target[None, :]).astype(BF)
    place = place.reshape(SLOTS * share, deep * cores, 48)
    main = plane_weight[:, :48, :]
    rest = plane_weight[:, 48:, :]

    def placed_rows(at, data):
        return lax.dot_general(
            at, data, (((1, 2), (0, 1)), ((), ())), preferred_element_type=F32
        ).astype(BF)

    last_cols = (
        placed_rows(place[:, :, :24], rest)[:, :64] + placed_rows(place[:, :, 24:], rest)[:, 64:]
    )
    split = SLOTS * share // 2
    my_weight = jnp.concatenate(
        [
            placed_rows(place, main),
            jnp.concatenate([last_cols[:split], last_cols[split:]], axis=1),
        ],
        axis=0,
    )
    weights = (my_weight,) + planes_of(my_weight)
    taps = (27 * order) // planes

    others = planes_of(key_vals)
    head_out = pl.pallas_call(
        functools.partial(attention_kernel, tok),
        out_shape=jax.ShapeDtypeStruct((plane_tok, HEAD_DIM), BF),
        in_specs=[VMEM] * 6,
        out_specs=VMEM,
        compiler_params=pltpu.CompilerParams(vmem_limit_bytes=40 << 20),
        cost_estimate=pl.CostEstimate(
            flops=2 * 2 * plane_tok * plane_tok * planes * HEAD_DIM,
            bytes_accessed=planes * plane_tok * HEAD_DIM * 4,
            transcendentals=plane_tok * plane_tok * planes,
        ),
        name="attention",
    )(got, key_vals, *others, ids_got.astype(F32)[:, None])
    returned = exchange(head_out.reshape(heads, tok, HEAD_DIM), HEAD_AXES)
    attended = returned.transpose(1, 0, 2).reshape(tok, local_cols)

    frames, tile_rows, tile_cols, _ = features.shape
    feat_f = features.astype(F32)
    scaled = (
        feat_f
        * lax.rsqrt(jnp.mean(feat_f * feat_f, axis=-1, keepdims=True) + EPS)
        * feat_gain
    )
    activated = jax.nn.silu(scaled).astype(BF)
    stacked = jnp.concatenate([frame_cache, activated], axis=0).reshape(-1, CH)
    lane = jnp.arange(parts * lanes)
    chan = jnp.where(lane % lanes < share, parts * (lane % lanes) + lane // lanes, -1)
    sort = (jnp.arange(CH)[:, None] == chan[None, :]).astype(BF)
    sorted_cells = jnp.dot(stacked, sort, preferred_element_type=F32).astype(BF)
    outgoing = sorted_cells.reshape(-1, parts, lanes).transpose(1, 0, 2)
    cells = exchange(outgoing, "rep").reshape(parts, 3, tile_rows, tile_cols, lanes)
    is_upper = me_core == 0
    outer = jnp.where(is_upper, cells[:, :, :1], cells[:, :, -1:])
    pairs = [(s, s - 1 if s % 2 == 0 else s + 1) for s in range(1, seq_count - 1)]
    beyond = lax.ppermute(outer, SEQ, pairs)
    mine = jnp.where(
        is_upper,
        jnp.concatenate([beyond, cells], axis=2),
        jnp.concatenate([cells, beyond], axis=2),
    )
    theirs = ring(mine, "core", 1)
    tall = jnp.where(
        is_upper,
        jnp.concatenate([mine, theirs], axis=2),
        jnp.concatenate([theirs, mine], axis=2),
    )
    is_left = me_grp == 0
    edge = jnp.where(is_left, tall[:, :, :, -1:], tall[:, :, :, :1])
    beside = ring(edge, "grp", 1)
    nothing = jnp.zeros_like(beside)
    wide = jnp.concatenate(
        [jnp.where(is_left, nothing, beside), tall, jnp.where(is_left, beside, nothing)], axis=3
    )
    slab = jnp.stack([wide[:, :, :, c : c + tile_cols] for c in range(3)])
    chip_cells = cores * tile_rows * tile_cols
    partial = pl.pallas_call(
        functools.partial(conv_kernel, share),
        out_shape=jax.ShapeDtypeStruct((parts, chip_cells + chip_cells // 2, 128), BF),
        in_specs=[pl.BlockSpec(memory_space=pltpu.SMEM)] + [VMEM] * 5,
        out_specs=VMEM,
        scratch_shapes=[
            pltpu.VMEM((SLOTS, lanes, 256), BF),
            pltpu.VMEM((parts, chip_cells, 256), F32),
            pltpu.VMEM((parts, chip_cells, 256), F32),
        ],
        compiler_params=pltpu.CompilerParams(vmem_limit_bytes=48 << 20),
        cost_estimate=pl.CostEstimate(
            flops=2 * parts * chip_cells * 32 * lanes * 256,
            bytes_accessed=27 * lanes * CH,
            transcendentals=0,
        ),
        name="convolution",
    )(taps.astype(jnp.int32), slab, *weights)
    sums_back = jnp.sum(exchange(partial, "rep").astype(F32), axis=0)
    tile_cells = tile_rows * tile_cols
    main_cols = sums_back[:chip_cells].reshape(cores, tile_cells, 128)
    last_cols = sums_back[chip_cells:].reshape(tile_cells, cores, 64).transpose(1, 0, 2)
    both = jnp.concatenate([main_cols, last_cols], axis=2)
    keep = jnp.where(is_upper, both[0], both[1])
    give = jnp.where(is_upper, both[1], both[0]).astype(BF)
    take = ring(give, "core", 1).astype(F32)
    convolved = jnp.where(
        is_upper,
        jnp.concatenate([keep, take], axis=1),
        jnp.concatenate([take, keep], axis=1),
    ).reshape(features.shape)
    decoded = (feat_f + convolved).astype(BF)
    return (attended, decoded)


def solution(mesh):
    grid = Mesh(
        mesh.devices.reshape((4, 8, 2) + mesh.devices.shape[1:]), ("x", "z", "core", "grp", "rep")
    )
    tokens = P(("rep",) + SEQ, "grp")
    image = P("rep", SEQ, "grp", None)
    placed = (
        tokens,
        tokens,
        tokens,
        P("grp"),
        P("grp"),
        P(("rep",) + SEQ),
        image,
        image,
        P(),
        P(SEQ, None),
    )
    return jax.shard_map(
        shards, mesh=grid, in_specs=placed, out_specs=(tokens, image), check_vma=False
    )
```

time: 188 us -> 142 us (0.76)
  local copies, waits for them, and re-layouts: 37.2 us -> 3.34 us
  blocking collectives: 25.2 us -> 0 us
  starting transfers between devices: 54.7 us -> 70.2 us
  between operations: 14.9 us -> 1.34 us
  waiting for transfers between devices: 32.1 us -> 43.3 us
  Pallas kernels: 0 us -> 6.83 us
  matrix products: 8.88 us -> 3.52 us
    ppermute x4 -> x11, starting transfers between devices: 14.7 us -> 42 us  [the longest x10 38.4 us: ring(): lax.ppermute(data, axis, [(i, (i + by) % count) for i in range(count)])]
    unnamed x36 -> x20, local copies, waits for them, and re-layouts: 24.1 us -> 0.06 us
    unnamed x1 -> x0, blocking collectives: 16.5 us -> none
    all_to_all x4 -> x5, starting transfers between devices: 40.1 us -> 28.2 us  [exchange(): return lax.all_to_all(data, axes, split_axis=0, concat_axis=0, tiled=True)]
    ppermute x4 -> x11, waiting for transfers between devices: 4.12 us -> 14.2 us  [the longest x1 9.41 us: shards(): beyond = lax.ppermute(outer, SEQ, pairs)]
    another operation x4 -> x1, local copies, waits for them, and re-layouts: 10.1 us -> 0.09 us  [shards(): ids_got.reshape(-1, HEAD_DIM)]
    psum x1 -> x0, blocking collectives: 8.68 us -> none  [shards(): lax.psum((jnp.sum(q_float * q_float, axis=-1), jnp.sum(k_float * k_float,...]
    pallas_call x0 -> x2, Pallas kernels: none -> 6.83 us  [the longest x1 3.97 us: shards(): pl.pallas_call(functools.partial(conv_kernel, share), out_shape=jax.Shape...]
  transfers between devices with their start and end apart: 9 -> 16, of which waited for: 3 -> 6; matrix products, arithmetic and copies ran while one was open for 24% -> 11% of each run, Pallas kernels for 0% -> 5%
where the time goes in v1:
time: 142 us; the launch traced here: 141 us
  starting transfers between devices  70.2 us (49%)
  waiting for transfers between devices  43.3 us (30%)
  other arithmetic  12.2 us (9%)
  Pallas kernels  6.83 us (5%)
  matrix products  3.52 us (2%)
  local copies, waits for them, and re-layouts  3.34 us (2%)
    ppermute x10, starting transfers between devices, ring(): lax.ppermute(data, axis, [(i, (i + by) % count) for i in range(count)])  38.4 us
    all_to_all x5, waiting for transfers between devices, exchange(): return lax.all_to_all(data, axes, split_axis=0, concat_axis=0, tiled=True)  29.1 us
    all_to_all x5, starting transfers between devices, exchange(): return lax.all_to_all(data, axes, split_axis=0, concat_axis=0, tiled=True)  28.2 us
    ppermute x1, waiting for transfers between devices, shards(): beyond = lax.ppermute(outer, SEQ, pairs)  9.41 us
    ppermute x10, waiting for transfers between devices, ring(): lax.ppermute(data, axis, [(i, (i + by) % count) for i in range(count)])  4.78 us
    pallas_call x1, Pallas kernels, shards(): pl.pallas_call(functools.partial(conv_kernel, share), out_shape=jax.Shape...  3.97 us
    ppermute x1, starting transfers between devices, shards(): beyond = lax.ppermute(outer, SEQ, pairs)  3.55 us
    select_n x2, other arithmetic, shards(): jnp.where(is_upper, jnp.concatenate([mine, theirs], axis=2), jnp.concaten...  3.29 us
  transfers between devices with their start and end apart: 16, of which 6 were waited for; matrix products, arithmetic and copies ran while one was open for 11% of the time, Pallas kernels for 5%

profile of v1, /device:TPU:1, one launch (start us, length us, event | category | flops | bytes accessed | tf_op | source)
XLA Modules:
  0.0 140.7 jit_solution(15727334949893770769)
XLA Ops:
  2.9 8.3 %collective-permute-start = (f32[2,32]{1,0:T(2,128)S(1)}, f32[2,32]{1,0:T(2,128)S(1)}, u32[]{:S(2)}, u32[]{:S(2)}) collective-permute-start(f32[2,32]{1,0:T(2,128)S(1)} %pad_maximum_fusion.6), channel_id=1, source_target_pairs={{0,4},{4,0},{1,5},{5,1},{2,6},{6,2},{3,7},{7,3},{8,12},{12,8},{9,1... | collective-permute-start | bytes 776 | tf_op jit(solution)/shard_map/ppermute | solution.py:98
  13.3 11.3 %all-to-all-start.3 = ((bf16[16,72,128]{2,1,0:T(8,128)(2,1)}), bf16[16,72,128]{2,1,0:T(8,128)(2,1)S(1)}, u32[]{:S(2)}, u32[]{:S(2)}) async-start(bf16[16,72,128]{2,1,0:T(8,128)(2,1)} %bitcast.23), calls=%async_computation.3 | async-start | bytes 589824 | tf_op jit(solution)/shard_map/all_to_all | solution.py:107
  28.0 9.0 %all-to-all-done.3 = bf16[16,72,128]{2,1,0:T(8,128)(2,1)S(1)} async-done(((bf16[16,72,128]{2,1,0:T(8,128)(2,1)}), bf16[16,72,128]{2,1,0:T(8,128)(2,1)S(1)}, u32[]{:S(2)}, u32[]{:S(2)}) %all-to-all-start.3) | async-done | bytes 294944 | tf_op jit(solution)/shard_map/all_to_all | solution.py:107
  37.0 3.5 %all-to-all-start.2 = ((bf16[4,384,128]{2,1,0:T(8,128)(2,1)}), bf16[4,384,128]{2,1,0:T(8,128)(2,1)S(1)}, u32[]{:S(2)}, u32[]{:S(2)}) async-start(bf16[4,384,128]{2,1,0:T(8,128)(2,1)} %bitcast.75), calls=%async_computation.2 | async-start | bytes 786432 | tf_op jit(solution)/shard_map/all_to_all | solution.py:107
  41.7 10.9 %all-to-all-done.2 = bf16[4,384,128]{2,1,0:T(8,128)(2,1)S(1)} async-done(((bf16[4,384,128]{2,1,0:T(8,128)(2,1)}), bf16[4,384,128]{2,1,0:T(8,128)(2,1)S(1)}, u32[]{:S(2)}, u32[]{:S(2)}) %all-to-all-start.2) | async-done | bytes 393248 | tf_op jit(solution)/shard_map/all_to_all | solution.py:107
  52.6 3.7 %all-to-all-start = ((bf16[16,104,128]{2,1,0:T(8,128)(2,1)}), bf16[16,104,128]{2,1,0:T(8,128)(2,1)S(1)}, u32[]{:S(2)}, u32[]{:S(2)}) async-start(bf16[16,104,128]{2,1,0:T(8,128)(2,1)} %pad_maximum_fusion.3), calls=%async_computation | async-start | bytes 851968 | tf_op jit(solution)/shard_map/all_to_all | solution.py:107
  57.3 3.5 %collective-permute-start.4 = (bf16[4,3,1,64,128]{4,3,2,1,0:T(8,128)(2,1)S(1)}, bf16[4,3,1,64,128]{4,3,2,1,0:T(8,128)(2,1)S(1)}, u32[]{:S(2)}, u32[]{:S(2)}) collective-permute-start(bf16[4,3,1,64,128]{4,3,2,1,0:T(8,128)(2,1)S(1)} %slice_select_fusion), channel_id=1, source_target_pairs={{8,16},{16,8},{24,32},{32,24},{40,48},{48,40},{56,64},{64,56},{72,... | collective-permute-start | bytes 589832 | tf_op jit(solution)/shard_map/ppermute | solution.py:236
  60.9 9.4 %collective-permute-done.4 = bf16[4,3,1,64,128]{4,3,2,1,0:T(8,128)(2,1)S(1)} collective-permute-done((bf16[4,3,1,64,128]{4,3,2,1,0:T(8,128)(2,1)S(1)}, bf16[4,3,1,64,128]{4,3,2,1,0:T(8,128)(2,1)S(1)}, u32[]{:S(2)}, u32[]{:S(2)}) %collective-permute-start.4) | collective-permute-done | bytes 196640 | tf_op jit(solution)/shard_map/ppermute | solution.py:236
  71.2 1.9 %collective-permute-start.5 = (bf16[4,3,3,64,128]{4,3,2,1,0:T(8,128)(2,1)}, bf16[4,3,3,64,128]{4,3,2,1,0:T(8,128)(2,1)}, u32[]{:S(2)}, u32[]{:S(2)}) collective-permute-start(bf16[4,3,3,64,128]{4,3,2,1,0:T(8,128)(2,1)} %maximum_select_fusion.2), channel_id=1, source_target_pairs={{0,8},{8,0},{1,9},{9,1},{2,10},{10,2},{3,11},{11,3},{4,12},{12,4},... | collective-permute-start | bytes 1769480 | tf_op jit(solution)/shard_map/ppermute | solution.py:98
  73.3 4.8 %collective-permute-start.1 = (bf16[1040,128]{1,0:T(8,128)(2,1)S(1)}, bf16[1040,128]{1,0:T(8,128)(2,1)S(1)}, u32[]{:S(2)}, u32[]{:S(2)}) collective-permute-start(bf16[1040,128]{1,0:T(8,128)(2,1)S(1)} %fusion.8.own_ref), channel_id=1, source_target_pairs={{0,128},{128,256},{256,384},{384,0},{1,129},{129,257},{257,385},{3... | collective-permute-start | bytes 798728 | tf_op jit(solution)/shard_map/ppermute | solution.py:98
  78.2 3.5 %collective-permute-start.2 = (bf16[1040,128]{1,0:T(8,128)(2,1)S(1)}, bf16[1040,128]{1,0:T(8,128)(2,1)S(1)}, u32[]{:S(2)}, u32[]{:S(2)}) collective-permute-start(bf16[1040,128]{1,0:T(8,128)(2,1)S(1)} %fusion.8.own_ref), channel_id=1, source_target_pairs={{0,384},{128,0},{256,128},{384,256},{1,385},{129,1},{257,129},{385... | collective-permute-start | bytes 798728 | tf_op jit(solution)/shard_map/ppermute | solution.py:98
  81.6 3.3 %collective-permute-start.3 = (bf16[1040,128]{1,0:T(8,128)(2,1)S(1)}, bf16[1040,128]{1,0:T(8,128)(2,1)S(1)}, u32[]{:S(2)}, u32[]{:S(2)}) collective-permute-start(bf16[1040,128]{1,0:T(8,128)(2,1)S(1)} %fusion.8.own_ref), channel_id=1, source_target_pairs={{0,256},{128,384},{256,0},{384,128},{1,257},{129,385},{257,1},{385... | collective-permute-start | bytes 798728 | tf_op jit(solution)/shard_map/ppermute | solution.py:98
  85.1 2.5 %collective-permute-start.7 = (bf16[1152,128]{1,0:T(8,128)(2,1)S(1)}, bf16[1152,128]{1,0:T(8,128)(2,1)S(1)}, u32[]{:S(2)}, u32[]{:S(2)}) collective-permute-start(bf16[1152,128]{1,0:T(8,128)(2,1)S(1)} %maximum_maximum_fusion.own_ref), channel_id=1, source_target_pairs={{0,128},{128,256},{256,384},{384,0},{1,129},{129,257},{257,385},{3... | collective-permute-start | bytes 884744 | tf_op jit(solution)/shard_map/ppermute | solution.py:98
  88.8 4.0 %collective-permute-start.8 = (bf16[1152,128]{1,0:T(8,128)(2,1)S(1)}, bf16[1152,128]{1,0:T(8,128)(2,1)S(1)}, u32[]{:S(2)}, u32[]{:S(2)}) collective-permute-start(bf16[1152,128]{1,0:T(8,128)(2,1)S(1)} %maximum_maximum_fusion.own_ref), channel_id=1, source_target_pairs={{0,384},{128,0},{256,128},{384,256},{1,385},{129,1},{257,129},{385... | collective-permute-start | bytes 884744 | tf_op jit(solution)/shard_map/ppermute | solution.py:98
  92.8 2.2 %collective-permute-start.9 = (bf16[1152,128]{1,0:T(8,128)(2,1)S(1)}, bf16[1152,128]{1,0:T(8,128)(2,1)S(1)}, u32[]{:S(2)}, u32[]{:S(2)}) collective-permute-start(bf16[1152,128]{1,0:T(8,128)(2,1)S(1)} %maximum_maximum_fusion.own_ref), channel_id=1, source_target_pairs={{0,256},{128,384},{256,0},{384,128},{1,257},{129,385},{257,1},{385... | collective-permute-start | bytes 884744 | tf_op jit(solution)/shard_map/ppermute | solution.py:98
  95.1 2.9 %attention.1 = bf16[512,128]{1,0:T(8,128)(2,1)} custom-call(bf16[16,104,128]{2,1,0:T(8,128)(2,1)S(1)} %all-to-all-done.q_ref, bf16[1040,128]{1,0:T(8,128)(2,1)S(1)} %fusion.8.own_ref, bf16[1040,128]{1,0:T(8,128)(2,1)S(1)} %collective-permute-done.1.b_ref, bf16[1040,128]{1,0:T(8,128)(2,1)S(1)} %collective-permute-done.2.c_ref, ...), custom_call_target="tpu_custom_call" | custom-call | flops 536870912 | bytes 1048576 | tf_op jit(solution)/shard_map/attention/pallas_call | solution.py:202
  97.9 6.3 %all-to-all-start.1 = ((bf16[16,32,128]{2,1,0:T(8,128)(2,1)}), bf16[16,32,128]{2,1,0:T(8,128)(2,1)S(1)}, u32[]{:S(2)}, u32[]{:S(2)}) async-start(bf16[16,32,128]{2,1,0:T(8,128)(2,1)} %bitcast.9), calls=%async_computation.1 | async-start | bytes 262144 | tf_op jit(solution)/shard_map/all_to_all | solution.py:107
  104.2 1.8 %maximum_select_fusion = bf16[4,3,6,64,128]{4,3,2,1,0:T(8,128)(2,1)S(1)} fusion(bf16[4,3,3,64,128]{4,3,2,1,0:T(8,128)(2,1)} %collective-permute-done.5, bf16[4,3,3,64,128]{4,3,2,1,0:T(8,128)(2,1)} %maximum_select_fusion.2, pred[]{:T(512)S(6)} %eq.76), kind=kLoop, calls=%fused_computation.11 | loop fusion | flops 1769472 | bytes 2359297 | tf_op jit(solution)/shard_map/jit(_where)/select_n | solution.py:243
  106.1 3.2 %collective-permute-start.6 = (bf16[4,3,6,1,128]{4,3,2,1,0:T(2,128)(2,1)S(1)}, bf16[4,3,6,1,128]{4,3,2,1,0:T(2,128)(2,1)S(1)}, u32[]{:S(2)}, u32[]{:S(2)}) collective-permute-start(bf16[4,3,6,1,128]{4,3,2,1,0:T(2,128)(2,1)S(1)} %broadcast_select_fusion.2), channel_id=1, source_target_pairs={{0,4},{4,0},{1,5},{5,1},{2,6},{6,2},{3,7},{7,3},{8,12},{12,8},{9,1... | collective-permute-start | bytes 55304 | tf_op jit(solution)/shard_map/ppermute | solution.py:98
  110.7 4.0 %collective-permute-done.6 = bf16[4,3,6,1,128]{4,3,2,1,0:T(2,128)(2,1)S(1)} collective-permute-done((bf16[4,3,6,1,128]{4,3,2,1,0:T(2,128)(2,1)S(1)}, bf16[4,3,6,1,128]{4,3,2,1,0:T(2,128)(2,1)S(1)}, u32[]{:S(2)}, u32[]{:S(2)}) %collective-permute-start.6) | collective-permute-done | bytes 18464 | tf_op jit(solution)/shard_map/ppermute | solution.py:98
  116.6 4.0 %convolution.15 = bf16[4,384,128]{2,1,0:T(8,128)(2,1)} custom-call(s32[4]{0:T(128)S(1)} %and_select_fusion.1.base_ref, bf16[3,4,3,6,64,128]{5,4,3,2,1,0:T(8,128)(2,1)S(1)} %pad_maximum_fusion.slab_ref, bf16[1152,128]{1,0:T(8,128)(2,1)S(1)} %maximum_maximum_fusion.own_ref, bf16[1152,128]{1,0:T(8,128)(2,1)S(1)} %collective-permute-done.7.b_ref, ...), custom_call_target="tpu_custom_call" | custom-call | flops 2147483648 | bytes 1327104 | tf_op jit(solution)/shard_map/convolution/pallas_call | solution.py:257
  120.6 3.5 %all-to-all-start.4 = ((bf16[4,384,128]{2,1,0:T(8,128)(2,1)}), bf16[4,384,128]{2,1,0:T(8,128)(2,1)S(1)}, u32[]{:S(2)}, u32[]{:S(2)}) async-start(bf16[4,384,128]{2,1,0:T(8,128)(2,1)} %convolution.15), calls=%async_computation.4 | async-start | bytes 786432 | tf_op jit(solution)/shard_map/all_to_all | solution.py:107
  124.8 9.1 %all-to-all-done.4 = bf16[4,384,128]{2,1,0:T(8,128)(2,1)S(1)} async-done(((bf16[4,384,128]{2,1,0:T(8,128)(2,1)}), bf16[4,384,128]{2,1,0:T(8,128)(2,1)S(1)}, u32[]{:S(2)}, u32[]{:S(2)}) %all-to-all-start.4) | async-done | bytes 393248 | tf_op jit(solution)/shard_map/all_to_all | solution.py:107
  134.2 4.7 %collective-permute-start.10 = (bf16[128,192]{0,1:T(8,128)(2,1)S(1)}, bf16[128,192]{0,1:T(8,128)(2,1)S(1)}, u32[]{:S(2)}, u32[]{:S(2)}) collective-permute-start(bf16[128,192]{0,1:T(8,128)(2,1)S(1)} %fusion.31), channel_id=1, source_target_pairs={{0,8},{8,0},{1,9},{9,1},{2,10},{10,2},{3,11},{11,3},{4,12},{12,4},... | collective-permute-start | bytes 147464 | tf_op jit(solution)/shard_map/ppermute | solution.py:98
  (93 shorter events, 17.9 us)
Async XLA Ops:
  0.6 24.0 %copy-start = (bf16[32,2048]{1,0:T(8,128)(2,1)S(1)}, bf16[32,2048]{1,0:T(8,128)(2,1)}, u32[]{:S(2)}) copy-start(bf16[32,2048]{1,0:T(8,128)(2,1)} %param.12) | copy-start | bytes 393220
  0.6 24.0 %copy-start.9 = (s32[32]{0:T(128)S(1)}, s32[32]{0:T(128)}, u32[]{:S(2)}) copy-start(s32[32]{0:T(128)} %param.15) | copy-start | bytes 388
  0.7 24.1 %copy-start.2 = (bf16[1,2,64,384]{3,2,1,0:T(8,128)(2,1)S(1)}, bf16[1,2,64,384]{3,2,1,0:T(8,128)(2,1)}, u32[]{:S(2)}) copy-start(bf16[1,2,64,384]{3,2,1,0:T(8,128)(2,1)} %param.16) | copy-start | bytes 294916
  0.7 24.2 %copy-start.8 = (f32[384]{0:T(512)S(1)}, f32[384]{0:T(512)}, u32[]{:S(2)}) copy-start(f32[384]{0:T(512)} %param.18) | copy-start | bytes 4612
  0.7 24.3 %copy-start.5 = (bf16[2,2,64,384]{3,2,1,0:T(8,128)(2,1)S(1)}, bf16[2,2,64,384]{3,2,1,0:T(8,128)(2,1)}, u32[]{:S(2)}) copy-start(bf16[2,2,64,384]{3,2,1,0:T(8,128)(2,1)} %param.17) | copy-start | bytes 589828
  2.9 24.0 %collective-permute-start = (f32[2,32]{1,0:T(2,128)S(1)}, f32[2,32]{1,0:T(2,128)S(1)}, u32[]{:S(2)}, u32[]{:S(2)}) collective-permute-start(f32[2,32]{1,0:T(2,128)S(1)} %pad_maximum_fusion.6), channel_id=1, source_target_pairs={{0,4},{4,0},{1,5},{5,1},{2,6},{6,2},{3,7},{7,3},{8,12},{12,8},{9,1... | collective-permute-start | bytes 776 | tf_op jit(solution)/shard_map/ppermute | solution.py:98
  13.3 23.6 %all-to-all-start.3 = ((bf16[16,72,128]{2,1,0:T(8,128)(2,1)}), bf16[16,72,128]{2,1,0:T(8,128)(2,1)S(1)}, u32[]{:S(2)}, u32[]{:S(2)}) async-start(bf16[16,72,128]{2,1,0:T(8,128)(2,1)} %bitcast.23), calls=%async_computation.3 | async-start | bytes 589824 | tf_op jit(solution)/shard_map/all_to_all | solution.py:107
  25.0 1.9 %copy-start.3 = (bf16[32,2048]{1,0:T(8,128)(2,1)S(1)}, bf16[32,2048]{1,0:T(8,128)(2,1)}, u32[]{:S(2)}) copy-start(bf16[32,2048]{1,0:T(8,128)(2,1)} %param.11) | copy-start | bytes 393220
  25.1 1.9 %copy-start.4 = (bf16[32,2048]{1,0:T(8,128)(2,1)S(1)}, bf16[32,2048]{1,0:T(8,128)(2,1)}, u32[]{:S(2)}) copy-start(bf16[32,2048]{1,0:T(8,128)(2,1)} %param.10) | copy-start | bytes 393220
  37.0 15.6 %all-to-all-start.2 = ((bf16[4,384,128]{2,1,0:T(8,128)(2,1)}), bf16[4,384,128]{2,1,0:T(8,128)(2,1)S(1)}, u32[]{:S(2)}, u32[]{:S(2)}) async-start(bf16[4,384,128]{2,1,0:T(8,128)(2,1)} %bitcast.75), calls=%async_computation.2 | async-start | bytes 786432 | tf_op jit(solution)/shard_map/all_to_all | solution.py:107
  52.6 20.5 %all-to-all-start = ((bf16[16,104,128]{2,1,0:T(8,128)(2,1)}), bf16[16,104,128]{2,1,0:T(8,128)(2,1)S(1)}, u32[]{:S(2)}, u32[]{:S(2)}) async-start(bf16[16,104,128]{2,1,0:T(8,128)(2,1)} %pad_maximum_fusion.3), calls=%async_computation | async-start | bytes 851968 | tf_op jit(solution)/shard_map/all_to_all | solution.py:107
  57.3 13.0 %collective-permute-start.4 = (bf16[4,3,1,64,128]{4,3,2,1,0:T(8,128)(2,1)S(1)}, bf16[4,3,1,64,128]{4,3,2,1,0:T(8,128)(2,1)S(1)}, u32[]{:S(2)}, u32[]{:S(2)}) collective-permute-start(bf16[4,3,1,64,128]{4,3,2,1,0:T(8,128)(2,1)S(1)} %slice_select_fusion), channel_id=1, source_target_pairs={{8,16},{16,8},{24,32},{32,24},{40,48},{48,40},{56,64},{64,56},{72,... | collective-permute-start | bytes 589832 | tf_op jit(solution)/shard_map/ppermute | solution.py:236
  71.2 33.0 %collective-permute-start.5 = (bf16[4,3,3,64,128]{4,3,2,1,0:T(8,128)(2,1)}, bf16[4,3,3,64,128]{4,3,2,1,0:T(8,128)(2,1)}, u32[]{:S(2)}, u32[]{:S(2)}) collective-permute-start(bf16[4,3,3,64,128]{4,3,2,1,0:T(8,128)(2,1)} %maximum_select_fusion.2), channel_id=1, source_target_pairs={{0,8},{8,0},{1,9},{9,1},{2,10},{10,2},{3,11},{11,3},{4,12},{12,4},... | collective-permute-start | bytes 1769480 | tf_op jit(solution)/shard_map/ppermute | solution.py:98
  73.3 15.5 %collective-permute-start.1 = (bf16[1040,128]{1,0:T(8,128)(2,1)S(1)}, bf16[1040,128]{1,0:T(8,128)(2,1)S(1)}, u32[]{:S(2)}, u32[]{:S(2)}) collective-permute-start(bf16[1040,128]{1,0:T(8,128)(2,1)S(1)} %fusion.8.own_ref), channel_id=1, source_target_pairs={{0,128},{128,256},{256,384},{384,0},{1,129},{129,257},{257,385},{3... | collective-permute-start | bytes 798728 | tf_op jit(solution)/shard_map/ppermute | solution.py:98
  78.2 14.6 %collective-permute-start.2 = (bf16[1040,128]{1,0:T(8,128)(2,1)S(1)}, bf16[1040,128]{1,0:T(8,128)(2,1)S(1)}, u32[]{:S(2)}, u32[]{:S(2)}) collective-permute-start(bf16[1040,128]{1,0:T(8,128)(2,1)S(1)} %fusion.8.own_ref), channel_id=1, source_target_pairs={{0,384},{128,0},{256,128},{384,256},{1,385},{129,1},{257,129},{385... | collective-permute-start | bytes 798728 | tf_op jit(solution)/shard_map/ppermute | solution.py:98
  81.6 13.4 %collective-permute-start.3 = (bf16[1040,128]{1,0:T(8,128)(2,1)S(1)}, bf16[1040,128]{1,0:T(8,128)(2,1)S(1)}, u32[]{:S(2)}, u32[]{:S(2)}) collective-permute-start(bf16[1040,128]{1,0:T(8,128)(2,1)S(1)} %fusion.8.own_ref), channel_id=1, source_target_pairs={{0,256},{128,384},{256,0},{384,128},{1,257},{129,385},{257,1},{385... | collective-permute-start | bytes 798728 | tf_op jit(solution)/shard_map/ppermute | solution.py:98
  85.1 31.5 %collective-permute-start.7 = (bf16[1152,128]{1,0:T(8,128)(2,1)S(1)}, bf16[1152,128]{1,0:T(8,128)(2,1)S(1)}, u32[]{:S(2)}, u32[]{:S(2)}) collective-permute-start(bf16[1152,128]{1,0:T(8,128)(2,1)S(1)} %maximum_maximum_fusion.own_ref), channel_id=1, source_target_pairs={{0,128},{128,256},{256,384},{384,0},{1,129},{129,257},{257,385},{3... | collective-permute-start | bytes 884744 | tf_op jit(solution)/shard_map/ppermute | solution.py:98
  88.8 27.8 %collective-permute-start.8 = (bf16[1152,128]{1,0:T(8,128)(2,1)S(1)}, bf16[1152,128]{1,0:T(8,128)(2,1)S(1)}, u32[]{:S(2)}, u32[]{:S(2)}) collective-permute-start(bf16[1152,128]{1,0:T(8,128)(2,1)S(1)} %maximum_maximum_fusion.own_ref), channel_id=1, source_target_pairs={{0,384},{128,0},{256,128},{384,256},{1,385},{129,1},{257,129},{385... | collective-permute-start | bytes 884744 | tf_op jit(solution)/shard_map/ppermute | solution.py:98
  92.8 23.8 %collective-permute-start.9 = (bf16[1152,128]{1,0:T(8,128)(2,1)S(1)}, bf16[1152,128]{1,0:T(8,128)(2,1)S(1)}, u32[]{:S(2)}, u32[]{:S(2)}) collective-permute-start(bf16[1152,128]{1,0:T(8,128)(2,1)S(1)} %maximum_maximum_fusion.own_ref), channel_id=1, source_target_pairs={{0,256},{128,384},{256,0},{384,128},{1,257},{129,385},{257,1},{385... | collective-permute-start | bytes 884744 | tf_op jit(solution)/shard_map/ppermute | solution.py:98
  97.9 22.7 %all-to-all-start.1 = ((bf16[16,32,128]{2,1,0:T(8,128)(2,1)}), bf16[16,32,128]{2,1,0:T(8,128)(2,1)S(1)}, u32[]{:S(2)}, u32[]{:S(2)}) async-start(bf16[16,32,128]{2,1,0:T(8,128)(2,1)} %bitcast.9), calls=%async_computation.1 | async-start | bytes 262144 | tf_op jit(solution)/shard_map/all_to_all | solution.py:107
  104.2 5.1 %copy-start.1 = (bf16[1,4,3,3,64,128]{5,4,3,2,1,0:T(8,128)(2,1)S(1)}, bf16[1,4,3,3,64,128]{5,4,3,2,1,0:T(8,128)(2,1)}, u32[]{:S(2)}) copy-start(bf16[1,4,3,3,64,128]{5,4,3,2,1,0:T(8,128)(2,1)} %fusion.66) | copy-start | bytes 1769476
  106.1 8.6 %collective-permute-start.6 = (bf16[4,3,6,1,128]{4,3,2,1,0:T(2,128)(2,1)S(1)}, bf16[4,3,6,1,128]{4,3,2,1,0:T(2,128)(2,1)S(1)}, u32[]{:S(2)}, u32[]{:S(2)}) collective-permute-start(bf16[4,3,6,1,128]{4,3,2,1,0:T(2,128)(2,1)S(1)} %broadcast_select_fusion.2), channel_id=1, source_target_pairs={{0,4},{4,0},{1,5},{5,1},{2,6},{6,2},{3,7},{7,3},{8,12},{12,8},{9,1... | collective-permute-start | bytes 55304 | tf_op jit(solution)/shard_map/ppermute | solution.py:98
  120.6 13.3 %all-to-all-start.4 = ((bf16[4,384,128]{2,1,0:T(8,128)(2,1)}), bf16[4,384,128]{2,1,0:T(8,128)(2,1)S(1)}, u32[]{:S(2)}, u32[]{:S(2)}) async-start(bf16[4,384,128]{2,1,0:T(8,128)(2,1)} %convolution.15), calls=%async_computation.4 | async-start | bytes 786432 | tf_op jit(solution)/shard_map/all_to_all | solution.py:107
  134.2 5.6 %collective-permute-start.10 = (bf16[128,192]{0,1:T(8,128)(2,1)S(1)}, bf16[128,192]{0,1:T(8,128)(2,1)S(1)}, u32[]{:S(2)}, u32[]{:S(2)}) collective-permute-start(bf16[128,192]{0,1:T(8,128)(2,1)S(1)} %fusion.31), channel_id=1, source_target_pairs={{0,8},{8,0},{1,9},{9,1},{2,10},{10,2},{3,11},{11,3},{4,12},{12,4},... | collective-permute-start | bytes 147464 | tf_op jit(solution)/shard_map/ppermute | solution.py:98
  (2 other events, 3.8 us)

commit v2 on v1

v2 whole, which is shorter than its diff:
```python
import functools
import math

import jax
import jax.numpy as jnp
from jax import lax
from jax.experimental import pallas as pl
from jax.experimental.pallas import tpu as pltpu
from jax.sharding import Mesh
from jax.sharding import PartitionSpec as P

HEADS = 32
HEAD_DIM = 128
CH = 384
WIDTH = HEADS * HEAD_DIM
EPS = 1e-06
X = ("xh", "xl")
SEQ = ("xh", "xl", "z", "core")
HEAD_AXES = ("xl", "z")
BF = jnp.bfloat16
F32 = jnp.float32
VMEM = pl.BlockSpec(memory_space=pltpu.VMEM)


def attention_kernel(tok, q_ref, pair_ref, other_ref, qid_ref, out_ref):
    groups = q_ref.shape[0]
    count = groups * tok
    scale = 1.0 / math.sqrt(HEAD_DIM)
    q = q_ref[:, :tok, :].reshape(count, HEAD_DIM)
    keys, vals, ids = [], [], []
    for ref in (pair_ref.at[0], pair_ref.at[1], other_ref.at[0], other_ref.at[1]):
        pairs = ref[: 2 * count, :].reshape(groups, 2 * tok, HEAD_DIM)
        keys.append(pairs[:, :tok].reshape(count, HEAD_DIM))
        vals.append(pairs[:, tok:].reshape(count, HEAD_DIM))
        rows = ref[2 * count : 2 * count + 16, :].astype(F32)
        ids.append(jnp.concatenate([rows[i : i + 1] for i in range(count // HEAD_DIM)], axis=1))
    step = 128
    for lo in range(0, count, step):
        q_id = qid_ref[lo : lo + step, :]
        scores = []
        for key, key_id in zip(keys, ids):
            s = lax.dot_general(
                q[lo : lo + step], key, (((1,), (1,)), ((), ())), preferred_element_type=F32
            )
            scores.append(jnp.where(q_id == key_id, s * scale, -1e30))
        top = functools.reduce(
            jnp.maximum, [jnp.max(s, axis=-1, keepdims=True) for s in scores]
        )
        total = jnp.zeros((step, 1), F32)
        mixed = jnp.zeros((step, HEAD_DIM), F32)
        for s, val in zip(scores, vals):
            probs = jnp.exp(s - top)
            total = total + jnp.sum(probs, axis=-1, keepdims=True)
            mixed = mixed + jnp.dot(probs.astype(BF), val, preferred_element_type=F32)
        out_ref[lo : lo + step, :] = (mixed / total).astype(BF)


SLOTS = 8


def conv_kernel(share, base_ref, slab_ref, own_ref, b_ref, c_ref, d_ref, out_ref, pad_ref, total_ref):
    _, _, high, cols, lanes = slab_ref.shape
    rows = high - 2
    step = 2
    pad_ref[...] = jnp.zeros_like(pad_ref)
    for p, ref in enumerate((own_ref, b_ref, c_ref, d_ref)):
        for j in range(SLOTS):
            pad_ref[j, :share, :] = ref[j * share : (j + 1) * share, :]
        for lo in range(0, rows, step):
            pieces = []
            for j in range(SLOTS):
                tap = jnp.minimum(base_ref[p] + j, 26)
                t, r, c = tap // 9, (tap // 3) % 3, tap % 3
                pieces.append(
                    slab_ref[c, t, pl.ds(r + lo, step), :, :].reshape(step * cols, lanes)
                )
            product = jnp.dot(
                jnp.concatenate(pieces, axis=1),
                pad_ref[...].reshape(SLOTS * lanes, CH),
                preferred_element_type=F32,
            )
            at = slice(lo * cols, (lo + step) * cols)
            if p == 0:
                total_ref[at, :] = product
            else:
                total_ref[at, :] += product
    out_ref[...] = total_ref[...].astype(BF)


def ring(data, axis, by):
    count = lax.axis_size(axis)
    return lax.ppermute(data, axis, [(i, (i + by) % count) for i in range(count)])


def three_parts(total):
    high = lax.reduce_precision(total, 8, 7)
    mid = lax.reduce_precision(total - high, 8, 7)
    return jnp.stack([high, mid, (total - high) - mid]).astype(BF)


def planes_of(data):
    count = lax.axis_size(X)
    return ring(data, X, 1), ring(data, X, count - 1), ring(data, X, 2)


def exchange(data, axes):
    return lax.all_to_all(data, axes, split_axis=0, concat_axis=0, tiled=True)


def shards(
    queries, keys, values, q_gain, k_gain, clip_ids, features, frame_cache, feat_gain, conv_weight
):
    tok, local_cols = queries.shape
    heads = local_cols // HEAD_DIM
    planes = lax.axis_size(X)
    plane_tok = heads * tok
    deep, cores = lax.axis_size("z"), lax.axis_size("core")
    seq_count = planes * deep * cores
    me_x, me_core = lax.axis_index(X), lax.axis_index("core")
    me_grp = lax.axis_index("grp")
    order = jnp.stack([me_x, me_x - 1, me_x + 1, me_x + 2]) % planes

    lanes = 128
    classes = 2 * cores
    share = CH // classes
    weight_rows = conv_weight.shape[0]
    held = jnp.arange(48)[:, None]

    def rows_of(kind):
        first = (kind + 2 * me_core) % classes
        late = (me_core == 1) & (kind >= 2)
        source = jnp.where(
            held < 40,
            classes * (held + late.astype(jnp.int32)) + first,
            jnp.where((held == 40) & (first < 2), jnp.where(me_core == 1, first, 160 + first), -1),
        )
        return source == jnp.arange(weight_rows)[None, :]

    pick = jnp.concatenate([rows_of(2 * me_grp + c) for c in range(cores)], axis=0).astype(BF)
    chosen = jnp.dot(pick, conv_weight, preferred_element_type=F32).astype(BF)
    chosen = chosen.reshape(1, cores, 48, CH)
    sent_weight = jnp.broadcast_to(chosen, (deep,) + chosen.shape[1:]).reshape(-1, 48, CH)
    plane_weight = exchange(sent_weight, ("z", "core"))

    q_f, k_f = queries.astype(F32), keys.astype(F32)
    sums = jnp.stack([jnp.sum(q_f * q_f, axis=-1), jnp.sum(k_f * k_f, axis=-1)])
    frames, tile_rows, tile_cols, _ = features.shape
    feat_f = features.astype(F32)
    scaled = (
        feat_f
        * lax.rsqrt(jnp.mean(feat_f * feat_f, axis=-1, keepdims=True) + EPS)
        * feat_gain
    )
    activated = jax.nn.silu(scaled).astype(BF)
    stacked = jnp.concatenate([frame_cache, activated], axis=0).reshape(-1, CH)
    lane = jnp.arange(classes * lanes)
    slot = lane // lanes
    kind = 2 * ((me_grp + slot // 2) % 2) + slot % 2
    chan = jnp.where(lane % lanes < share, classes * (lane % lanes) + kind, -1)
    sort = (jnp.arange(CH)[:, None] == chan[None, :]).astype(BF)
    sorted_cells = jnp.dot(stacked, sort, preferred_element_type=F32).astype(BF)
    sorted_cells = sorted_cells.reshape(-1, classes, lanes).transpose(1, 0, 2)
    count = sorted_cells.shape[1]
    parts_of = jnp.pad(three_parts(sums).reshape(-1, tok), ((0, 10), (0, lanes - tok)))
    outgoing = jnp.concatenate([sorted_cells[2:].reshape(2 * count, lanes), parts_of], axis=0)
    incoming = ring(outgoing, "grp", 1)
    theirs = incoming[2 * count : 2 * count + 6, :tok].astype(F32).reshape(3, 2, tok)
    sums = sums + ((theirs[0] + theirs[1]) + theirs[2])
    mine = sorted_cells[:2].reshape(2, 3, tile_rows, tile_cols, lanes)
    other = incoming[: 2 * count].reshape(2, 3, tile_rows, tile_cols, lanes)
    is_left, is_upper = me_grp == 0, me_core == 0
    wide = jnp.where(
        is_left,
        jnp.concatenate([mine, other], axis=3),
        jnp.concatenate([other, mine], axis=3),
    )
    outer = jnp.where(is_upper, wide[:, :, :1], wide[:, :, -1:])
    pairs = [(s, s - 1 if s % 2 == 0 else s + 1) for s in range(1, seq_count - 1)]
    beyond = lax.ppermute(outer, SEQ, pairs)
    held_rows = jnp.where(
        is_upper,
        jnp.concatenate([beyond, wide], axis=2),
        jnp.concatenate([wide, beyond], axis=2),
    )
    keep = jnp.where(is_upper, held_rows[0], held_rows[1])
    give = jnp.where(is_upper, held_rows[1], held_rows[0])
    take = ring(give, "core", 1)
    tall = jnp.where(
        is_upper,
        jnp.concatenate([keep, take], axis=1),
        jnp.concatenate([take, keep], axis=1),
    )
    full_cols = 2 * tile_cols
    padded = jnp.pad(tall, ((0, 0), (0, 0), (1, 1), (0, 0)))
    slab = jnp.stack([padded[:, :, c : c + full_cols] for c in range(3)])

    scales = lax.rsqrt(sums / WIDTH + EPS)
    q_norm = (q_f * scales[0][:, None] * q_gain).astype(BF)
    k_norm = (k_f * scales[1][:, None] * k_gain).astype(BF)
    id_row = jnp.pad(clip_ids.astype(BF)[None, :], ((0, 7), (0, HEAD_DIM - tok)))

    def by_head(data):
        return data.reshape(tok, heads, HEAD_DIM).transpose(1, 0, 2)

    payload = jnp.concatenate(
        [
            by_head(q_norm),
            by_head(k_norm),
            by_head(values),
            jnp.broadcast_to(id_row[None], (heads,) + id_row.shape),
        ],
        axis=1,
    )
    got = exchange(payload, HEAD_AXES)
    ids_got = got[:, 3 * tok, :tok].reshape(-1)
    id_block = jnp.pad(ids_got.reshape(-1, HEAD_DIM), ((0, 16 - plane_tok // HEAD_DIM), (0, 0)))
    key_vals = jnp.concatenate(
        [got[:, tok : 3 * tok, :].reshape(2 * plane_tok, HEAD_DIM), id_block], axis=0
    )

    spot_item = jnp.arange(deep * cores * 48)
    spot, item = spot_item // 48, spot_item % 48
    target = 81 * (spot // cores) + jnp.where(item == 40, 40, item + 41 * (spot % cores))
    target = jnp.where(item > 40, -1, target + (648 * me_x) % share)
    place = (jnp.arange(SLOTS * share)[:, None] == target[None, :]).astype(BF)
    my_weight = jnp.dot(
        place, plane_weight.reshape(-1, CH), preferred_element_type=F32
    ).astype(BF)
    weights = (my_weight,) + planes_of(my_weight)
    taps = (27 * order) // planes

    pair = jnp.stack([key_vals, ring(key_vals, "xh", 1)])
    other_pair = ring(pair, "core", 1)
    head_out = pl.pallas_call(
        functools.partial(attention_kernel, tok),
        out_shape=jax.ShapeDtypeStruct((plane_tok, HEAD_DIM), BF),
        in_specs=[VMEM] * 4,
        out_specs=VMEM,
        compiler_params=pltpu.CompilerParams(vmem_limit_bytes=40 << 20),
        cost_estimate=pl.CostEstimate(
            flops=2 * 2 * plane_tok * plane_tok * planes * HEAD_DIM,
            bytes_accessed=planes * plane_tok * HEAD_DIM * 4,
            transcendentals=plane_tok * plane_tok * planes,
        ),
        name="attention",
    )(got, pair, other_pair, ids_got.astype(F32)[:, None])
    returned = exchange(head_out.reshape(heads, tok, HEAD_DIM), HEAD_AXES)
    attended = returned.transpose(1, 0, 2).reshape(tok, local_cols)

    cells = cores * tile_rows * full_cols
    partial = pl.pallas_call(
        functools.partial(conv_kernel, share),
        out_shape=jax.ShapeDtypeStruct((cells, CH), BF),
        in_specs=[pl.BlockSpec(memory_space=pltpu.SMEM)] + [VMEM] * 5,
        out_specs=VMEM,
        scratch_shapes=[
            pltpu.VMEM((SLOTS, lanes, CH), BF),
            pltpu.VMEM((cells, CH), F32),
        ],
        compiler_params=pltpu.CompilerParams(vmem_limit_bytes=48 << 20),
        cost_estimate=pl.CostEstimate(
            flops=2 * cells * planes * SLOTS * lanes * CH,
            bytes_accessed=planes * SLOTS * share * CH * 2,
            transcendentals=0,
        ),
        name="convolution",
    )(taps.astype(jnp.int32), slab, *weights)
    by_core = partial.reshape(cores, tile_rows, 2, tile_cols, CH)
    keep = jnp.where(is_upper, by_core[0], by_core[1]).astype(F32)
    give = jnp.where(is_upper, by_core[1], by_core[0])
    by_half = keep + ring(give, "core", 1).astype(F32)
    keep = jnp.where(is_left, by_half[:, 0], by_half[:, 1])
    give = jnp.where(is_left, by_half[:, 1], by_half[:, 0]).astype(BF)
    convolved = keep + ring(give, "grp", 1).astype(F32)
    decoded = (feat_f + convolved.reshape(features.shape)).astype(BF)
    return (attended, decoded)


def solution(mesh):
    grid = Mesh(
        mesh.devices.reshape((2, 2, 8, 2) + mesh.devices.shape[1:]),
        ("xh", "xl", "z", "core", "grp", "rep"),
    )
    tokens = P(("rep",) + SEQ, "grp")
    image = P("rep", SEQ, "grp", None)
    placed = (
        tokens,
        tokens,
        tokens,
        P("grp"),
        P("grp"),
        P(("rep",) + SEQ),
        image,
        image,
        P(),
        P(SEQ, None),
    )
    return jax.shard_map(
        shards, mesh=grid, in_specs=placed, out_specs=(tokens, image), check_vma=False
    )
```

time: 142 us -> 120 us (0.85)
  starting transfers between devices: 70.2 us -> 59.4 us
  other arithmetic: 12.2 us -> 7.84 us
  waiting for transfers between devices: 43.3 us -> 40 us
  matrix products: 3.52 us -> 1.37 us
    all_to_all x5 -> x3, waiting for transfers between devices: 29.1 us -> 7.39 us  [exchange(): return lax.all_to_all(data, axes, split_axis=0, concat_axis=0, tiled=True)]
    ppermute x10 -> x9, waiting for transfers between devices: 4.78 us -> 19.3 us  [ring(): lax.ppermute(data, axis, [(i, (i + by) % count) for i in range(count)])]
    ppermute x10 -> x9, starting transfers between devices: 38.4 us -> 31 us  [ring(): lax.ppermute(data, axis, [(i, (i + by) % count) for i in range(count)])]
    select_n x9 -> x10, other arithmetic: 4.36 us -> 0.43 us  [the longest x1 0.12 us: shards(): jnp.where(is_left, jnp.concatenate([mine, other], axis=3), jnp.concatenat...]
    ppermute x1, waiting for transfers between devices: 9.41 us -> 13.3 us  [shards(): beyond = lax.ppermute(outer, SEQ, pairs)]
    all_to_all x5 -> x3, starting transfers between devices: 28.2 us -> 24.9 us  [exchange(): return lax.all_to_all(data, axes, split_axis=0, concat_axis=0, tiled=True)]
    another operation x3 -> x5, other arithmetic: 1.78 us -> 0.31 us  [the longest x1 0.19 us: shards(): slab = jnp.stack([padded[:, :, c:c + full_cols] for c in range(3)])]
  transfers between devices with their start and end apart: 16 -> 13, of which waited for: 6 -> 5; matrix products, arithmetic and copies ran while one was open for 11% -> 4% of each run, Pallas kernels for 5% -> 5%
where the time goes in v2:
time: 120 us; the launch traced here: 119 us
  starting transfers between devices  59.4 us (50%)
  waiting for transfers between devices  40 us (33%)
  other arithmetic  7.84 us (7%)
  Pallas kernels  6.55 us (5%)
  local copies, waits for them, and re-layouts  2.56 us (2%)
  matrix products  1.37 us (1%)
  between operations  1.27 us (1%)
    ppermute x9, starting transfers between devices, ring(): lax.ppermute(data, axis, [(i, (i + by) % count) for i in range(count)])  31 us
    all_to_all x3, starting transfers between devices, exchange(): return lax.all_to_all(data, axes, split_axis=0, concat_axis=0, tiled=True)  24.9 us
    ppermute x9, waiting for transfers between devices, ring(): lax.ppermute(data, axis, [(i, (i + by) % count) for i in range(count)])  19.3 us
    ppermute x1, waiting for transfers between devices, shards(): beyond = lax.ppermute(outer, SEQ, pairs)  13.3 us
    all_to_all x3, waiting for transfers between devices, exchange(): return lax.all_to_all(data, axes, split_axis=0, concat_axis=0, tiled=True)  7.39 us
    pallas_call x1, Pallas kernels, shards(): pl.pallas_call(functools.partial(conv_kernel, share), out_shape=jax.Shape...  3.68 us
    ppermute x1, starting transfers between devices, shards(): beyond = lax.ppermute(outer, SEQ, pairs)  3.54 us
    pallas_call x1, Pallas kernels, shards(): pl.pallas_call(functools.partial(attention_kernel, tok), out_shape=jax.Sh...  2.87 us
  transfers between devices with their start and end apart: 13, of which 5 were waited for; matrix products, arithmetic and copies ran while one was open for 4% of the time, Pallas kernels for 5%

profile of v2, /device:TPU:1, one launch (start us, length us, event | category | flops | bytes accessed | tf_op | source)
XLA Modules:
  0.0 119.1 jit_solution(12004168143217126151)
XLA Ops:
  0.7 1.1 fusion.8
  1.7 1.0 fusion.11
  2.8 1.0 fusion.15
  3.9 1.0 fusion.22
  4.9 1.0 pad_maximum_fusion.3
  6.5 8.3 %collective-permute-start = (bf16[784,128]{1,0:T(8,128)(2,1)S(1)}, bf16[784,128]{1,0:T(8,128)(2,1)S(1)}, u32[]{:S(2)}, u32[]{:S(2)}) collective-permute-start(bf16[784,128]{1,0:T(8,128)(2,1)S(1)} %fusion.14), channel_id=1, source_target_pairs={{0,4},{4,0},{1,5},{5,1},{2,6},{6,2},{3,7},{7,3},{8,12},{12,8},{9,1... | collective-permute-start | bytes 602120 | tf_op jit(solution)/shard_map/ppermute | solution.py:92
  16.0 11.3 %all-to-all-start.2 = ((bf16[16,48,384]{2,1,0:T(8,128)(2,1)}), bf16[16,48,384]{2,1,0:T(8,128)(2,1)S(1)}, u32[]{:S(2)}, u32[]{:S(2)}) async-start(bf16[16,48,384]{2,1,0:T(8,128)(2,1)} %bitcast.30), calls=%async_computation.2 | async-start | bytes 1179648 | tf_op jit(solution)/shard_map/all_to_all | solution.py:107
  27.7 3.5 %collective-permute-start.3 = (bf16[2,3,1,128,128]{4,3,2,1,0:T(8,128)(2,1)S(1)}, bf16[2,3,1,128,128]{4,3,2,1,0:T(8,128)(2,1)S(1)}, u32[]{:S(2)}, u32[]{:S(2)}) collective-permute-start(bf16[2,3,1,128,128]{4,3,2,1,0:T(8,128)(2,1)S(1)} %slice_select_fusion), channel_id=1, source_target_pairs={{8,16},{16,8},{24,32},{32,24},{40,48},{48,40},{56,64},{64,56},{72,... | collective-permute-start | bytes 589832 | tf_op jit(solution)/shard_map/ppermute | solution.py:179
  31.3 13.3 %collective-permute-done.3 = bf16[2,3,1,128,128]{4,3,2,1,0:T(8,128)(2,1)S(1)} collective-permute-done((bf16[2,3,1,128,128]{4,3,2,1,0:T(8,128)(2,1)S(1)}, bf16[2,3,1,128,128]{4,3,2,1,0:T(8,128)(2,1)S(1)}, u32[]{:S(2)}, u32[]{:S(2)}) %collective-permute-start.3) | collective-permute-done | bytes 196640 | tf_op jit(solution)/shard_map/ppermute | solution.py:179
  44.7 1.9 %collective-permute-start.4 = (bf16[3,3,128,128]{3,2,1,0:T(8,128)(2,1)S(1)}, bf16[3,3,128,128]{3,2,1,0:T(8,128)(2,1)S(1)}, u32[]{:S(2)}, u32[]{:S(2)}) collective-permute-start(bf16[3,3,128,128]{3,2,1,0:T(8,128)(2,1)S(1)} %get-tuple-element.5), channel_id=1, source_target_pairs={{0,8},{8,0},{1,9},{9,1},{2,10},{10,2},{3,11},{11,3},{4,12},{12,4},... | collective-permute-start | bytes 884744 | tf_op jit(solution)/shard_map/ppermute | solution.py:92
  47.7 7.1 %all-to-all-start = ((bf16[16,104,128]{2,1,0:T(8,128)(2,1)}), bf16[16,104,128]{2,1,0:T(8,128)(2,1)S(1)}, u32[]{:S(2)}, u32[]{:S(2)}) async-start(bf16[16,104,128]{2,1,0:T(8,128)(2,1)} %pad_maximum_fusion.2), calls=%async_computation | async-start | bytes 851968 | tf_op jit(solution)/shard_map/all_to_all | solution.py:107
  56.1 4.4 %collective-permute-start.7 = (bf16[768,384]{1,0:T(8,128)(2,1)S(1)}, bf16[768,384]{1,0:T(8,128)(2,1)S(1)}, u32[]{:S(2)}, u32[]{:S(2)}) collective-permute-start(bf16[768,384]{1,0:T(8,128)(2,1)S(1)} %fusion.1.own_ref), channel_id=1, source_target_pairs={{0,256},{128,384},{256,0},{384,128},{1,257},{129,385},{257,1},{385... | collective-permute-start | bytes 1769480 | tf_op jit(solution)/shard_map/ppermute | solution.py:92
  60.4 3.2 %collective-permute-start.6 = (bf16[768,384]{1,0:T(8,128)(2,1)S(1)}, bf16[768,384]{1,0:T(8,128)(2,1)}, u32[]{:S(2)}, u32[]{:S(2)}) collective-permute-start(bf16[768,384]{1,0:T(8,128)(2,1)S(1)} %fusion.1.own_ref), channel_id=1, source_target_pairs={{0,384},{128,0},{256,128},{384,256},{1,385},{129,1},{257,129},{385... | collective-permute-start | bytes 1769480 | tf_op jit(solution)/shard_map/ppermute | solution.py:92
  63.6 2.1 %collective-permute-start.5 = (bf16[768,384]{1,0:T(8,128)(2,1)S(1)}, bf16[768,384]{1,0:T(8,128)(2,1)}, u32[]{:S(2)}, u32[]{:S(2)}) collective-permute-start(bf16[768,384]{1,0:T(8,128)(2,1)S(1)} %fusion.1.own_ref), channel_id=1, source_target_pairs={{0,128},{128,256},{256,384},{384,0},{1,129},{129,257},{257,385},{3... | collective-permute-start | bytes 1769480 | tf_op jit(solution)/shard_map/ppermute | solution.py:92
  66.8 4.4 %collective-permute-start.1 = (bf16[1040,128]{1,0:T(8,128)(2,1)S(1)}, bf16[1040,128]{1,0:T(8,128)(2,1)S(1)}, u32[]{:S(2)}, u32[]{:S(2)}) collective-permute-start(bf16[1040,128]{1,0:T(8,128)(2,1)S(1)} %get-tuple-element.11), channel_id=1, source_target_pairs={{0,256},{256,0},{1,257},{257,1},{2,258},{258,2},{3,259},{259,3},{4... | collective-permute-start | bytes 798728 | tf_op jit(solution)/shard_map/ppermute | solution.py:92
  71.2 6.1 %collective-permute-done.7.d_ref = bf16[768,384]{1,0:T(8,128)(2,1)S(1)} collective-permute-done((bf16[768,384]{1,0:T(8,128)(2,1)S(1)}, bf16[768,384]{1,0:T(8,128)(2,1)S(1)}, u32[]{:S(2)}, u32[]{:S(2)}) %collective-permute-start.7) | collective-permute-done | bytes 589856 | tf_op jit(solution)/shard_map/ppermute | solution.py:92
  77.3 13.3 %collective-permute-done.6.c_ref = bf16[768,384]{1,0:T(8,128)(2,1)} collective-permute-done((bf16[768,384]{1,0:T(8,128)(2,1)S(1)}, bf16[768,384]{1,0:T(8,128)(2,1)}, u32[]{:S(2)}, u32[]{:S(2)}) %collective-permute-start.6) | collective-permute-done | bytes 589856 | tf_op jit(solution)/shard_map/ppermute | solution.py:92
  90.5 3.7 %convolution.11 = bf16[512,384]{1,0:T(8,128)(2,1)S(1)} custom-call(s32[4]{0:T(128)S(1)} %and_select_fusion.2.base_ref, bf16[3,3,6,128,128]{4,3,2,1,0:T(8,128)(2,1)S(1)} %pad_maximum_fusion.slab_ref, bf16[768,384]{1,0:T(8,128)(2,1)S(1)} %fusion.1.own_ref, bf16[768,384]{1,0:T(8,128)(2,1)} %collective-permute-done.5.b_ref, ...), custom_call_target="tpu_custom_call" | custom-call | flops 1610612736 | bytes 2359296 | tf_op jit(solution)/shard_map/convolution/pallas_call | solution.py:251
  94.3 3.0 %collective-permute-start.8 = (bf16[2,2,64,384]{3,2,0,1:T(8,128)(2,1)S(1)}, bf16[2,2,64,384]{3,2,0,1:T(8,128)(2,1)S(1)}, u32[]{:S(2)}, u32[]{:S(2)}) collective-permute-start(bf16[2,2,64,384]{3,2,0,1:T(8,128)(2,1)S(1)} %copy.22), channel_id=1, source_target_pairs={{0,8},{8,0},{1,9},{9,1},{2,10},{10,2},{3,11},{11,3},{4,12},{12,4},... | collective-permute-start | bytes 589832 | tf_op jit(solution)/shard_map/ppermute | solution.py:92
  97.3 1.9 %collective-permute-start.2 = (bf16[2,1040,128]{2,1,0:T(8,128)(2,1)S(1)}, bf16[2,1040,128]{2,1,0:T(8,128)(2,1)S(1)}, u32[]{:S(2)}, u32[]{:S(2)}) collective-permute-start(bf16[2,1040,128]{2,1,0:T(8,128)(2,1)S(1)} %pad_maximum_fusion.1.pair_ref), channel_id=1, source_target_pairs={{0,8},{8,0},{1,9},{9,1},{2,10},{10,2},{3,11},{11,3},{4,12},{12,4},... | collective-permute-start | bytes 1597448 | tf_op jit(solution)/shard_map/ppermute | solution.py:92
  99.4 1.9 %collective-permute-start.9 = (bf16[2,64,384]{2,1,0:T(8,128)(2,1)S(1)}, bf16[2,64,384]{2,1,0:T(8,128)(2,1)S(1)}, u32[]{:S(2)}, u32[]{:S(2)}) collective-permute-start(bf16[2,64,384]{2,1,0:T(8,128)(2,1)S(1)} %fusion.26), channel_id=1, source_target_pairs={{0,4},{4,0},{1,5},{5,1},{2,6},{6,2},{3,7},{7,3},{8,12},{12,8},{9,1... | collective-permute-start | bytes 294920 | tf_op jit(solution)/shard_map/ppermute | solution.py:92
  101.6 2.9 %attention.1 = bf16[512,128]{1,0:T(8,128)(2,1)} custom-call(bf16[16,104,128]{2,1,0:T(8,128)(2,1)S(1)} %all-to-all-done.q_ref, bf16[2,1040,128]{2,1,0:T(8,128)(2,1)S(1)} %pad_maximum_fusion.1.pair_ref, bf16[2,1040,128]{2,1,0:T(8,128)(2,1)S(1)} %collective-permute-done.2.other_ref, f32[512,1]{1,0:T(8,128)S(1)} %reshape.438.qid_ref), custom_call_target="tpu_custom_call" | custom-call | flops 536870912 | bytes 1048576 | tf_op jit(solution)/shard_map/attention/pallas_call | solution.py:234
  104.5 6.5 %all-to-all-start.1 = ((bf16[16,32,128]{2,1,0:T(8,128)(2,1)}), bf16[16,32,128]{2,1,0:T(8,128)(2,1)S(1)}, u32[]{:S(2)}, u32[]{:S(2)}) async-start(bf16[16,32,128]{2,1,0:T(8,128)(2,1)} %bitcast.16), calls=%async_computation.1 | async-start | bytes 262144 | tf_op jit(solution)/shard_map/all_to_all | solution.py:107
  111.7 6.7 %all-to-all-done.1 = bf16[16,32,128]{2,1,0:T(8,128)(2,1)S(1)} async-done(((bf16[16,32,128]{2,1,0:T(8,128)(2,1)}), bf16[16,32,128]{2,1,0:T(8,128)(2,1)S(1)}, u32[]{:S(2)}, u32[]{:S(2)}) %all-to-all-start.1) | async-done | bytes 131104 | tf_op jit(solution)/shard_map/all_to_all | solution.py:107
  (75 shorter events, 7.3 us)
Async XLA Ops:
  0.6 26.8 %copy-start = (bf16[32,2048]{1,0:T(8,128)(2,1)S(1)}, bf16[32,2048]{1,0:T(8,128)(2,1)}, u32[]{:S(2)}) copy-start(bf16[32,2048]{1,0:T(8,128)(2,1)} %param.12) | copy-start | bytes 393220
  4.9 10.0 %copy-start.4 = (bf16[162,384]{1,0:T(8,128)(2,1)S(1)}, bf16[162,384]{1,0:T(8,128)(2,1)}, u32[]{:S(2)}) copy-start(bf16[162,384]{1,0:T(8,128)(2,1)} %param.19) | copy-start | bytes 373252
  6.4 20.9 %copy-start.7 = (s32[32]{0:T(128)S(1)}, s32[32]{0:T(128)}, u32[]{:S(2)}) copy-start(s32[32]{0:T(128)} %param.15) | copy-start | bytes 388
  6.5 21.0 %collective-permute-start = (bf16[784,128]{1,0:T(8,128)(2,1)S(1)}, bf16[784,128]{1,0:T(8,128)(2,1)S(1)}, u32[]{:S(2)}, u32[]{:S(2)}) collective-permute-start(bf16[784,128]{1,0:T(8,128)(2,1)S(1)} %fusion.14), channel_id=1, source_target_pairs={{0,4},{4,0},{1,5},{5,1},{2,6},{6,2},{3,7},{7,3},{8,12},{12,8},{9,1... | collective-permute-start | bytes 602120 | tf_op jit(solution)/shard_map/ppermute | solution.py:92
  16.0 31.7 %all-to-all-start.2 = ((bf16[16,48,384]{2,1,0:T(8,128)(2,1)}), bf16[16,48,384]{2,1,0:T(8,128)(2,1)S(1)}, u32[]{:S(2)}, u32[]{:S(2)}) async-start(bf16[16,48,384]{2,1,0:T(8,128)(2,1)} %bitcast.30), calls=%async_computation.2 | async-start | bytes 1179648 | tf_op jit(solution)/shard_map/all_to_all | solution.py:107
  27.5 19.1 %copy-start.2 = (bf16[32,2048]{1,0:T(8,128)(2,1)S(1)}, bf16[32,2048]{1,0:T(8,128)(2,1)}, u32[]{:S(2)}) copy-start(bf16[32,2048]{1,0:T(8,128)(2,1)} %param.11) | copy-start | bytes 393220
  27.5 19.1 %copy-start.3 = (bf16[32,2048]{1,0:T(8,128)(2,1)S(1)}, bf16[32,2048]{1,0:T(8,128)(2,1)}, u32[]{:S(2)}) copy-start(bf16[32,2048]{1,0:T(8,128)(2,1)} %param.10) | copy-start | bytes 393220
  27.5 19.1 %copy-start.5 = (f32[2048]{0:T(1024)S(1)}, f32[2048]{0:T(1024)}, u32[]{:S(2)}) copy-start(f32[2048]{0:T(1024)} %param.14) | copy-start | bytes 24580
  27.5 19.1 %copy-start.6 = (f32[2048]{0:T(1024)S(1)}, f32[2048]{0:T(1024)}, u32[]{:S(2)}) copy-start(f32[2048]{0:T(1024)} %param.13) | copy-start | bytes 24580
  27.7 16.9 %collective-permute-start.3 = (bf16[2,3,1,128,128]{4,3,2,1,0:T(8,128)(2,1)S(1)}, bf16[2,3,1,128,128]{4,3,2,1,0:T(8,128)(2,1)S(1)}, u32[]{:S(2)}, u32[]{:S(2)}) collective-permute-start(bf16[2,3,1,128,128]{4,3,2,1,0:T(8,128)(2,1)S(1)} %slice_select_fusion), channel_id=1, source_target_pairs={{8,16},{16,8},{24,32},{32,24},{40,48},{48,40},{56,64},{64,56},{72,... | collective-permute-start | bytes 589832 | tf_op jit(solution)/shard_map/ppermute | solution.py:179
  44.7 10.1 %collective-permute-start.4 = (bf16[3,3,128,128]{3,2,1,0:T(8,128)(2,1)S(1)}, bf16[3,3,128,128]{3,2,1,0:T(8,128)(2,1)S(1)}, u32[]{:S(2)}, u32[]{:S(2)}) collective-permute-start(bf16[3,3,128,128]{3,2,1,0:T(8,128)(2,1)S(1)} %get-tuple-element.5), channel_id=1, source_target_pairs={{0,8},{8,0},{1,9},{9,1},{2,10},{10,2},{3,11},{11,3},{4,12},{12,4},... | collective-permute-start | bytes 884744 | tf_op jit(solution)/shard_map/ppermute | solution.py:92
  47.7 18.9 %all-to-all-start = ((bf16[16,104,128]{2,1,0:T(8,128)(2,1)}), bf16[16,104,128]{2,1,0:T(8,128)(2,1)S(1)}, u32[]{:S(2)}, u32[]{:S(2)}) async-start(bf16[16,104,128]{2,1,0:T(8,128)(2,1)} %pad_maximum_fusion.2), calls=%async_computation | async-start | bytes 851968 | tf_op jit(solution)/shard_map/all_to_all | solution.py:107
  56.1 21.2 %collective-permute-start.7 = (bf16[768,384]{1,0:T(8,128)(2,1)S(1)}, bf16[768,384]{1,0:T(8,128)(2,1)S(1)}, u32[]{:S(2)}, u32[]{:S(2)}) collective-permute-start(bf16[768,384]{1,0:T(8,128)(2,1)S(1)} %fusion.1.own_ref), channel_id=1, source_target_pairs={{0,256},{128,384},{256,0},{384,128},{1,257},{129,385},{257,1},{385... | collective-permute-start | bytes 1769480 | tf_op jit(solution)/shard_map/ppermute | solution.py:92
  60.4 30.1 %collective-permute-start.6 = (bf16[768,384]{1,0:T(8,128)(2,1)S(1)}, bf16[768,384]{1,0:T(8,128)(2,1)}, u32[]{:S(2)}, u32[]{:S(2)}) collective-permute-start(bf16[768,384]{1,0:T(8,128)(2,1)S(1)} %fusion.1.own_ref), channel_id=1, source_target_pairs={{0,384},{128,0},{256,128},{384,256},{1,385},{129,1},{257,129},{385... | collective-permute-start | bytes 1769480 | tf_op jit(solution)/shard_map/ppermute | solution.py:92
  63.6 26.9 %collective-permute-start.5 = (bf16[768,384]{1,0:T(8,128)(2,1)S(1)}, bf16[768,384]{1,0:T(8,128)(2,1)}, u32[]{:S(2)}, u32[]{:S(2)}) collective-permute-start(bf16[768,384]{1,0:T(8,128)(2,1)S(1)} %fusion.1.own_ref), channel_id=1, source_target_pairs={{0,128},{128,256},{256,384},{384,0},{1,129},{129,257},{257,385},{3... | collective-permute-start | bytes 1769480 | tf_op jit(solution)/shard_map/ppermute | solution.py:92
  66.8 30.4 %collective-permute-start.1 = (bf16[1040,128]{1,0:T(8,128)(2,1)S(1)}, bf16[1040,128]{1,0:T(8,128)(2,1)S(1)}, u32[]{:S(2)}, u32[]{:S(2)}) collective-permute-start(bf16[1040,128]{1,0:T(8,128)(2,1)S(1)} %get-tuple-element.11), channel_id=1, source_target_pairs={{0,256},{256,0},{1,257},{257,1},{2,258},{258,2},{3,259},{259,3},{4... | collective-permute-start | bytes 798728 | tf_op jit(solution)/shard_map/ppermute | solution.py:92
  94.3 5.0 %collective-permute-start.8 = (bf16[2,2,64,384]{3,2,0,1:T(8,128)(2,1)S(1)}, bf16[2,2,64,384]{3,2,0,1:T(8,128)(2,1)S(1)}, u32[]{:S(2)}, u32[]{:S(2)}) collective-permute-start(bf16[2,2,64,384]{3,2,0,1:T(8,128)(2,1)S(1)} %copy.22), channel_id=1, source_target_pairs={{0,8},{8,0},{1,9},{9,1},{2,10},{10,2},{3,11},{11,3},{4,12},{12,4},... | collective-permute-start | bytes 589832 | tf_op jit(solution)/shard_map/ppermute | solution.py:92
  97.3 4.3 %collective-permute-start.2 = (bf16[2,1040,128]{2,1,0:T(8,128)(2,1)S(1)}, bf16[2,1040,128]{2,1,0:T(8,128)(2,1)S(1)}, u32[]{:S(2)}, u32[]{:S(2)}) collective-permute-start(bf16[2,1040,128]{2,1,0:T(8,128)(2,1)S(1)} %pad_maximum_fusion.1.pair_ref), channel_id=1, source_target_pairs={{0,8},{8,0},{1,9},{9,1},{2,10},{10,2},{3,11},{11,3},{4,12},{12,4},... | collective-permute-start | bytes 1597448 | tf_op jit(solution)/shard_map/ppermute | solution.py:92
  99.3 11.7 %copy-start.1 = (bf16[1,2,64,384]{3,2,1,0:T(8,128)(2,1)S(1)}, bf16[1,2,64,384]{3,2,1,0:T(8,128)(2,1)}, u32[]{:S(2)}) copy-start(bf16[1,2,64,384]{3,2,1,0:T(8,128)(2,1)} %param.16) | copy-start | bytes 294916
  99.4 11.6 %collective-permute-start.9 = (bf16[2,64,384]{2,1,0:T(8,128)(2,1)S(1)}, bf16[2,64,384]{2,1,0:T(8,128)(2,1)S(1)}, u32[]{:S(2)}, u32[]{:S(2)}) collective-permute-start(bf16[2,64,384]{2,1,0:T(8,128)(2,1)S(1)} %fusion.26), channel_id=1, source_target_pairs={{0,4},{4,0},{1,5},{5,1},{2,6},{6,2},{3,7},{7,3},{8,12},{12,8},{9,1... | collective-permute-start | bytes 294920 | tf_op jit(solution)/shard_map/ppermute | solution.py:92
  104.5 13.9 %all-to-all-start.1 = ((bf16[16,32,128]{2,1,0:T(8,128)(2,1)}), bf16[16,32,128]{2,1,0:T(8,128)(2,1)S(1)}, u32[]{:S(2)}, u32[]{:S(2)}) async-start(bf16[16,32,128]{2,1,0:T(8,128)(2,1)} %bitcast.16), calls=%async_computation.1 | async-start | bytes 262144 | tf_op jit(solution)/shard_map/all_to_all | solution.py:107

commit v3 on v1

--- a/solution.py
+++ b/solution.py
@@ -14,20 +14,21 @@
 CH = 384
 WIDTH = HEADS * HEAD_DIM
 EPS = 1e-06
-SEQ = ("x", "z", "core")
-HEAD_AXES = ("z", "core")
+X = ("xh", "xl")
+SEQ = ("xh", "xl", "z", "core")
+HEAD_AXES = ("xl", "z")
 BF = jnp.bfloat16
 F32 = jnp.float32
 VMEM = pl.BlockSpec(memory_space=pltpu.VMEM)
 
 
-def attention_kernel(tok, q_ref, own_ref, b_ref, c_ref, d_ref, qid_ref, out_ref):
+def attend(tok, q_ref, blocks, qid_ref, out_ref):
     groups = q_ref.shape[0]
     count = groups * tok
     scale = 1.0 / math.sqrt(HEAD_DIM)
     q = q_ref[:, :tok, :].reshape(count, HEAD_DIM)
     keys, vals, ids = [], [], []
-    for ref in (own_ref, b_ref, c_ref, d_ref):
+    for ref in blocks:
         pairs = ref[: 2 * count, :].reshape(groups, 2 * tok, HEAD_DIM)
         keys.append(pairs[:, :tok].reshape(count, HEAD_DIM))
         vals.append(pairs[:, tok:].reshape(count, HEAD_DIM))
@@ -54,16 +55,44 @@
         out_ref[lo : lo + step, :] = (mixed / total).astype(BF)
 
 
+def lay_out(core, left, cells_ref, halo_ref, slab_ref):
+    _, parts, frames, _, cols, lanes = slab_ref.shape
+    at = lax.broadcasted_iota(jnp.int32, (cols, lanes), 0)
+
+    def put(part, t, row, cells, beside):
+        wide = cells.astype(F32)
+        before = jnp.where(at == 0, beside * left, pltpu.roll(wide, 1, axis=0))
+        after = jnp.where(at == cols - 1, beside * (1.0 - left), pltpu.roll(wide, cols - 1, axis=0))
+        slab_ref[0, part, t, row] = before.astype(BF)
+        slab_ref[1, part, t, row] = cells
+        slab_ref[2, part, t, row] = after.astype(BF)
+
+    def one_part(part, _):
+        base = pl.multiple_of(part * (2 * frames * cols + 16), 16)
+        beside = cells_ref[pl.ds(base + 2 * frames * cols, 16), :].astype(F32)
+        halo_base = pl.multiple_of(part * (frames * cols + 16), 16)
+        beyond = halo_ref[pl.ds(halo_base + frames * cols, 16), :].astype(F32)
+        for t in range(frames):
+            for r in range(2):
+                k = 2 * t + r
+                cells = cells_ref[pl.ds(base + k * cols, cols), :]
+                put(part, t, 1 + 2 * core + r, cells, beside[k : k + 1])
+            put(part, t, 5 * core, halo_ref[pl.ds(halo_base + t * cols, cols), :], beyond[t : t + 1])
+        return 0
+
+    lax.fori_loop(0, parts, one_part, 0)
+
+
 SLOTS = 8
 
 
-def conv_kernel(share, base_ref, slab_ref, own_ref, b_ref, c_ref, d_ref, out_ref, pad_ref, low_ref, high_ref):
+def convolve(share, taps, slab_ref, planes, out_ref, pad_ref, low_ref, high_ref):
     _, parts, _, high, cols, lanes = slab_ref.shape
     rows = high - 2
     cells = rows * cols
     half = SLOTS // 2
     pad_ref[...] = jnp.zeros_like(pad_ref)
-    for p, ref in enumerate((own_ref, b_ref, c_ref, d_ref)):
+    for p, ref in enumerate(planes):
         for j in range(SLOTS):
             pad_ref[j, :share, :128] = ref[j * share : (j + 1) * share, :]
             start = SLOTS * share + (j % half) * share
@@ -72,7 +101,7 @@
             for side, total_ref in ((0, low_ref), (1, high_ref)):
                 pieces = []
                 for j in range(half):
-                    tap = jnp.minimum(base_ref[p] + side * half + j, 26)
+                    tap = jnp.minimum(taps(p) + side * half + j, 26)
                     t, r, c = tap // 9, (tap // 3) % 3, tap % 3
                     pieces.append(
                         slab_ref[c, part, t, pl.ds(r, rows), :, :].reshape(cells, lanes)
@@ -93,14 +122,42 @@
         out_ref[part, cells:, :] = rest.astype(BF)
 
 
+def attention_kernel(tok, block, q_ref, mine_ref, theirs_ref, qid_ref, out_ref):
+    blocks = [r.at[pl.ds(i * block, block)] for r in (mine_ref, theirs_ref) for i in range(2)]
+    attend(tok, q_ref, blocks, qid_ref, out_ref)
+
+
+def conv_kernel(share, sizes, place_ref, mine_ref, theirs_ref, *refs):
+    *planes, conv_ref, slab_ref, pad_ref, low_ref, high_ref = refs
+    block, cells, halo = sizes
+    core, left = place_ref[0], place_ref[1].astype(F32)
+    for own, ref in ((core, mine_ref), (1 - core, theirs_ref)):
+        lay_out(
+            own, left, ref.at[pl.ds(2 * block, cells)], ref.at[pl.ds(2 * block + cells, halo)], slab_ref
+        )
+    convolve(share, lambda p: place_ref[2 + p], slab_ref, planes, conv_ref, pad_ref, low_ref, high_ref)
+
+
+def activate(cells, gain):
+    cells = cells.astype(F32)
+    scale = lax.rsqrt(jnp.mean(cells * cells, axis=-1, keepdims=True) + EPS)
+    return jax.nn.silu(cells * scale * gain).astype(BF)
+
+
+def three_parts(total):
+    high = lax.reduce_precision(total, 8, 7)
+    mid = lax.reduce_precision(total - high, 8, 7)
+    return jnp.stack([high, mid, (total - high) - mid]).astype(BF)
+
+
 def ring(data, axis, by):
     count = lax.axis_size(axis)
     return lax.ppermute(data, axis, [(i, (i + by) % count) for i in range(count)])
 
 
 def planes_of(data):
-    count = lax.axis_size("x")
-    return ring(data, "x", 1), ring(data, "x", count - 1), ring(data, "x", 2)
+    count = lax.axis_size(X)
+    return ring(data, X, 1), ring(data, X, count - 1), ring(data, X, 2)
 
 
 def exchange(data, axes):
@@ -112,20 +169,38 @@
 ):
     tok, local_cols = queries.shape
     heads = local_cols // HEAD_DIM
-    planes = lax.axis_size("x")
+    planes = lax.axis_size(X)
     plane_tok = heads * tok
     deep, cores = lax.axis_size("z"), lax.axis_size("core")
     seq_count = planes * deep * cores
-    me_x, me_core = lax.axis_index("x"), lax.axis_index("core")
+    me_x, me_core = lax.axis_index(X), lax.axis_index("core")
     me_grp, me_rep = lax.axis_index("grp"), lax.axis_index("rep")
     parts = lax.axis_size("rep")
     order = jnp.stack([me_x, me_x - 1, me_x + 1, me_x + 2]) % planes
 
     q_f, k_f = queries.astype(F32), keys.astype(F32)
     sums = jnp.stack([jnp.sum(q_f * q_f, axis=-1), jnp.sum(k_f * k_f, axis=-1)])
-    sums = sums + ring(sums, "grp", 1)
-
     lanes = 128
+    frames, tile_rows, tile_cols, _ = features.shape
+    is_left, is_upper = me_grp == 0, me_core == 0
+    raw_edge = jnp.concatenate(
+        [
+            jnp.where(is_left, frame_cache[:, :, -1], frame_cache[:, :, 0]),
+            jnp.where(is_left, features[:, :, -1], features[:, :, 0]),
+        ]
+    )
+    edge_count = raw_edge.shape[0] * raw_edge.shape[1]
+    first_out = jnp.concatenate(
+        [
+            jnp.pad(three_parts(sums).reshape(6, tok), ((0, 0), (0, lanes - tok))),
+            raw_edge.reshape(-1, lanes),
+        ]
+    )
+    first_in = ring(first_out, "grp", 1)
+    theirs = first_in[:6, :tok].astype(F32).reshape(3, 2, tok)
+    sums = sums + ((theirs[0] + theirs[1]) + theirs[2])
+    beside = first_in[6:].reshape(edge_count, CH)
+
     share = CH // parts
     weight_rows = conv_weight.shape[0]
     first = (me_rep + 2 * me_core) % parts
@@ -144,7 +219,7 @@
         [halves[:, :, :128], jnp.concatenate([last[:, :24], last[:, 24:]], axis=2)], axis=1
     )
     sent_weight = jnp.broadcast_to(halves[None], (deep,) + halves.shape).reshape(-1, 72, 128)
-    plane_weight = exchange(sent_weight, HEAD_AXES)
+    plane_weight = exchange(sent_weight, ("z", "core"))
 
     scales = lax.rsqrt(sums / WIDTH + EPS)
     q_norm = (q_f * scales[0][:, None] * q_gain).astype(BF)
@@ -164,12 +239,6 @@
         axis=1,
     )
     got = exchange(payload, HEAD_AXES)
-    ids_got = got[:, 3 * tok, :tok].reshape(-1)
-    id_block = jnp.pad(ids_got.reshape(-1, HEAD_DIM), ((0, 16 - plane_tok // HEAD_DIM), (0, 0)))
-    key_vals = jnp.concatenate(
-        [got[:, tok : 3 * tok, :].reshape(2 * plane_tok, HEAD_DIM), id_block], axis=0
-    )
-
     slot = jnp.arange(deep * cores * 48)
     spot, item = slot // 48, slot % 48
     target = 81 * (spot // cores) + jnp.where(item == 40, 40, item + 41 * (spot % cores))
@@ -197,69 +266,68 @@
     )
     weights = (my_weight,) + planes_of(my_weight)
     taps = (27 * order) // planes
-
-    others = planes_of(key_vals)
+    got, *near = lax.optimization_barrier((got,) + weights[1:3])
+    weights = weights[:1] + tuple(near) + weights[3:]
+
+    feat_f = features.astype(F32)
+    stacked = jnp.concatenate([frame_cache, activate(features, feat_gain)], axis=0)
+    lane = jnp.arange(parts * lanes)
+    chan = jnp.where(
+        lane % lanes < share, parts * (lane % lanes) + (me_rep + lane // lanes) % parts, -1
+    )
+    sort = (jnp.arange(CH)[:, None] == chan[None, :]).astype(BF)
+
+    def by_class(data):
+        data = jnp.dot(data, sort, preferred_element_type=F32).astype(BF)
+        return data.reshape(-1, parts, lanes).transpose(1, 0, 2)
+
+    beside = jnp.concatenate([beside[:-2], activate(beside[-2:], feat_gain)])
+    beside = jnp.pad(beside, ((0, 16 - edge_count), (0, 0)))
+    outgoing = jnp.concatenate([by_class(stacked.reshape(-1, CH)), by_class(beside)], axis=1)
+    cells = jnp.stack([outgoing[0]] + [ring(outgoing[by], "rep", by) for by in range(1, parts)])
+    main = cells[:, : 6 * tile_cols].reshape(parts, 3, tile_rows, tile_cols, lanes)
+    ends = cells[:, 6 * tile_cols : 6 * tile_cols + 6].reshape(parts, 3, tile_rows, lanes)
+    outer = jnp.where(is_upper, main[:, :, 0], main[:, :, -1]).reshape(parts, -1, lanes)
+    outer_ends = jnp.where(is_upper, ends[:, :, 0], ends[:, :, -1])
+    outer = jnp.concatenate([outer, jnp.pad(outer_ends, ((0, 0), (0, 13), (0, 0)))], axis=1)
+    steps = [(s, s - 1 if s % 2 == 0 else s + 1) for s in range(1, seq_count - 1)]
+    beyond = lax.ppermute(outer, SEQ, steps)
+
+    ids_got = got[:, 3 * tok, :tok].reshape(-1)
+    id_block = jnp.pad(ids_got.reshape(-1, HEAD_DIM), ((0, 16 - plane_tok // HEAD_DIM), (0, 0)))
+    key_vals = jnp.concatenate(
+        [got[:, tok : 3 * tok, :].reshape(2 * plane_tok, HEAD_DIM), id_block], axis=0
+    )
+
+    cells, beyond = cells.reshape(-1, lanes), beyond.reshape(-1, lanes)
+    across = ring(key_vals, "xh", 1)
+    across, *weights = lax.optimization_barrier((across,) + weights)
+    mine = jnp.concatenate([key_vals, across, cells, beyond])
+    theirs = ring(mine, "core", 1)
+    sizes = key_vals.shape[0], cells.shape[0], beyond.shape[0]
+    chip_cells = cores * tile_rows * tile_cols
+    place = jnp.concatenate([jnp.stack([me_core, me_grp]), taps]).astype(jnp.int32)
     head_out = pl.pallas_call(
-        functools.partial(attention_kernel, tok),
+        functools.partial(attention_kernel, tok, sizes[0]),
         out_shape=jax.ShapeDtypeStruct((plane_tok, HEAD_DIM), BF),
-        in_specs=[VMEM] * 6,
+        in_specs=[VMEM] * 4,
         out_specs=VMEM,
         compiler_params=pltpu.CompilerParams(vmem_limit_bytes=40 << 20),
         cost_estimate=pl.CostEstimate(
-            flops=2 * 2 * plane_tok * plane_tok * planes * HEAD_DIM,
+            flops=4 * plane_tok * plane_tok * planes * HEAD_DIM,
             bytes_accessed=planes * plane_tok * HEAD_DIM * 4,
             transcendentals=plane_tok * plane_tok * planes,
         ),
         name="attention",
-    )(got, key_vals, *others, ids_got.astype(F32)[:, None])
-    returned = exchange(head_out.reshape(heads, tok, HEAD_DIM), HEAD_AXES)
-    attended = returned.transpose(1, 0, 2).reshape(tok, local_cols)
-
-    frames, tile_rows, tile_cols, _ = features.shape
-    feat_f = features.astype(F32)
-    scaled = (
-        feat_f
-        * lax.rsqrt(jnp.mean(feat_f * feat_f, axis=-1, keepdims=True) + EPS)
-        * feat_gain
-    )
-    activated = jax.nn.silu(scaled).astype(BF)
-    stacked = jnp.concatenate([frame_cache, activated], axis=0).reshape(-1, CH)
-    lane = jnp.arange(parts * lanes)
-    chan = jnp.where(lane % lanes < share, parts * (lane % lanes) + lane // lanes, -1)
-    sort = (jnp.arange(CH)[:, None] == chan[None, :]).astype(BF)
-    sorted_cells = jnp.dot(stacked, sort, preferred_element_type=F32).astype(BF)
-    outgoing = sorted_cells.reshape(-1, parts, lanes).transpose(1, 0, 2)
-    cells = exchange(outgoing, "rep").reshape(parts, 3, tile_rows, tile_cols, lanes)
-    is_upper = me_core == 0
-    outer = jnp.where(is_upper, cells[:, :, :1], cells[:, :, -1:])
-    pairs = [(s, s - 1 if s % 2 == 0 else s + 1) for s in range(1, seq_count - 1)]
-    beyond = lax.ppermute(outer, SEQ, pairs)
-    mine = jnp.where(
-        is_upper,
-        jnp.concatenate([beyond, cells], axis=2),
-        jnp.concatenate([cells, beyond], axis=2),
-    )
-    theirs = ring(mine, "core", 1)
-    tall = jnp.where(
-        is_upper,
-        jnp.concatenate([mine, theirs], axis=2),
-        jnp.concatenate([theirs, mine], axis=2),
-    )
-    is_left = me_grp == 0
-    edge = jnp.where(is_left, tall[:, :, :, -1:], tall[:, :, :, :1])
-    beside = ring(edge, "grp", 1)
-    nothing = jnp.zeros_like(beside)
-    wide = jnp.concatenate(
-        [jnp.where(is_left, nothing, beside), tall, jnp.where(is_left, beside, nothing)], axis=3
-    )
-    slab = jnp.stack([wide[:, :, :, c : c + tile_cols] for c in range(3)])
-    chip_cells = cores * tile_rows * tile_cols
+    )(got, mine, theirs, ids_got.astype(F32)[:, None])
+    place, head_out = lax.optimization_barrier((place, head_out))
     partial = pl.pallas_call(
-        functools.partial(conv_kernel, share),
+        functools.partial(conv_kernel, share, sizes),
         out_shape=jax.ShapeDtypeStruct((parts, chip_cells + chip_cells // 2, 128), BF),
-        in_specs=[pl.BlockSpec(memory_space=pltpu.SMEM)] + [VMEM] * 5,
+        in_specs=[pl.BlockSpec(memory_space=pltpu.SMEM)] + [VMEM] * (2 + len(weights)),
         out_specs=VMEM,
         scratch_shapes=[
+            pltpu.VMEM((3, parts, 3, cores * tile_rows + 2, tile_cols, lanes), BF),
             pltpu.VMEM((SLOTS, lanes, 256), BF),
             pltpu.VMEM((parts, chip_cells, 256), F32),
             pltpu.VMEM((parts, chip_cells, 256), F32),
@@ -271,8 +339,12 @@
             transcendentals=0,
         ),
         name="convolution",
-    )(taps.astype(jnp.int32), slab, *weights)
-    sums_back = jnp.sum(exchange(partial, "rep").astype(F32), axis=0)
+    )(place, mine, theirs, *weights)
+    returned = exchange(head_out.reshape(heads, tok, HEAD_DIM), HEAD_AXES)
+
+    sums_back = partial[0].astype(F32)
+    for by in range(1, parts):
+        sums_back = sums_back + ring(partial[by], "rep", parts - by).astype(F32)
     tile_cells = tile_rows * tile_cols
     main_cols = sums_back[:chip_cells].reshape(cores, tile_cells, 128)
     last_cols = sums_back[chip_cells:].reshape(tile_cells, cores, 64).transpose(1, 0, 2)
@@ -285,13 +357,15 @@
         jnp.concatenate([keep, take], axis=1),
         jnp.concatenate([take, keep], axis=1),
     ).reshape(features.shape)
+    attended = returned.transpose(1, 0, 2).reshape(tok, local_cols)
     decoded = (feat_f + convolved).astype(BF)
     return (attended, decoded)
 
 
 def solution(mesh):
     grid = Mesh(
-        mesh.devices.reshape((4, 8, 2) + mesh.devices.shape[1:]), ("x", "z", "core", "grp", "rep")
+        mesh.devices.reshape((2, 2, 8, 2) + mesh.devices.shape[1:]),
+        ("xh", "xl", "z", "core", "grp", "rep"),
     )
     tokens = P(("rep",) + SEQ, "grp")
     image = P("rep", SEQ, "grp", None)

time: 142 us -> 116 us (0.82)
  waiting for transfers between devices: 43.3 us -> 14.3 us
  starting transfers between devices: 70.2 us -> 76.9 us
  other arithmetic: 12.2 us -> 6.5 us
    all_to_all x5 -> x3, waiting for transfers between devices: 29.1 us -> 3.23 us  [exchange(): return lax.all_to_all(data, axes, split_axis=0, concat_axis=0, tiled=True)]
    ppermute x10 -> x13, starting transfers between devices: 38.4 us -> 45.2 us  [ring(): lax.ppermute(data, axis, [(i, (i + by) % count) for i in range(count)])]
    ppermute x1, waiting for transfers between devices: 9.41 us -> 3.38 us  [shards(): beyond = lax.ppermute(outer, SEQ, steps)]
    select_n x7 -> x5, other arithmetic: 4.34 us -> 0.82 us  [the longest x1 0.77 us: shards(): jnp.where(is_left, frame_cache[:, :, -1], frame_cache[:, :, 0])]
    ppermute x10 -> x13, waiting for transfers between devices: 4.78 us -> 7.72 us  [ring(): lax.ppermute(data, axis, [(i, (i + by) % count) for i in range(count)])]
    all_to_all x5 -> x3, starting transfers between devices: 28.2 us -> 25.3 us  [exchange(): return lax.all_to_all(data, axes, split_axis=0, concat_axis=0, tiled=True)]
    ppermute x1, starting transfers between devices: 3.55 us -> 6.39 us  [shards(): beyond = lax.ppermute(outer, SEQ, steps)]
    another operation x3, other arithmetic: 1.78 us -> 0.08 us  [the longest x1 0.06 us: shards(): jnp.stack([outgoing[0]] + [ring(outgoing[by], 'rep', by) for by in range(...]
  transfers between devices with their start and end apart: 16 -> 17, of which waited for: 6 -> 7; matrix products, arithmetic and copies ran while one was open for 11% -> 8% of each run, Pallas kernels for 5% -> 0%
where the time goes in v3:
time: 116 us; the launch traced here: 114 us
  starting transfers between devices  76.9 us (66%)
  waiting for transfers between devices  14.3 us (12%)
  Pallas kernels  6.87 us (6%)
  other arithmetic  6.5 us (6%)
  local copies, waits for them, and re-layouts  4.37 us (4%)
  matrix products  3.77 us (3%)
  between operations  1.51 us (1%)
    ppermute x13, starting transfers between devices, ring(): lax.ppermute(data, axis, [(i, (i + by) % count) for i in range(count)])  45.2 us
    all_to_all x3, starting transfers between devices, exchange(): return lax.all_to_all(data, axes, split_axis=0, concat_axis=0, tiled=True)  25.3 us
    ppermute x13, waiting for transfers between devices, ring(): lax.ppermute(data, axis, [(i, (i + by) % count) for i in range(count)])  7.72 us
    ppermute x1, starting transfers between devices, shards(): beyond = lax.ppermute(outer, SEQ, steps)  6.39 us
    pallas_call x1, Pallas kernels, shards(): pl.pallas_call(functools.partial(conv_kernel, share, sizes), out_shape=ja...  4.01 us
    ppermute x1, waiting for transfers between devices, shards(): beyond = lax.ppermute(outer, SEQ, steps)  3.38 us
    all_to_all x3, waiting for transfers between devices, exchange(): return lax.all_to_all(data, axes, split_axis=0, concat_axis=0, tiled=True)  3.23 us
    pallas_call x1, Pallas kernels, shards(): pl.pallas_call(functools.partial(attention_kernel, tok, sizes[0]), out_sh...  2.86 us
  transfers between devices with their start and end apart: 17, of which 7 were waited for; matrix products, arithmetic and copies ran while one was open for 8% of the time, Pallas kernels for 0%

profile of v3, /device:TPU:1, one launch (start us, length us, event | category | flops | bytes accessed | tf_op | source)
XLA Modules:
  0.0 114.2 jit_solution(16411170935122279099)
XLA Ops:
  4.4 8.3 %collective-permute-start = (bf16[24,128]{1,0:T(8,128)(2,1)S(1)}, bf16[24,128]{1,0:T(8,128)(2,1)S(1)}, u32[]{:S(2)}, u32[]{:S(2)}) collective-permute-start(bf16[24,128]{1,0:T(8,128)(2,1)S(1)} %fusion.68), channel_id=1, source_target_pairs={{0,4},{4,0},{1,5},{5,1},{2,6},{6,2},{3,7},{7,3},{8,12},{12,8},{9,1... | collective-permute-start | bytes 18440 | tf_op jit(solution)/shard_map/ppermute | solution.py:155
  14.9 11.3 %all-to-all-start.1 = ((bf16[16,72,128]{2,1,0:T(8,128)(2,1)}), bf16[16,72,128]{2,1,0:T(8,128)(2,1)S(1)}, u32[]{:S(2)}, u32[]{:S(2)}) async-start(bf16[16,72,128]{2,1,0:T(8,128)(2,1)} %bitcast.18), calls=%async_computation.1 | async-start | bytes 589824 | tf_op jit(solution)/shard_map/all_to_all | solution.py:164
  28.8 2.5 %collective-permute-start.7 = (bf16[400,128]{1,0:T(8,128)(2,1)S(1)}, bf16[400,128]{1,0:T(8,128)(2,1)S(1)}, u32[]{:S(2)}, u32[]{:S(2)}) collective-permute-start(bf16[400,128]{1,0:T(8,128)(2,1)S(1)} %get-tuple-element.24), channel_id=1, source_target_pairs={{0,3},{1,0},{2,1},{3,2},{4,7},{5,4},{6,5},{7,6},{8,11},{9,8},{10,9... | collective-permute-start | bytes 307208 | tf_op jit(solution)/shard_map/ppermute | solution.py:155
  31.4 2.9 %collective-permute-start.6 = (bf16[400,128]{1,0:T(8,128)(2,1)S(1)}, bf16[400,128]{1,0:T(8,128)(2,1)S(1)}, u32[]{:S(2)}, u32[]{:S(2)}) collective-permute-start(bf16[400,128]{1,0:T(8,128)(2,1)S(1)} %get-tuple-element.25), channel_id=1, source_target_pairs={{0,2},{1,3},{2,0},{3,1},{4,6},{5,7},{6,4},{7,5},{8,10},{9,11},{10,... | collective-permute-start | bytes 307208 | tf_op jit(solution)/shard_map/ppermute | solution.py:155
  34.2 2.3 %collective-permute-start.5 = (bf16[400,128]{1,0:T(8,128)(2,1)S(1)}, bf16[400,128]{1,0:T(8,128)(2,1)S(1)}, u32[]{:S(2)}, u32[]{:S(2)}) collective-permute-start(bf16[400,128]{1,0:T(8,128)(2,1)S(1)} %get-tuple-element.23), channel_id=1, source_target_pairs={{0,1},{1,2},{2,3},{3,0},{4,5},{5,6},{6,7},{7,4},{8,9},{9,10},{10,1... | collective-permute-start | bytes 307208 | tf_op jit(solution)/shard_map/ppermute | solution.py:155
  37.3 1.2 %all-to-all-done.1 = bf16[16,72,128]{2,1,0:T(8,128)(2,1)S(1)} async-done(((bf16[16,72,128]{2,1,0:T(8,128)(2,1)}), bf16[16,72,128]{2,1,0:T(8,128)(2,1)S(1)}, u32[]{:S(2)}, u32[]{:S(2)}) %all-to-all-start.1) | async-done | bytes 294944 | tf_op jit(solution)/shard_map/all_to_all | solution.py:164
  38.6 6.4 %all-to-all-start = ((bf16[16,104,128]{2,1,0:T(8,128)(2,1)}), bf16[16,104,128]{2,1,0:T(8,128)(2,1)S(1)}, u32[]{:S(2)}, u32[]{:S(2)}) async-start(bf16[16,104,128]{2,1,0:T(8,128)(2,1)} %pad_maximum_fusion), calls=%async_computation | async-start | bytes 851968 | tf_op jit(solution)/shard_map/all_to_all | solution.py:164
  47.2 3.3 %collective-permute-start.1 = (bf16[1152,128]{1,0:T(8,128)(2,1)S(1)}, bf16[1152,128]{1,0:T(8,128)(2,1)S(1)}, u32[]{:S(2)}, u32[]{:S(2)}) collective-permute-start(bf16[1152,128]{1,0:T(8,128)(2,1)S(1)} %maximum_maximum_fusion.refs_0_), channel_id=1, source_target_pairs={{0,128},{128,256},{256,384},{384,0},{1,129},{129,257},{257,385},{3... | collective-permute-start | bytes 884744 | tf_op jit(solution)/shard_map/ppermute | solution.py:155
  50.5 3.2 %collective-permute-start.2 = (bf16[1152,128]{1,0:T(8,128)(2,1)S(1)}, bf16[1152,128]{1,0:T(8,128)(2,1)S(1)}, u32[]{:S(2)}, u32[]{:S(2)}) collective-permute-start(bf16[1152,128]{1,0:T(8,128)(2,1)S(1)} %maximum_maximum_fusion.refs_0_), channel_id=1, source_target_pairs={{0,384},{128,0},{256,128},{384,256},{1,385},{129,1},{257,129},{385... | collective-permute-start | bytes 884744 | tf_op jit(solution)/shard_map/ppermute | solution.py:155
  53.9 3.1 %collective-permute-start.4 = (bf16[1152,128]{1,0:T(8,128)(2,1)S(1)}, bf16[1152,128]{1,0:T(8,128)(2,1)S(1)}, u32[]{:S(2)}, u32[]{:S(2)}) collective-permute-start(bf16[1152,128]{1,0:T(8,128)(2,1)S(1)} %maximum_maximum_fusion.refs_0_), channel_id=1, source_target_pairs={{0,256},{128,384},{256,0},{384,128},{1,257},{129,385},{257,1},{385... | collective-permute-start | bytes 884744 | tf_op jit(solution)/shard_map/ppermute | solution.py:155
  58.3 3.4 %collective-permute-done.2.refs_2_ = bf16[1152,128]{1,0:T(8,128)(2,1)S(1)} collective-permute-done((bf16[1152,128]{1,0:T(8,128)(2,1)S(1)}, bf16[1152,128]{1,0:T(8,128)(2,1)S(1)}, u32[]{:S(2)}, u32[]{:S(2)}) %collective-permute-start.2) | collective-permute-done | bytes 294944 | tf_op jit(solution)/shard_map/ppermute | solution.py:155
  62.6 4.4 %collective-permute-start.3 = (bf16[1040,128]{1,0:T(8,128)(2,1)S(1)}, bf16[1040,128]{1,0:T(8,128)(2,1)S(1)}, u32[]{:S(2)}, u32[]{:S(2)}) collective-permute-start(bf16[1040,128]{1,0:T(8,128)(2,1)S(1)} %pad_maximum_fusion.3), channel_id=1, source_target_pairs={{0,256},{256,0},{1,257},{257,1},{2,258},{258,2},{3,259},{259,3},{4... | collective-permute-start | bytes 798728 | tf_op jit(solution)/shard_map/ppermute | solution.py:155
  67.0 6.4 %collective-permute-start.8 = (bf16[4,208,128]{2,1,0:T(8,128)(2,1)S(1)}, bf16[4,208,128]{2,1,0:T(8,128)(2,1)S(1)}, u32[]{:S(2)}, u32[]{:S(2)}) collective-permute-start(bf16[4,208,128]{2,1,0:T(8,128)(2,1)S(1)} %fusion.14), channel_id=1, source_target_pairs={{8,16},{16,8},{24,32},{32,24},{40,48},{48,40},{56,64},{64,56},{72,... | collective-permute-start | bytes 638984 | tf_op jit(solution)/shard_map/ppermute | solution.py:294
  73.5 3.4 %collective-permute-done.8 = bf16[4,208,128]{2,1,0:T(8,128)(2,1)S(1)} collective-permute-done((bf16[4,208,128]{2,1,0:T(8,128)(2,1)S(1)}, bf16[4,208,128]{2,1,0:T(8,128)(2,1)S(1)}, u32[]{:S(2)}, u32[]{:S(2)}) %collective-permute-start.8) | collective-permute-done | bytes 213024 | tf_op jit(solution)/shard_map/ppermute | solution.py:294
  77.0 1.9 %collective-permute-start.9 = (bf16[4512,128]{1,0:T(8,128)(2,1)S(1)}, bf16[4512,128]{1,0:T(8,128)(2,1)S(1)}, u32[]{:S(2)}, u32[]{:S(2)}) collective-permute-start(bf16[4512,128]{1,0:T(8,128)(2,1)S(1)} %constant_dynamic-update-slice_fusion.mine_ref), channel_id=1, source_target_pairs={{0,8},{8,0},{1,9},{9,1},{2,10},{10,2},{3,11},{11,3},{4,12},{12,4},... | collective-permute-start | bytes 3465224 | tf_op jit(solution)/shard_map/ppermute | solution.py:155
  79.4 2.3 %collective-permute-done.9.theirs_ref = bf16[4512,128]{1,0:T(8,128)(2,1)S(1)} collective-permute-done((bf16[4512,128]{1,0:T(8,128)(2,1)S(1)}, bf16[4512,128]{1,0:T(8,128)(2,1)S(1)}, u32[]{:S(2)}, u32[]{:S(2)}) %collective-permute-start.9) | collective-permute-done | bytes 1155104 | tf_op jit(solution)/shard_map/ppermute | solution.py:155
  81.7 2.9 %attention.1 = bf16[512,128]{1,0:T(8,128)(2,1)} custom-call(bf16[16,104,128]{2,1,0:T(8,128)(2,1)S(1)} %all-to-all-done.q_ref, bf16[4512,128]{1,0:T(8,128)(2,1)S(1)} %constant_dynamic-update-slice_fusion.mine_ref, bf16[4512,128]{1,0:T(8,128)(2,1)S(1)} %collective-permute-done.9.theirs_ref, f32[512,1]{1,0:T(8,128)S(1)} %reshape.474.qid_ref), custom_call_target="tpu_custom_call" | custom-call | flops 536870912 | bytes 1048576 | tf_op jit(solution)/shard_map/attention/pallas_call | solution.py:310
  84.5 4.0 %convolution.19 = bf16[4,384,128]{2,1,0:T(8,128)(2,1)S(1)} custom-call(s32[6]{0:T(128)S(1)} %pad_add_fusion.place_ref, bf16[4512,128]{1,0:T(8,128)(2,1)S(1)} %constant_dynamic-update-slice_fusion.mine_ref, bf16[4512,128]{1,0:T(8,128)(2,1)S(1)} %collective-permute-done.9.theirs_ref, bf16[1152,128]{1,0:T(8,128)(2,1)S(1)} %maximum_maximum_fusion.refs_0_, ...), custom_call_target="tpu_custom_call" | custom-call | flops 2147483648 | bytes 1327104 | tf_op jit(solution)/shard_map/convolution/pallas_call | solution.py:324
  88.6 3.2 %collective-permute-start.12 = (bf16[384,128]{1,0:T(8,128)(2,1)S(1)}, bf16[384,128]{1,0:T(8,128)(2,1)S(1)}, u32[]{:S(2)}, u32[]{:S(2)}) collective-permute-start(bf16[384,128]{1,0:T(8,128)(2,1)S(1)} %get-tuple-element.27), channel_id=1, source_target_pairs={{0,1},{1,2},{2,3},{3,0},{4,5},{5,6},{6,7},{7,4},{8,9},{9,10},{10,1... | collective-permute-start | bytes 294920 | tf_op jit(solution)/shard_map/ppermute | solution.py:155
  91.8 3.8 %collective-permute-start.11 = (bf16[384,128]{1,0:T(8,128)(2,1)S(1)}, bf16[384,128]{1,0:T(8,128)(2,1)S(1)}, u32[]{:S(2)}, u32[]{:S(2)}) collective-permute-start(bf16[384,128]{1,0:T(8,128)(2,1)S(1)} %get-tuple-element.28), channel_id=1, source_target_pairs={{0,2},{1,3},{2,0},{3,1},{4,6},{5,7},{6,4},{7,5},{8,10},{9,11},{10,... | collective-permute-start | bytes 294920 | tf_op jit(solution)/shard_map/ppermute | solution.py:155
  95.6 3.0 %collective-permute-start.10 = (bf16[384,128]{1,0:T(8,128)(2,1)S(1)}, bf16[384,128]{1,0:T(8,128)(2,1)S(1)}, u32[]{:S(2)}, u32[]{:S(2)}) collective-permute-start(bf16[384,128]{1,0:T(8,128)(2,1)S(1)} %get-tuple-element.26), channel_id=1, source_target_pairs={{0,3},{1,0},{2,1},{3,2},{4,7},{5,4},{6,5},{7,6},{8,11},{9,8},{10,9... | collective-permute-start | bytes 294920 | tf_op jit(solution)/shard_map/ppermute | solution.py:155
  98.5 7.6 %all-to-all-start.2 = ((bf16[16,32,128]{2,1,0:T(8,128)(2,1)}), bf16[16,32,128]{2,1,0:T(8,128)(2,1)S(1)}, u32[]{:S(2)}, u32[]{:S(2)}) async-start(bf16[16,32,128]{2,1,0:T(8,128)(2,1)} %bitcast.38), calls=%async_computation.2 | async-start | bytes 262144 | tf_op jit(solution)/shard_map/all_to_all | solution.py:164
  106.5 3.4 %collective-permute-start.13 = (bf16[128,192]{1,0:T(8,128)(2,1)S(1)}, bf16[128,192]{1,0:T(8,128)(2,1)S(1)}, u32[]{:S(2)}, u32[]{:S(2)}) collective-permute-start(bf16[128,192]{1,0:T(8,128)(2,1)S(1)} %fusion.39), channel_id=1, source_target_pairs={{0,8},{8,0},{1,9},{9,1},{2,10},{10,2},{3,11},{11,3},{4,12},{12,4},... | collective-permute-start | bytes 147464 | tf_op jit(solution)/shard_map/ppermute | solution.py:155
  111.6 2.0 %all-to-all-done.2 = bf16[16,32,128]{2,1,0:T(8,128)(2,1)S(1)} async-done(((bf16[16,32,128]{2,1,0:T(8,128)(2,1)}), bf16[16,32,128]{2,1,0:T(8,128)(2,1)S(1)}, u32[]{:S(2)}, u32[]{:S(2)}) %all-to-all-start.2) | async-done | bytes 131104 | tf_op jit(solution)/shard_map/all_to_all | solution.py:164
  (132 shorter events, 16.7 us)
Async XLA Ops:
  0.6 25.7 %copy-start = (bf16[32,2048]{1,0:T(8,128)(2,1)S(1)}, bf16[32,2048]{1,0:T(8,128)(2,1)}, u32[]{:S(2)}) copy-start(bf16[32,2048]{1,0:T(8,128)(2,1)} %param.12) | copy-start | bytes 393220
  0.6 25.6 %copy-start.7 = (bf16[1,2,64,384]{3,2,1,0:T(8,128)(2,1)S(1)}, bf16[1,2,64,384]{3,2,1,0:T(8,128)(2,1)}, u32[]{:S(2)}) copy-start(bf16[1,2,64,384]{3,2,1,0:T(8,128)(2,1)} %param.16) | copy-start | bytes 294916
  0.7 25.7 %copy-start.14 = (s32[32]{0:T(128)S(1)}, s32[32]{0:T(128)}, u32[]{:S(2)}) copy-start(s32[32]{0:T(128)} %param.15) | copy-start | bytes 388
  4.4 23.2 %collective-permute-start = (bf16[24,128]{1,0:T(8,128)(2,1)S(1)}, bf16[24,128]{1,0:T(8,128)(2,1)S(1)}, u32[]{:S(2)}, u32[]{:S(2)}) collective-permute-start(bf16[24,128]{1,0:T(8,128)(2,1)S(1)} %fusion.68), channel_id=1, source_target_pairs={{0,4},{4,0},{1,5},{5,1},{2,6},{6,2},{3,7},{7,3},{8,12},{12,8},{9,1... | collective-permute-start | bytes 18440 | tf_op jit(solution)/shard_map/ppermute | solution.py:155
  13.9 13.0 %copy-start.13 = (f32[384]{0:T(512)S(1)}, f32[384]{0:T(512)}, u32[]{:S(2)}) copy-start(f32[384]{0:T(512)} %param.18) | copy-start | bytes 4612
  14.1 13.0 %copy-start.10 = (bf16[2,2,64,384]{3,2,1,0:T(8,128)(2,1)S(1)}, bf16[2,2,64,384]{3,2,1,0:T(8,128)(2,1)}, u32[]{:S(2)}) copy-start(bf16[2,2,64,384]{3,2,1,0:T(8,128)(2,1)} %param.17) | copy-start | bytes 589828
  14.9 23.6 %all-to-all-start.1 = ((bf16[16,72,128]{2,1,0:T(8,128)(2,1)}), bf16[16,72,128]{2,1,0:T(8,128)(2,1)S(1)}, u32[]{:S(2)}, u32[]{:S(2)}) async-start(bf16[16,72,128]{2,1,0:T(8,128)(2,1)} %bitcast.18), calls=%async_computation.1 | async-start | bytes 589824 | tf_op jit(solution)/shard_map/all_to_all | solution.py:164
  28.8 24.9 %collective-permute-start.7 = (bf16[400,128]{1,0:T(8,128)(2,1)S(1)}, bf16[400,128]{1,0:T(8,128)(2,1)S(1)}, u32[]{:S(2)}, u32[]{:S(2)}) collective-permute-start(bf16[400,128]{1,0:T(8,128)(2,1)S(1)} %get-tuple-element.24), channel_id=1, source_target_pairs={{0,3},{1,0},{2,1},{3,2},{4,7},{5,4},{6,5},{7,6},{8,11},{9,8},{10,9... | collective-permute-start | bytes 307208 | tf_op jit(solution)/shard_map/ppermute | solution.py:155
  31.4 22.4 %collective-permute-start.6 = (bf16[400,128]{1,0:T(8,128)(2,1)S(1)}, bf16[400,128]{1,0:T(8,128)(2,1)S(1)}, u32[]{:S(2)}, u32[]{:S(2)}) collective-permute-start(bf16[400,128]{1,0:T(8,128)(2,1)S(1)} %get-tuple-element.25), channel_id=1, source_target_pairs={{0,2},{1,3},{2,0},{3,1},{4,6},{5,7},{6,4},{7,5},{8,10},{9,11},{10,... | collective-permute-start | bytes 307208 | tf_op jit(solution)/shard_map/ppermute | solution.py:155
  34.2 19.5 %collective-permute-start.5 = (bf16[400,128]{1,0:T(8,128)(2,1)S(1)}, bf16[400,128]{1,0:T(8,128)(2,1)S(1)}, u32[]{:S(2)}, u32[]{:S(2)}) collective-permute-start(bf16[400,128]{1,0:T(8,128)(2,1)S(1)} %get-tuple-element.23), channel_id=1, source_target_pairs={{0,1},{1,2},{2,3},{3,0},{4,5},{5,6},{6,7},{7,4},{8,9},{9,10},{10,1... | collective-permute-start | bytes 307208 | tf_op jit(solution)/shard_map/ppermute | solution.py:155
  38.6 18.5 %all-to-all-start = ((bf16[16,104,128]{2,1,0:T(8,128)(2,1)}), bf16[16,104,128]{2,1,0:T(8,128)(2,1)S(1)}, u32[]{:S(2)}, u32[]{:S(2)}) async-start(bf16[16,104,128]{2,1,0:T(8,128)(2,1)} %pad_maximum_fusion), calls=%async_computation | async-start | bytes 851968 | tf_op jit(solution)/shard_map/all_to_all | solution.py:164
  47.2 11.1 %collective-permute-start.1 = (bf16[1152,128]{1,0:T(8,128)(2,1)S(1)}, bf16[1152,128]{1,0:T(8,128)(2,1)S(1)}, u32[]{:S(2)}, u32[]{:S(2)}) collective-permute-start(bf16[1152,128]{1,0:T(8,128)(2,1)S(1)} %maximum_maximum_fusion.refs_0_), channel_id=1, source_target_pairs={{0,128},{128,256},{256,384},{384,0},{1,129},{129,257},{257,385},{3... | collective-permute-start | bytes 884744 | tf_op jit(solution)/shard_map/ppermute | solution.py:155
  50.5 11.1 %collective-permute-start.2 = (bf16[1152,128]{1,0:T(8,128)(2,1)S(1)}, bf16[1152,128]{1,0:T(8,128)(2,1)S(1)}, u32[]{:S(2)}, u32[]{:S(2)}) collective-permute-start(bf16[1152,128]{1,0:T(8,128)(2,1)S(1)} %maximum_maximum_fusion.refs_0_), channel_id=1, source_target_pairs={{0,384},{128,0},{256,128},{384,256},{1,385},{129,1},{257,129},{385... | collective-permute-start | bytes 884744 | tf_op jit(solution)/shard_map/ppermute | solution.py:155
  53.9 19.5 %collective-permute-start.4 = (bf16[1152,128]{1,0:T(8,128)(2,1)S(1)}, bf16[1152,128]{1,0:T(8,128)(2,1)S(1)}, u32[]{:S(2)}, u32[]{:S(2)}) collective-permute-start(bf16[1152,128]{1,0:T(8,128)(2,1)S(1)} %maximum_maximum_fusion.refs_0_), channel_id=1, source_target_pairs={{0,256},{128,384},{256,0},{384,128},{1,257},{129,385},{257,1},{385... | collective-permute-start | bytes 884744 | tf_op jit(solution)/shard_map/ppermute | solution.py:155
  62.6 10.8 %collective-permute-start.3 = (bf16[1040,128]{1,0:T(8,128)(2,1)S(1)}, bf16[1040,128]{1,0:T(8,128)(2,1)S(1)}, u32[]{:S(2)}, u32[]{:S(2)}) collective-permute-start(bf16[1040,128]{1,0:T(8,128)(2,1)S(1)} %pad_maximum_fusion.3), channel_id=1, source_target_pairs={{0,256},{256,0},{1,257},{257,1},{2,258},{258,2},{3,259},{259,3},{4... | collective-permute-start | bytes 798728 | tf_op jit(solution)/shard_map/ppermute | solution.py:155
  67.0 9.9 %collective-permute-start.8 = (bf16[4,208,128]{2,1,0:T(8,128)(2,1)S(1)}, bf16[4,208,128]{2,1,0:T(8,128)(2,1)S(1)}, u32[]{:S(2)}, u32[]{:S(2)}) collective-permute-start(bf16[4,208,128]{2,1,0:T(8,128)(2,1)S(1)} %fusion.14), channel_id=1, source_target_pairs={{8,16},{16,8},{24,32},{32,24},{40,48},{48,40},{56,64},{64,56},{72,... | collective-permute-start | bytes 638984 | tf_op jit(solution)/shard_map/ppermute | solution.py:294
  77.0 4.7 %collective-permute-start.9 = (bf16[4512,128]{1,0:T(8,128)(2,1)S(1)}, bf16[4512,128]{1,0:T(8,128)(2,1)S(1)}, u32[]{:S(2)}, u32[]{:S(2)}) collective-permute-start(bf16[4512,128]{1,0:T(8,128)(2,1)S(1)} %constant_dynamic-update-slice_fusion.mine_ref), channel_id=1, source_target_pairs={{0,8},{8,0},{1,9},{9,1},{2,10},{10,2},{3,11},{11,3},{4,12},{12,4},... | collective-permute-start | bytes 3465224 | tf_op jit(solution)/shard_map/ppermute | solution.py:155
  79.4 5.2 %copy-start.2 = (bf16[1152,128]{1,0:T(8,128)(2,1)S(1)}, bf16[1152,128]{1,0:T(8,128)(2,1)}, u32[]{:S(2)}) copy-start(bf16[1152,128]{1,0:T(8,128)(2,1)} %copy-done.1) | copy-start | bytes 884740
  79.4 5.2 %copy-start.4 = (bf16[1152,128]{1,0:T(8,128)(2,1)S(1)}, bf16[1152,128]{1,0:T(8,128)(2,1)}, u32[]{:S(2)}) copy-start(bf16[1152,128]{1,0:T(8,128)(2,1)} %copy-done.3) | copy-start | bytes 884740
  88.6 17.6 %collective-permute-start.12 = (bf16[384,128]{1,0:T(8,128)(2,1)S(1)}, bf16[384,128]{1,0:T(8,128)(2,1)S(1)}, u32[]{:S(2)}, u32[]{:S(2)}) collective-permute-start(bf16[384,128]{1,0:T(8,128)(2,1)S(1)} %get-tuple-element.27), channel_id=1, source_target_pairs={{0,1},{1,2},{2,3},{3,0},{4,5},{5,6},{6,7},{7,4},{8,9},{9,10},{10,1... | collective-permute-start | bytes 294920 | tf_op jit(solution)/shard_map/ppermute | solution.py:155
  91.8 14.4 %collective-permute-start.11 = (bf16[384,128]{1,0:T(8,128)(2,1)S(1)}, bf16[384,128]{1,0:T(8,128)(2,1)S(1)}, u32[]{:S(2)}, u32[]{:S(2)}) collective-permute-start(bf16[384,128]{1,0:T(8,128)(2,1)S(1)} %get-tuple-element.28), channel_id=1, source_target_pairs={{0,2},{1,3},{2,0},{3,1},{4,6},{5,7},{6,4},{7,5},{8,10},{9,11},{10,... | collective-permute-start | bytes 294920 | tf_op jit(solution)/shard_map/ppermute | solution.py:155
  95.6 10.6 %collective-permute-start.10 = (bf16[384,128]{1,0:T(8,128)(2,1)S(1)}, bf16[384,128]{1,0:T(8,128)(2,1)S(1)}, u32[]{:S(2)}, u32[]{:S(2)}) collective-permute-start(bf16[384,128]{1,0:T(8,128)(2,1)S(1)} %get-tuple-element.26), channel_id=1, source_target_pairs={{0,3},{1,0},{2,1},{3,2},{4,7},{5,4},{6,5},{7,6},{8,11},{9,8},{10,9... | collective-permute-start | bytes 294920 | tf_op jit(solution)/shard_map/ppermute | solution.py:155
  98.5 15.0 %all-to-all-start.2 = ((bf16[16,32,128]{2,1,0:T(8,128)(2,1)}), bf16[16,32,128]{2,1,0:T(8,128)(2,1)S(1)}, u32[]{:S(2)}, u32[]{:S(2)}) async-start(bf16[16,32,128]{2,1,0:T(8,128)(2,1)} %bitcast.38), calls=%async_computation.2 | async-start | bytes 262144 | tf_op jit(solution)/shard_map/all_to_all | solution.py:164
  106.5 4.3 %collective-permute-start.13 = (bf16[128,192]{1,0:T(8,128)(2,1)S(1)}, bf16[128,192]{1,0:T(8,128)(2,1)S(1)}, u32[]{:S(2)}, u32[]{:S(2)}) collective-permute-start(bf16[128,192]{1,0:T(8,128)(2,1)S(1)} %fusion.39), channel_id=1, source_target_pairs={{0,8},{8,0},{1,9},{9,1},{2,10},{10,2},{3,11},{11,3},{4,12},{12,4},... | collective-permute-start | bytes 147464 | tf_op jit(solution)/shard_map/ppermute | solution.py:155
  (8 other events, 17.3 us)

commit v4 on v3

--- a/solution.py
+++ b/solution.py
@@ -86,7 +86,7 @@
 SLOTS = 8
 
 
-def convolve(share, taps, slab_ref, planes, out_ref, pad_ref, low_ref, high_ref):
+def convolve(share, taps, order, slab_ref, planes, out_ref, pad_ref, low_ref, high_ref):
     _, parts, _, high, cols, lanes = slab_ref.shape
     rows = high - 2
     cells = rows * cols
@@ -116,10 +116,10 @@
     lane = lax.broadcasted_iota(jnp.int32, (cells // 2, 128), 1)
     for part in range(parts):
         low, top = low_ref[part], high_ref[part]
-        out_ref[part, :cells, :] = (low[:, :128] + top[:, :128]).astype(BF)
+        out_ref[order(part), :cells, :] = (low[:, :128] + top[:, :128]).astype(BF)
         rest = low[:, 128:] + pltpu.roll(top[:, 128:], 64, axis=1)
         rest = jnp.where(lane < 64, rest[: cells // 2], pltpu.roll(rest[cells // 2 :], 64, axis=1))
-        out_ref[part, cells:, :] = rest.astype(BF)
+        out_ref[order(part), cells:, :] = rest.astype(BF)
 
 
 def attention_kernel(tok, block, q_ref, mine_ref, theirs_ref, qid_ref, out_ref):
@@ -135,7 +135,10 @@
         lay_out(
             own, left, ref.at[pl.ds(2 * block, cells)], ref.at[pl.ds(2 * block + cells, halo)], slab_ref
         )
-    convolve(share, lambda p: place_ref[2 + p], slab_ref, planes, conv_ref, pad_ref, low_ref, high_ref)
+    convolve(
+        share, lambda p: place_ref[2 + p], lambda i: place_ref[2 + len(planes) + i],
+        slab_ref, planes, conv_ref, pad_ref, low_ref, high_ref,
+    )
 
 
 def activate(cells, gain):
@@ -153,6 +156,10 @@
 def ring(data, axis, by):
     count = lax.axis_size(axis)
     return lax.ppermute(data, axis, [(i, (i + by) % count) for i in range(count)])
+
+
+def swap(data, axis, bit):
+    return lax.ppermute(data, axis, [(i, i ^ bit) for i in range(lax.axis_size(axis))])
 
 
 def planes_of(data):
@@ -266,8 +273,8 @@
     )
     weights = (my_weight,) + planes_of(my_weight)
     taps = (27 * order) // planes
-    got, *near = lax.optimization_barrier((got,) + weights[1:3])
-    weights = weights[:1] + tuple(near) + weights[3:]
+    got, before = lax.optimization_barrier((got, weights[1]))
+    weights = (weights[0], before) + weights[2:]
 
     feat_f = features.astype(F32)
     stacked = jnp.concatenate([frame_cache, activate(features, feat_gain)], axis=0)
@@ -306,7 +313,8 @@
     theirs = ring(mine, "core", 1)
     sizes = key_vals.shape[0], cells.shape[0], beyond.shape[0]
     chip_cells = cores * tile_rows * tile_cols
-    place = jnp.concatenate([jnp.stack([me_core, me_grp]), taps]).astype(jnp.int32)
+    spots = me_rep ^ ((me_rep - jnp.arange(parts)) % parts)
+    place = jnp.concatenate([jnp.stack([me_core, me_grp]), taps, spots]).astype(jnp.int32)
     head_out = pl.pallas_call(
         functools.partial(attention_kernel, tok, sizes[0]),
         out_shape=jax.ShapeDtypeStruct((plane_tok, HEAD_DIM), BF),
@@ -342,9 +350,9 @@
     )(place, mine, theirs, *weights)
     returned = exchange(head_out.reshape(heads, tok, HEAD_DIM), HEAD_AXES)
 
-    sums_back = partial[0].astype(F32)
-    for by in range(1, parts):
-        sums_back = sums_back + ring(partial[by], "rep", parts - by).astype(F32)
+    from_two = swap(partial[2:], "rep", 2)
+    sums_back = partial[:2].astype(F32) + from_two.astype(F32)
+    sums_back = sums_back[0] + swap(sums_back[1].astype(BF), "rep", 1).astype(F32)
     tile_cells = tile_rows * tile_cols
     main_cols = sums_back[:chip_cells].reshape(cores, tile_cells, 128)
     last_cols = sums_back[chip_cells:].reshape(tile_cells, cores, 64).transpose(1, 0, 2)

time: 116 us -> 113 us (0.974)
  waiting for transfers between devices: 14.3 us -> 13 us
  starting transfers between devices: 76.9 us -> 75.7 us
    ppermute x13 -> x10, starting transfers between devices: 45.2 us -> 37.7 us  [ring(): lax.ppermute(data, axis, [(i, (i + by) % count) for i in range(count)])]
    ppermute x0 -> x2, starting transfers between devices: none -> 6.35 us  [swap(): lax.ppermute(data, axis, [(i, i ^ bit) for i in range(lax.axis_size(axis))])]
    ppermute x1, waiting for transfers between devices: 3.38 us -> 0.26 us  [shards(): beyond = lax.ppermute(outer, SEQ, steps)]
    ppermute x0 -> x2, waiting for transfers between devices: none -> 1.79 us  [swap(): lax.ppermute(data, axis, [(i, i ^ bit) for i in range(lax.axis_size(axis))])]
    ppermute x13 -> x10, waiting for transfers between devices: 7.72 us -> 6.69 us  [ring(): lax.ppermute(data, axis, [(i, (i + by) % count) for i in range(count)])]
  transfers between devices with their start and end apart: 17 -> 16, of which waited for: 7 -> 8; matrix products, arithmetic and copies ran while one was open for 8% -> 9% of each run, Pallas kernels for 0% -> 0%
where the time goes in v4:
time: 113 us; the launch traced here: 112 us
  starting transfers between devices  75.7 us (67%)
  waiting for transfers between devices  13 us (12%)
  Pallas kernels  6.87 us (6%)
  other arithmetic  6.52 us (6%)
  local copies, waits for them, and re-layouts  4.98 us (4%)
  matrix products  3.78 us (3%)
  between operations  1.47 us (1%)
    ppermute x10, starting transfers between devices, ring(): lax.ppermute(data, axis, [(i, (i + by) % count) for i in range(count)])  37.7 us
    all_to_all x3, starting transfers between devices, exchange(): return lax.all_to_all(data, axes, split_axis=0, concat_axis=0, tiled=True)  25.2 us
    ppermute x10, waiting for transfers between devices, ring(): lax.ppermute(data, axis, [(i, (i + by) % count) for i in range(count)])  6.69 us
    ppermute x1, starting transfers between devices, shards(): beyond = lax.ppermute(outer, SEQ, steps)  6.41 us
    ppermute x2, starting transfers between devices, swap(): lax.ppermute(data, axis, [(i, i ^ bit) for i in range(lax.axis_size(axis))])  6.35 us
    all_to_all x3, waiting for transfers between devices, exchange(): return lax.all_to_all(data, axes, split_axis=0, concat_axis=0, tiled=True)  4.21 us
    pallas_call x1, Pallas kernels, shards(): pl.pallas_call(functools.partial(conv_kernel, share, sizes), out_shape=ja...  4.01 us
    pallas_call x1, Pallas kernels, shards(): pl.pallas_call(functools.partial(attention_kernel, tok, sizes[0]), out_sh...  2.86 us
  transfers between devices with their start and end apart: 16, of which 8 were waited for; matrix products, arithmetic and copies ran while one was open for 9% of the time, Pallas kernels for 0%

profile of v4, /device:TPU:1, one launch (start us, length us, event | category | flops | bytes accessed | tf_op | source)
XLA Modules:
  0.0 112.2 jit_solution(18307920921666687064)
XLA Ops:
  4.4 8.3 %collective-permute-start = (bf16[24,128]{1,0:T(8,128)(2,1)S(1)}, bf16[24,128]{1,0:T(8,128)(2,1)S(1)}, u32[]{:S(2)}, u32[]{:S(2)}) collective-permute-start(bf16[24,128]{1,0:T(8,128)(2,1)S(1)} %fusion.68), channel_id=1, source_target_pairs={{0,4},{4,0},{1,5},{5,1},{2,6},{6,2},{3,7},{7,3},{8,12},{12,8},{9,1... | collective-permute-start | bytes 18440 | tf_op jit(solution)/shard_map/ppermute | solution.py:158
  12.8 1.1 convolution_convert_fusion.1
  14.9 11.3 %all-to-all-start.1 = ((bf16[16,72,128]{2,1,0:T(8,128)(2,1)}), bf16[16,72,128]{2,1,0:T(8,128)(2,1)S(1)}, u32[]{:S(2)}, u32[]{:S(2)}) async-start(bf16[16,72,128]{2,1,0:T(8,128)(2,1)} %bitcast.18), calls=%async_computation.1 | async-start | bytes 589824 | tf_op jit(solution)/shard_map/all_to_all | solution.py:171
  28.8 2.5 %collective-permute-start.7 = (bf16[400,128]{1,0:T(8,128)(2,1)S(1)}, bf16[400,128]{1,0:T(8,128)(2,1)S(1)}, u32[]{:S(2)}, u32[]{:S(2)}) collective-permute-start(bf16[400,128]{1,0:T(8,128)(2,1)S(1)} %get-tuple-element.22), channel_id=1, source_target_pairs={{0,3},{1,0},{2,1},{3,2},{4,7},{5,4},{6,5},{7,6},{8,11},{9,8},{10,9... | collective-permute-start | bytes 307208 | tf_op jit(solution)/shard_map/ppermute | solution.py:158
  31.4 2.9 %collective-permute-start.6 = (bf16[400,128]{1,0:T(8,128)(2,1)S(1)}, bf16[400,128]{1,0:T(8,128)(2,1)S(1)}, u32[]{:S(2)}, u32[]{:S(2)}) collective-permute-start(bf16[400,128]{1,0:T(8,128)(2,1)S(1)} %get-tuple-element.23), channel_id=1, source_target_pairs={{0,2},{1,3},{2,0},{3,1},{4,6},{5,7},{6,4},{7,5},{8,10},{9,11},{10,... | collective-permute-start | bytes 307208 | tf_op jit(solution)/shard_map/ppermute | solution.py:158
  34.2 2.3 %collective-permute-start.5 = (bf16[400,128]{1,0:T(8,128)(2,1)S(1)}, bf16[400,128]{1,0:T(8,128)(2,1)S(1)}, u32[]{:S(2)}, u32[]{:S(2)}) collective-permute-start(bf16[400,128]{1,0:T(8,128)(2,1)S(1)} %get-tuple-element.21), channel_id=1, source_target_pairs={{0,1},{1,2},{2,3},{3,0},{4,5},{5,6},{6,7},{7,4},{8,9},{9,10},{10,1... | collective-permute-start | bytes 307208 | tf_op jit(solution)/shard_map/ppermute | solution.py:158
  37.3 1.2 %all-to-all-done.1 = bf16[16,72,128]{2,1,0:T(8,128)(2,1)S(1)} async-done(((bf16[16,72,128]{2,1,0:T(8,128)(2,1)}), bf16[16,72,128]{2,1,0:T(8,128)(2,1)S(1)}, u32[]{:S(2)}, u32[]{:S(2)}) %all-to-all-start.1) | async-done | bytes 294944 | tf_op jit(solution)/shard_map/all_to_all | solution.py:171
  38.6 6.4 %all-to-all-start = ((bf16[16,104,128]{2,1,0:T(8,128)(2,1)}), bf16[16,104,128]{2,1,0:T(8,128)(2,1)S(1)}, u32[]{:S(2)}, u32[]{:S(2)}) async-start(bf16[16,104,128]{2,1,0:T(8,128)(2,1)} %pad_maximum_fusion), calls=%async_computation | async-start | bytes 851968 | tf_op jit(solution)/shard_map/all_to_all | solution.py:171
  47.2 3.3 %collective-permute-start.1 = (bf16[1152,128]{1,0:T(8,128)(2,1)S(1)}, bf16[1152,128]{1,0:T(8,128)(2,1)S(1)}, u32[]{:S(2)}, u32[]{:S(2)}) collective-permute-start(bf16[1152,128]{1,0:T(8,128)(2,1)S(1)} %maximum_maximum_fusion.refs_0_), channel_id=1, source_target_pairs={{0,128},{128,256},{256,384},{384,0},{1,129},{129,257},{257,385},{3... | collective-permute-start | bytes 884744 | tf_op jit(solution)/shard_map/ppermute | solution.py:158
  51.4 3.2 %collective-permute-start.3 = (bf16[1152,128]{1,0:T(8,128)(2,1)S(1)}, bf16[1152,128]{1,0:T(8,128)(2,1)S(1)}, u32[]{:S(2)}, u32[]{:S(2)}) collective-permute-start(bf16[1152,128]{1,0:T(8,128)(2,1)S(1)} %maximum_maximum_fusion.refs_0_), channel_id=1, source_target_pairs={{0,384},{128,0},{256,128},{384,256},{1,385},{129,1},{257,129},{385... | collective-permute-start | bytes 884744 | tf_op jit(solution)/shard_map/ppermute | solution.py:158
  54.6 3.1 %collective-permute-start.4 = (bf16[1152,128]{1,0:T(8,128)(2,1)S(1)}, bf16[1152,128]{1,0:T(8,128)(2,1)S(1)}, u32[]{:S(2)}, u32[]{:S(2)}) collective-permute-start(bf16[1152,128]{1,0:T(8,128)(2,1)S(1)} %maximum_maximum_fusion.refs_0_), channel_id=1, source_target_pairs={{0,256},{128,384},{256,0},{384,128},{1,257},{129,385},{257,1},{385... | collective-permute-start | bytes 884744 | tf_op jit(solution)/shard_map/ppermute | solution.py:158
  59.1 4.5 %collective-permute-start.2 = (bf16[1040,128]{1,0:T(8,128)(2,1)S(1)}, bf16[1040,128]{1,0:T(8,128)(2,1)S(1)}, u32[]{:S(2)}, u32[]{:S(2)}) collective-permute-start(bf16[1040,128]{1,0:T(8,128)(2,1)S(1)} %pad_maximum_fusion.3), channel_id=1, source_target_pairs={{0,256},{256,0},{1,257},{257,1},{2,258},{258,2},{3,259},{259,3},{4... | collective-permute-start | bytes 798728 | tf_op jit(solution)/shard_map/ppermute | solution.py:158
  63.7 6.4 %collective-permute-start.8 = (bf16[4,208,128]{2,1,0:T(8,128)(2,1)S(1)}, bf16[4,208,128]{2,1,0:T(8,128)(2,1)S(1)}, u32[]{:S(2)}, u32[]{:S(2)}) collective-permute-start(bf16[4,208,128]{2,1,0:T(8,128)(2,1)S(1)} %fusion.14), channel_id=1, source_target_pairs={{8,16},{16,8},{24,32},{32,24},{40,48},{48,40},{56,64},{64,56},{72,... | collective-permute-start | bytes 638984 | tf_op jit(solution)/shard_map/ppermute | solution.py:301
  70.1 3.4 %collective-permute-done.2 = bf16[1040,128]{1,0:T(8,128)(2,1)S(1)} collective-permute-done((bf16[1040,128]{1,0:T(8,128)(2,1)S(1)}, bf16[1040,128]{1,0:T(8,128)(2,1)S(1)}, u32[]{:S(2)}, u32[]{:S(2)}) %collective-permute-start.2) | collective-permute-done | bytes 266272 | tf_op jit(solution)/shard_map/ppermute | solution.py:158
  73.9 3.6 %collective-permute-start.9 = (bf16[4512,128]{1,0:T(8,128)(2,1)S(1)}, bf16[4512,128]{1,0:T(8,128)(2,1)S(1)}, u32[]{:S(2)}, u32[]{:S(2)}) collective-permute-start(bf16[4512,128]{1,0:T(8,128)(2,1)S(1)} %constant_dynamic-update-slice_fusion.mine_ref), channel_id=1, source_target_pairs={{0,8},{8,0},{1,9},{9,1},{2,10},{10,2},{3,11},{11,3},{4,12},{12,4},... | collective-permute-start | bytes 3465224 | tf_op jit(solution)/shard_map/ppermute | solution.py:158
  78.0 1.9 %collective-permute-done.9.theirs_ref = bf16[4512,128]{1,0:T(8,128)(2,1)S(1)} collective-permute-done((bf16[4512,128]{1,0:T(8,128)(2,1)S(1)}, bf16[4512,128]{1,0:T(8,128)(2,1)S(1)}, u32[]{:S(2)}, u32[]{:S(2)}) %collective-permute-start.9) | collective-permute-done | bytes 1155104 | tf_op jit(solution)/shard_map/ppermute | solution.py:158
  79.9 2.9 %attention.1 = bf16[512,128]{1,0:T(8,128)(2,1)} custom-call(bf16[16,104,128]{2,1,0:T(8,128)(2,1)S(1)} %all-to-all-done.q_ref, bf16[4512,128]{1,0:T(8,128)(2,1)S(1)} %constant_dynamic-update-slice_fusion.mine_ref, bf16[4512,128]{1,0:T(8,128)(2,1)S(1)} %collective-permute-done.9.theirs_ref, f32[512,1]{1,0:T(8,128)S(1)} %reshape.472.qid_ref), custom_call_target="tpu_custom_call" | custom-call | flops 536870912 | bytes 1048576 | tf_op jit(solution)/shard_map/attention/pallas_call | solution.py:318
  82.8 4.0 %convolution.19 = bf16[4,384,128]{2,1,0:T(8,128)(2,1)S(1)} custom-call(s32[10]{0:T(128)S(1)} %pad_add_fusion.place_ref, bf16[4512,128]{1,0:T(8,128)(2,1)S(1)} %constant_dynamic-update-slice_fusion.mine_ref, bf16[4512,128]{1,0:T(8,128)(2,1)S(1)} %collective-permute-done.9.theirs_ref, bf16[1152,128]{1,0:T(8,128)(2,1)S(1)} %maximum_maximum_fusion.refs_0_, ...), custom_call_target="tpu_custom_call" | custom-call | flops 2147483648 | bytes 1327104 | tf_op jit(solution)/shard_map/convolution/pallas_call | solution.py:332
  86.8 3.8 %collective-permute-start.10 = (bf16[2,384,128]{2,1,0:T(8,128)(2,1)S(1)}, bf16[2,384,128]{2,1,0:T(8,128)(2,1)S(1)}, u32[]{:S(2)}, u32[]{:S(2)}) collective-permute-start(bf16[2,384,128]{2,1,0:T(8,128)(2,1)S(1)} %slice.216), channel_id=1, source_target_pairs={{0,2},{1,3},{2,0},{3,1},{4,6},{5,7},{6,4},{7,5},{8,10},{9,11},{10,... | collective-permute-start | bytes 589832 | tf_op jit(solution)/shard_map/ppermute | solution.py:162
  90.6 7.5 %all-to-all-start.2 = ((bf16[16,32,128]{2,1,0:T(8,128)(2,1)}), bf16[16,32,128]{2,1,0:T(8,128)(2,1)S(1)}, u32[]{:S(2)}, u32[]{:S(2)}) async-start(bf16[16,32,128]{2,1,0:T(8,128)(2,1)} %bitcast.38), calls=%async_computation.2 | async-start | bytes 262144 | tf_op jit(solution)/shard_map/all_to_all | solution.py:171
  98.2 1.8 %collective-permute-done.10 = bf16[2,384,128]{2,1,0:T(8,128)(2,1)S(1)} collective-permute-done((bf16[2,384,128]{2,1,0:T(8,128)(2,1)S(1)}, bf16[2,384,128]{2,1,0:T(8,128)(2,1)S(1)}, u32[]{:S(2)}, u32[]{:S(2)}) %collective-permute-start.10) | collective-permute-done | bytes 196640 | tf_op jit(solution)/shard_map/ppermute | solution.py:162
  100.0 2.6 %collective-permute-start.11 = (bf16[384,128]{1,0:T(8,128)(2,1)S(1)}, bf16[384,128]{1,0:T(8,128)(2,1)S(1)}, u32[]{:S(2)}, u32[]{:S(2)}) collective-permute-start(bf16[384,128]{1,0:T(8,128)(2,1)S(1)} %fusion.36), channel_id=1, source_target_pairs={{0,1},{1,0},{2,3},{3,2},{4,5},{5,4},{6,7},{7,6},{8,9},{9,8},{10,11... | collective-permute-start | bytes 294920 | tf_op jit(solution)/shard_map/ppermute | solution.py:162
  102.6 3.0 %all-to-all-done.2 = bf16[16,32,128]{2,1,0:T(8,128)(2,1)S(1)} async-done(((bf16[16,32,128]{2,1,0:T(8,128)(2,1)}), bf16[16,32,128]{2,1,0:T(8,128)(2,1)S(1)}, u32[]{:S(2)}, u32[]{:S(2)}) %all-to-all-start.2) | async-done | bytes 131104 | tf_op jit(solution)/shard_map/all_to_all | solution.py:171
  106.5 4.0 %collective-permute-start.12 = (bf16[128,192]{1,0:T(8,128)(2,1)S(1)}, bf16[128,192]{1,0:T(8,128)(2,1)S(1)}, u32[]{:S(2)}, u32[]{:S(2)}) collective-permute-start(bf16[128,192]{1,0:T(8,128)(2,1)S(1)} %fusion.39), channel_id=1, source_target_pairs={{0,8},{8,0},{1,9},{9,1},{2,10},{10,2},{3,11},{11,3},{4,12},{12,4},... | collective-permute-start | bytes 147464 | tf_op jit(solution)/shard_map/ppermute | solution.py:158
  (134 shorter events, 15.8 us)
Async XLA Ops:
  0.6 25.7 %copy-start = (bf16[32,2048]{1,0:T(8,128)(2,1)S(1)}, bf16[32,2048]{1,0:T(8,128)(2,1)}, u32[]{:S(2)}) copy-start(bf16[32,2048]{1,0:T(8,128)(2,1)} %param.12) | copy-start | bytes 393220
  0.6 25.6 %copy-start.8 = (bf16[1,2,64,384]{3,2,1,0:T(8,128)(2,1)S(1)}, bf16[1,2,64,384]{3,2,1,0:T(8,128)(2,1)}, u32[]{:S(2)}) copy-start(bf16[1,2,64,384]{3,2,1,0:T(8,128)(2,1)} %param.16) | copy-start | bytes 294916
  0.7 25.7 %copy-start.15 = (s32[32]{0:T(128)S(1)}, s32[32]{0:T(128)}, u32[]{:S(2)}) copy-start(s32[32]{0:T(128)} %param.15) | copy-start | bytes 388
  4.4 23.2 %collective-permute-start = (bf16[24,128]{1,0:T(8,128)(2,1)S(1)}, bf16[24,128]{1,0:T(8,128)(2,1)S(1)}, u32[]{:S(2)}, u32[]{:S(2)}) collective-permute-start(bf16[24,128]{1,0:T(8,128)(2,1)S(1)} %fusion.68), channel_id=1, source_target_pairs={{0,4},{4,0},{1,5},{5,1},{2,6},{6,2},{3,7},{7,3},{8,12},{12,8},{9,1... | collective-permute-start | bytes 18440 | tf_op jit(solution)/shard_map/ppermute | solution.py:158
  13.9 13.0 %copy-start.14 = (f32[384]{0:T(512)S(1)}, f32[384]{0:T(512)}, u32[]{:S(2)}) copy-start(f32[384]{0:T(512)} %param.18) | copy-start | bytes 4612
  14.1 13.0 %copy-start.11 = (bf16[2,2,64,384]{3,2,1,0:T(8,128)(2,1)S(1)}, bf16[2,2,64,384]{3,2,1,0:T(8,128)(2,1)}, u32[]{:S(2)}) copy-start(bf16[2,2,64,384]{3,2,1,0:T(8,128)(2,1)} %param.17) | copy-start | bytes 589828
  14.9 23.6 %all-to-all-start.1 = ((bf16[16,72,128]{2,1,0:T(8,128)(2,1)}), bf16[16,72,128]{2,1,0:T(8,128)(2,1)S(1)}, u32[]{:S(2)}, u32[]{:S(2)}) async-start(bf16[16,72,128]{2,1,0:T(8,128)(2,1)} %bitcast.18), calls=%async_computation.1 | async-start | bytes 589824 | tf_op jit(solution)/shard_map/all_to_all | solution.py:171
  28.8 21.7 %collective-permute-start.7 = (bf16[400,128]{1,0:T(8,128)(2,1)S(1)}, bf16[400,128]{1,0:T(8,128)(2,1)S(1)}, u32[]{:S(2)}, u32[]{:S(2)}) collective-permute-start(bf16[400,128]{1,0:T(8,128)(2,1)S(1)} %get-tuple-element.22), channel_id=1, source_target_pairs={{0,3},{1,0},{2,1},{3,2},{4,7},{5,4},{6,5},{7,6},{8,11},{9,8},{10,9... | collective-permute-start | bytes 307208 | tf_op jit(solution)/shard_map/ppermute | solution.py:158
  31.4 19.2 %collective-permute-start.6 = (bf16[400,128]{1,0:T(8,128)(2,1)S(1)}, bf16[400,128]{1,0:T(8,128)(2,1)S(1)}, u32[]{:S(2)}, u32[]{:S(2)}) collective-permute-start(bf16[400,128]{1,0:T(8,128)(2,1)S(1)} %get-tuple-element.23), channel_id=1, source_target_pairs={{0,2},{1,3},{2,0},{3,1},{4,6},{5,7},{6,4},{7,5},{8,10},{9,11},{10,... | collective-permute-start | bytes 307208 | tf_op jit(solution)/shard_map/ppermute | solution.py:158
  34.2 16.3 %collective-permute-start.5 = (bf16[400,128]{1,0:T(8,128)(2,1)S(1)}, bf16[400,128]{1,0:T(8,128)(2,1)S(1)}, u32[]{:S(2)}, u32[]{:S(2)}) collective-permute-start(bf16[400,128]{1,0:T(8,128)(2,1)S(1)} %get-tuple-element.21), channel_id=1, source_target_pairs={{0,1},{1,2},{2,3},{3,0},{4,5},{5,6},{6,7},{7,4},{8,9},{9,10},{10,1... | collective-permute-start | bytes 307208 | tf_op jit(solution)/shard_map/ppermute | solution.py:158
  38.6 19.2 %all-to-all-start = ((bf16[16,104,128]{2,1,0:T(8,128)(2,1)}), bf16[16,104,128]{2,1,0:T(8,128)(2,1)S(1)}, u32[]{:S(2)}, u32[]{:S(2)}) async-start(bf16[16,104,128]{2,1,0:T(8,128)(2,1)} %pad_maximum_fusion), calls=%async_computation | async-start | bytes 851968 | tf_op jit(solution)/shard_map/all_to_all | solution.py:171
  47.2 11.1 %collective-permute-start.1 = (bf16[1152,128]{1,0:T(8,128)(2,1)S(1)}, bf16[1152,128]{1,0:T(8,128)(2,1)S(1)}, u32[]{:S(2)}, u32[]{:S(2)}) collective-permute-start(bf16[1152,128]{1,0:T(8,128)(2,1)S(1)} %maximum_maximum_fusion.refs_0_), channel_id=1, source_target_pairs={{0,128},{128,256},{256,384},{384,0},{1,129},{129,257},{257,385},{3... | collective-permute-start | bytes 884744 | tf_op jit(solution)/shard_map/ppermute | solution.py:158
  51.4 18.7 %collective-permute-start.3 = (bf16[1152,128]{1,0:T(8,128)(2,1)S(1)}, bf16[1152,128]{1,0:T(8,128)(2,1)S(1)}, u32[]{:S(2)}, u32[]{:S(2)}) collective-permute-start(bf16[1152,128]{1,0:T(8,128)(2,1)S(1)} %maximum_maximum_fusion.refs_0_), channel_id=1, source_target_pairs={{0,384},{128,0},{256,128},{384,256},{1,385},{129,1},{257,129},{385... | collective-permute-start | bytes 884744 | tf_op jit(solution)/shard_map/ppermute | solution.py:158
  54.6 15.5 %collective-permute-start.4 = (bf16[1152,128]{1,0:T(8,128)(2,1)S(1)}, bf16[1152,128]{1,0:T(8,128)(2,1)S(1)}, u32[]{:S(2)}, u32[]{:S(2)}) collective-permute-start(bf16[1152,128]{1,0:T(8,128)(2,1)S(1)} %maximum_maximum_fusion.refs_0_), channel_id=1, source_target_pairs={{0,256},{128,384},{256,0},{384,128},{1,257},{129,385},{257,1},{385... | collective-permute-start | bytes 884744 | tf_op jit(solution)/shard_map/ppermute | solution.py:158
  59.1 14.4 %collective-permute-start.2 = (bf16[1040,128]{1,0:T(8,128)(2,1)S(1)}, bf16[1040,128]{1,0:T(8,128)(2,1)S(1)}, u32[]{:S(2)}, u32[]{:S(2)}) collective-permute-start(bf16[1040,128]{1,0:T(8,128)(2,1)S(1)} %pad_maximum_fusion.3), channel_id=1, source_target_pairs={{0,256},{256,0},{1,257},{257,1},{2,258},{258,2},{3,259},{259,3},{4... | collective-permute-start | bytes 798728 | tf_op jit(solution)/shard_map/ppermute | solution.py:158
  63.7 10.2 %collective-permute-start.8 = (bf16[4,208,128]{2,1,0:T(8,128)(2,1)S(1)}, bf16[4,208,128]{2,1,0:T(8,128)(2,1)S(1)}, u32[]{:S(2)}, u32[]{:S(2)}) collective-permute-start(bf16[4,208,128]{2,1,0:T(8,128)(2,1)S(1)} %fusion.14), channel_id=1, source_target_pairs={{8,16},{16,8},{24,32},{32,24},{40,48},{48,40},{56,64},{64,56},{72,... | collective-permute-start | bytes 638984 | tf_op jit(solution)/shard_map/ppermute | solution.py:301
  73.9 6.0 %collective-permute-start.9 = (bf16[4512,128]{1,0:T(8,128)(2,1)S(1)}, bf16[4512,128]{1,0:T(8,128)(2,1)S(1)}, u32[]{:S(2)}, u32[]{:S(2)}) collective-permute-start(bf16[4512,128]{1,0:T(8,128)(2,1)S(1)} %constant_dynamic-update-slice_fusion.mine_ref), channel_id=1, source_target_pairs={{0,8},{8,0},{1,9},{9,1},{2,10},{10,2},{3,11},{11,3},{4,12},{12,4},... | collective-permute-start | bytes 3465224 | tf_op jit(solution)/shard_map/ppermute | solution.py:158
  78.0 4.8 %copy-start.2 = (bf16[1152,128]{1,0:T(8,128)(2,1)S(1)}, bf16[1152,128]{1,0:T(8,128)(2,1)}, u32[]{:S(2)}) copy-start(bf16[1152,128]{1,0:T(8,128)(2,1)} %copy-done.1) | copy-start | bytes 884740
  78.0 4.8 %copy-start.4 = (bf16[1152,128]{1,0:T(8,128)(2,1)S(1)}, bf16[1152,128]{1,0:T(8,128)(2,1)}, u32[]{:S(2)}) copy-start(bf16[1152,128]{1,0:T(8,128)(2,1)} %copy-done.3) | copy-start | bytes 884740
  78.0 4.8 %copy-start.6 = (bf16[1152,128]{1,0:T(8,128)(2,1)S(1)}, bf16[1152,128]{1,0:T(8,128)(2,1)}, u32[]{:S(2)}) copy-start(bf16[1152,128]{1,0:T(8,128)(2,1)} %copy-done.5) | copy-start | bytes 884740
  86.8 13.1 %collective-permute-start.10 = (bf16[2,384,128]{2,1,0:T(8,128)(2,1)S(1)}, bf16[2,384,128]{2,1,0:T(8,128)(2,1)S(1)}, u32[]{:S(2)}, u32[]{:S(2)}) collective-permute-start(bf16[2,384,128]{2,1,0:T(8,128)(2,1)S(1)} %slice.216), channel_id=1, source_target_pairs={{0,2},{1,3},{2,0},{3,1},{4,6},{5,7},{6,4},{7,5},{8,10},{9,11},{10,... | collective-permute-start | bytes 589832 | tf_op jit(solution)/shard_map/ppermute | solution.py:162
  90.6 15.0 %all-to-all-start.2 = ((bf16[16,32,128]{2,1,0:T(8,128)(2,1)}), bf16[16,32,128]{2,1,0:T(8,128)(2,1)S(1)}, u32[]{:S(2)}, u32[]{:S(2)}) async-start(bf16[16,32,128]{2,1,0:T(8,128)(2,1)} %bitcast.38), calls=%async_computation.2 | async-start | bytes 262144 | tf_op jit(solution)/shard_map/all_to_all | solution.py:171
  100.0 6.2 %collective-permute-start.11 = (bf16[384,128]{1,0:T(8,128)(2,1)S(1)}, bf16[384,128]{1,0:T(8,128)(2,1)S(1)}, u32[]{:S(2)}, u32[]{:S(2)}) collective-permute-start(bf16[384,128]{1,0:T(8,128)(2,1)S(1)} %fusion.36), channel_id=1, source_target_pairs={{0,1},{1,0},{2,3},{3,2},{4,5},{5,4},{6,7},{7,6},{8,9},{9,8},{10,11... | collective-permute-start | bytes 294920 | tf_op jit(solution)/shard_map/ppermute | solution.py:162
  106.5 4.9 %collective-permute-start.12 = (bf16[128,192]{1,0:T(8,128)(2,1)S(1)}, bf16[128,192]{1,0:T(8,128)(2,1)S(1)}, u32[]{:S(2)}, u32[]{:S(2)}) collective-permute-start(bf16[128,192]{1,0:T(8,128)(2,1)S(1)} %fusion.39), channel_id=1, source_target_pairs={{0,8},{8,0},{1,9},{9,1},{2,10},{10,2},{3,11},{11,3},{4,12},{12,4},... | collective-permute-start | bytes 147464 | tf_op jit(solution)/shard_map/ppermute | solution.py:158
  (8 other events, 16.6 us)

commit v5 on v4

--- a/solution.py
+++ b/solution.py
@@ -279,9 +279,9 @@
     feat_f = features.astype(F32)
     stacked = jnp.concatenate([frame_cache, activate(features, feat_gain)], axis=0)
     lane = jnp.arange(parts * lanes)
-    chan = jnp.where(
-        lane % lanes < share, parts * (lane % lanes) + (me_rep + lane // lanes) % parts, -1
-    )
+    slot = lane // lanes
+    kind = me_rep ^ (2 * (slot % 2) + slot // 2)
+    chan = jnp.where(lane % lanes < share, parts * (lane % lanes) + kind, -1)
     sort = (jnp.arange(CH)[:, None] == chan[None, :]).astype(BF)
 
     def by_class(data):
@@ -291,7 +291,9 @@
     beside = jnp.concatenate([beside[:-2], activate(beside[-2:], feat_gain)])
     beside = jnp.pad(beside, ((0, 16 - edge_count), (0, 0)))
     outgoing = jnp.concatenate([by_class(stacked.reshape(-1, CH)), by_class(beside)], axis=1)
-    cells = jnp.stack([outgoing[0]] + [ring(outgoing[by], "rep", by) for by in range(1, parts)])
+    from_one = swap(outgoing[2:], "rep", 1)
+    from_two = swap(jnp.stack([outgoing[1], from_one[1]]), "rep", 2)
+    cells = jnp.concatenate([jnp.stack([outgoing[0], from_one[0]]), from_two])
     main = cells[:, : 6 * tile_cols].reshape(parts, 3, tile_rows, tile_cols, lanes)
     ends = cells[:, 6 * tile_cols : 6 * tile_cols + 6].reshape(parts, 3, tile_rows, lanes)
     outer = jnp.where(is_upper, main[:, :, 0], main[:, :, -1]).reshape(parts, -1, lanes)
@@ -313,7 +315,7 @@
     theirs = ring(mine, "core", 1)
     sizes = key_vals.shape[0], cells.shape[0], beyond.shape[0]
     chip_cells = cores * tile_rows * tile_cols
-    spots = me_rep ^ ((me_rep - jnp.arange(parts)) % parts)
+    spots = jnp.arange(parts)
     place = jnp.concatenate([jnp.stack([me_core, me_grp]), taps, spots]).astype(jnp.int32)
     head_out = pl.pallas_call(
         functools.partial(attention_kernel, tok, sizes[0]),

time: 113 us -> 117 us (1.035)
  waiting for transfers between devices: 13 us -> 16.7 us
  starting transfers between devices: 75.7 us -> 73.5 us
  other arithmetic: 6.52 us -> 8.45 us
    ppermute x10 -> x7, starting transfers between devices: 37.7 us -> 29.6 us  [ring(): lax.ppermute(data, axis, [(i, (i + by) % count) for i in range(count)])]
    ppermute x2 -> x4, waiting for transfers between devices: 1.79 us -> 6.7 us  [swap(): lax.ppermute(data, axis, [(i, i ^ bit) for i in range(lax.axis_size(axis))])]
    ppermute x2 -> x4, starting transfers between devices: 6.35 us -> 10.4 us  [swap(): lax.ppermute(data, axis, [(i, i ^ bit) for i in range(lax.axis_size(axis))])]
    all_to_all x3, starting transfers between devices: 25.2 us -> 26.9 us  [exchange(): return lax.all_to_all(data, axes, split_axis=0, concat_axis=0, tiled=True)]
    ppermute x10 -> x7, waiting for transfers between devices: 6.69 us -> 6 us  [ring(): lax.ppermute(data, axis, [(i, (i + by) % count) for i in range(count)])]
  transfers between devices with their start and end apart: 16 -> 15, of which waited for: 8 -> 7; matrix products, arithmetic and copies ran while one was open for 9% -> 10% of each run, Pallas kernels for 0% -> 0%
where the time goes in v5:
time: 117 us; the launch traced here: 116 us
  starting transfers between devices  73.5 us (63%)
  waiting for transfers between devices  16.7 us (14%)
  other arithmetic  8.45 us (7%)
  Pallas kernels  6.87 us (6%)
  local copies, waits for them, and re-layouts  5.61 us (5%)
  matrix products  3.77 us (3%)
  between operations  1.51 us (1%)
    ppermute x7, starting transfers between devices, ring(): lax.ppermute(data, axis, [(i, (i + by) % count) for i in range(count)])  29.6 us
    all_to_all x3, starting transfers between devices, exchange(): return lax.all_to_all(data, axes, split_axis=0, concat_axis=0, tiled=True)  26.9 us
    ppermute x4, starting transfers between devices, swap(): lax.ppermute(data, axis, [(i, i ^ bit) for i in range(lax.axis_size(axis))])  10.4 us
    ppermute x4, waiting for transfers between devices, swap(): lax.ppermute(data, axis, [(i, i ^ bit) for i in range(lax.axis_size(axis))])  6.7 us
    ppermute x1, starting transfers between devices, shards(): beyond = lax.ppermute(outer, SEQ, steps)  6.55 us
    ppermute x7, waiting for transfers between devices, ring(): lax.ppermute(data, axis, [(i, (i + by) % count) for i in range(count)])  6 us
    pallas_call x1, Pallas kernels, shards(): pl.pallas_call(functools.partial(conv_kernel, share, sizes), out_shape=ja...  4.01 us
    all_to_all x3, waiting for transfers between devices, exchange(): return lax.all_to_all(data, axes, split_axis=0, concat_axis=0, tiled=True)  3.79 us
  transfers between devices with their start and end apart: 15, of which 7 were waited for; matrix products, arithmetic and copies ran while one was open for 10% of the time, Pallas kernels for 0%

profile of v5, /device:TPU:1, one launch (start us, length us, event | category | flops | bytes accessed | tf_op | source)
XLA Modules:
  0.0 116.4 jit_solution(7154469354477771227)
XLA Ops:
  0.7 1.1 fusion.11
  4.5 8.3 %collective-permute-start = (bf16[24,128]{1,0:T(8,128)(2,1)S(1)}, bf16[24,128]{1,0:T(8,128)(2,1)S(1)}, u32[]{:S(2)}, u32[]{:S(2)}) collective-permute-start(bf16[24,128]{1,0:T(8,128)(2,1)S(1)} %fusion.66), channel_id=1, source_target_pairs={{0,4},{4,0},{1,5},{5,1},{2,6},{6,2},{3,7},{7,3},{8,12},{12,8},{9,1... | collective-permute-start | bytes 18440 | tf_op jit(solution)/shard_map/ppermute | solution.py:158
  12.8 1.1 convolution_convert_fusion.1
  14.9 11.3 %all-to-all-start.1 = ((bf16[16,72,128]{2,1,0:T(8,128)(2,1)}), bf16[16,72,128]{2,1,0:T(8,128)(2,1)S(1)}, u32[]{:S(2)}, u32[]{:S(2)}) async-start(bf16[16,72,128]{2,1,0:T(8,128)(2,1)} %bitcast.18), calls=%async_computation.1 | async-start | bytes 589824 | tf_op jit(solution)/shard_map/all_to_all | solution.py:171
  29.3 2.3 %collective-permute-start.5 = (bf16[2,400,128]{2,0,1:T(2,128)(2,1)S(1)}, bf16[2,400,128]{2,0,1:T(2,128)(2,1)S(1)}, u32[]{:S(2)}, u32[]{:S(2)}) collective-permute-start(bf16[2,400,128]{2,0,1:T(2,128)(2,1)S(1)} %fusion.15), channel_id=1, source_target_pairs={{0,1},{1,0},{2,3},{3,2},{4,5},{5,4},{6,7},{7,6},{8,9},{9,8},{10,11... | collective-permute-start | bytes 614408 | tf_op jit(solution)/shard_map/ppermute | solution.py:162
  32.7 5.0 %collective-permute-done.5 = bf16[2,400,128]{2,0,1:T(2,128)(2,1)S(1)} collective-permute-done((bf16[2,400,128]{2,0,1:T(2,128)(2,1)S(1)}, bf16[2,400,128]{2,0,1:T(2,128)(2,1)S(1)}, u32[]{:S(2)}, u32[]{:S(2)}) %collective-permute-start.5) | collective-permute-done | bytes 204832 | tf_op jit(solution)/shard_map/ppermute | solution.py:162
  38.6 2.4 %collective-permute-start.6 = (bf16[2,400,128]{2,0,1:T(2,128)(2,1)S(1)}, bf16[2,400,128]{2,0,1:T(2,128)(2,1)S(1)}, u32[]{:S(2)}, u32[]{:S(2)}) collective-permute-start(bf16[2,400,128]{2,0,1:T(2,128)(2,1)S(1)} %fusion.18), channel_id=1, source_target_pairs={{0,2},{1,3},{2,0},{3,1},{4,6},{5,7},{6,4},{7,5},{8,10},{9,11},{10,... | collective-permute-start | bytes 614408 | tf_op jit(solution)/shard_map/ppermute | solution.py:162
  41.1 7.4 %all-to-all-start = ((bf16[16,104,128]{2,1,0:T(8,128)(2,1)}), bf16[16,104,128]{2,1,0:T(8,128)(2,1)S(1)}, u32[]{:S(2)}, u32[]{:S(2)}) async-start(bf16[16,104,128]{2,1,0:T(8,128)(2,1)} %pad_maximum_fusion), calls=%async_computation | async-start | bytes 851968 | tf_op jit(solution)/shard_map/all_to_all | solution.py:171
  50.7 3.3 %collective-permute-start.1 = (bf16[1152,128]{1,0:T(8,128)(2,1)S(1)}, bf16[1152,128]{1,0:T(8,128)(2,1)S(1)}, u32[]{:S(2)}, u32[]{:S(2)}) collective-permute-start(bf16[1152,128]{1,0:T(8,128)(2,1)S(1)} %maximum_maximum_fusion.refs_0_), channel_id=1, source_target_pairs={{0,128},{128,256},{256,384},{384,0},{1,129},{129,257},{257,385},{3... | collective-permute-start | bytes 884744 | tf_op jit(solution)/shard_map/ppermute | solution.py:158
  55.7 3.2 %collective-permute-start.3 = (bf16[1152,128]{1,0:T(8,128)(2,1)S(1)}, bf16[1152,128]{1,0:T(8,128)(2,1)S(1)}, u32[]{:S(2)}, u32[]{:S(2)}) collective-permute-start(bf16[1152,128]{1,0:T(8,128)(2,1)S(1)} %maximum_maximum_fusion.refs_0_), channel_id=1, source_target_pairs={{0,384},{128,0},{256,128},{384,256},{1,385},{129,1},{257,129},{385... | collective-permute-start | bytes 884744 | tf_op jit(solution)/shard_map/ppermute | solution.py:158
  58.9 3.1 %collective-permute-start.4 = (bf16[1152,128]{1,0:T(8,128)(2,1)S(1)}, bf16[1152,128]{1,0:T(8,128)(2,1)S(1)}, u32[]{:S(2)}, u32[]{:S(2)}) collective-permute-start(bf16[1152,128]{1,0:T(8,128)(2,1)S(1)} %maximum_maximum_fusion.refs_0_), channel_id=1, source_target_pairs={{0,256},{128,384},{256,0},{384,128},{1,257},{129,385},{257,1},{385... | collective-permute-start | bytes 884744 | tf_op jit(solution)/shard_map/ppermute | solution.py:158
  62.9 3.9 %collective-permute-start.2 = (bf16[1040,128]{1,0:T(8,128)(2,1)S(1)}, bf16[1040,128]{1,0:T(8,128)(2,1)S(1)}, u32[]{:S(2)}, u32[]{:S(2)}) collective-permute-start(bf16[1040,128]{1,0:T(8,128)(2,1)S(1)} %pad_maximum_fusion.3), channel_id=1, source_target_pairs={{0,256},{256,0},{1,257},{257,1},{2,258},{258,2},{3,259},{259,3},{4... | collective-permute-start | bytes 798728 | tf_op jit(solution)/shard_map/ppermute | solution.py:158
  67.0 6.6 %collective-permute-start.7 = (bf16[4,208,128]{2,1,0:T(8,128)(2,1)S(1)}, bf16[4,208,128]{2,1,0:T(8,128)(2,1)S(1)}, u32[]{:S(2)}, u32[]{:S(2)}) collective-permute-start(bf16[4,208,128]{2,1,0:T(8,128)(2,1)S(1)} %fusion.14), channel_id=1, source_target_pairs={{8,16},{16,8},{24,32},{32,24},{40,48},{48,40},{56,64},{64,56},{72,... | collective-permute-start | bytes 638984 | tf_op jit(solution)/shard_map/ppermute | solution.py:303
  73.6 3.4 %collective-permute-done.2 = bf16[1040,128]{1,0:T(8,128)(2,1)S(1)} collective-permute-done((bf16[1040,128]{1,0:T(8,128)(2,1)S(1)}, bf16[1040,128]{1,0:T(8,128)(2,1)S(1)}, u32[]{:S(2)}, u32[]{:S(2)}) %collective-permute-start.2) | collective-permute-done | bytes 266272 | tf_op jit(solution)/shard_map/ppermute | solution.py:158
  77.4 3.7 %collective-permute-start.8 = (bf16[4512,128]{1,0:T(8,128)(2,1)S(1)}, bf16[4512,128]{1,0:T(8,128)(2,1)S(1)}, u32[]{:S(2)}, u32[]{:S(2)}) collective-permute-start(bf16[4512,128]{1,0:T(8,128)(2,1)S(1)} %constant_dynamic-update-slice_fusion.mine_ref), channel_id=1, source_target_pairs={{0,8},{8,0},{1,9},{9,1},{2,10},{10,2},{3,11},{11,3},{4,12},{12,4},... | collective-permute-start | bytes 3465224 | tf_op jit(solution)/shard_map/ppermute | solution.py:158
  81.6 1.7 %collective-permute-done.8.theirs_ref = bf16[4512,128]{1,0:T(8,128)(2,1)S(1)} collective-permute-done((bf16[4512,128]{1,0:T(8,128)(2,1)S(1)}, bf16[4512,128]{1,0:T(8,128)(2,1)S(1)}, u32[]{:S(2)}, u32[]{:S(2)}) %collective-permute-start.8) | collective-permute-done | bytes 1155104 | tf_op jit(solution)/shard_map/ppermute | solution.py:158
  83.4 2.9 %attention.1 = bf16[512,128]{1,0:T(8,128)(2,1)} custom-call(bf16[16,104,128]{2,1,0:T(8,128)(2,1)S(1)} %all-to-all-done.q_ref, bf16[4512,128]{1,0:T(8,128)(2,1)S(1)} %constant_dynamic-update-slice_fusion.mine_ref, bf16[4512,128]{1,0:T(8,128)(2,1)S(1)} %collective-permute-done.8.theirs_ref, f32[512,1]{1,0:T(8,128)S(1)} %reshape.489.qid_ref), custom_call_target="tpu_custom_call" | custom-call | flops 536870912 | bytes 1048576 | tf_op jit(solution)/shard_map/attention/pallas_call | solution.py:320
  86.2 4.0 %convolution.15 = bf16[4,384,128]{2,1,0:T(8,128)(2,1)S(1)} custom-call(s32[10]{0:T(128)S(1)} %pad_add_fusion.place_ref, bf16[4512,128]{1,0:T(8,128)(2,1)S(1)} %constant_dynamic-update-slice_fusion.mine_ref, bf16[4512,128]{1,0:T(8,128)(2,1)S(1)} %collective-permute-done.8.theirs_ref, bf16[1152,128]{1,0:T(8,128)(2,1)S(1)} %maximum_maximum_fusion.refs_0_, ...), custom_call_target="tpu_custom_call" | custom-call | flops 2147483648 | bytes 1327104 | tf_op jit(solution)/shard_map/convolution/pallas_call | solution.py:334
  90.3 3.8 %collective-permute-start.9 = (bf16[2,384,128]{2,1,0:T(8,128)(2,1)S(1)}, bf16[2,384,128]{2,1,0:T(8,128)(2,1)S(1)}, u32[]{:S(2)}, u32[]{:S(2)}) collective-permute-start(bf16[2,384,128]{2,1,0:T(8,128)(2,1)S(1)} %slice.220), channel_id=1, source_target_pairs={{0,2},{1,3},{2,0},{3,1},{4,6},{5,7},{6,4},{7,5},{8,10},{9,11},{10,... | collective-permute-start | bytes 589832 | tf_op jit(solution)/shard_map/ppermute | solution.py:162
  94.0 8.3 %all-to-all-start.2 = ((bf16[16,32,128]{2,1,0:T(8,128)(2,1)}), bf16[16,32,128]{2,1,0:T(8,128)(2,1)S(1)}, u32[]{:S(2)}, u32[]{:S(2)}) async-start(bf16[16,32,128]{2,1,0:T(8,128)(2,1)} %bitcast.32), calls=%async_computation.2 | async-start | bytes 262144 | tf_op jit(solution)/shard_map/all_to_all | solution.py:171
  102.3 1.7 %collective-permute-done.9 = bf16[2,384,128]{2,1,0:T(8,128)(2,1)S(1)} collective-permute-done((bf16[2,384,128]{2,1,0:T(8,128)(2,1)S(1)}, bf16[2,384,128]{2,1,0:T(8,128)(2,1)S(1)}, u32[]{:S(2)}, u32[]{:S(2)}) %collective-permute-start.9) | collective-permute-done | bytes 196640 | tf_op jit(solution)/shard_map/ppermute | solution.py:162
  104.1 1.9 %collective-permute-start.10 = (bf16[384,128]{1,0:T(8,128)(2,1)S(1)}, bf16[384,128]{1,0:T(8,128)(2,1)S(1)}, u32[]{:S(2)}, u32[]{:S(2)}) collective-permute-start(bf16[384,128]{1,0:T(8,128)(2,1)S(1)} %fusion.34), channel_id=1, source_target_pairs={{0,1},{1,0},{2,3},{3,2},{4,5},{5,4},{6,7},{7,6},{8,9},{9,8},{10,11... | collective-permute-start | bytes 294920 | tf_op jit(solution)/shard_map/ppermute | solution.py:162
  106.0 3.8 %all-to-all-done.2 = bf16[16,32,128]{2,1,0:T(8,128)(2,1)S(1)} async-done(((bf16[16,32,128]{2,1,0:T(8,128)(2,1)}), bf16[16,32,128]{2,1,0:T(8,128)(2,1)S(1)}, u32[]{:S(2)}, u32[]{:S(2)}) %all-to-all-start.2) | async-done | bytes 131104 | tf_op jit(solution)/shard_map/all_to_all | solution.py:171
  110.7 4.0 %collective-permute-start.11 = (bf16[128,192]{1,0:T(8,128)(2,1)S(1)}, bf16[128,192]{1,0:T(8,128)(2,1)S(1)}, u32[]{:S(2)}, u32[]{:S(2)}) collective-permute-start(bf16[128,192]{1,0:T(8,128)(2,1)S(1)} %fusion.37), channel_id=1, source_target_pairs={{0,8},{8,0},{1,9},{9,1},{2,10},{10,2},{3,11},{11,3},{4,12},{12,4},... | collective-permute-start | bytes 147464 | tf_op jit(solution)/shard_map/ppermute | solution.py:158
  (137 shorter events, 16.8 us)
Async XLA Ops:
  0.6 25.7 %copy-start = (bf16[32,2048]{1,0:T(8,128)(2,1)S(1)}, bf16[32,2048]{1,0:T(8,128)(2,1)}, u32[]{:S(2)}) copy-start(bf16[32,2048]{1,0:T(8,128)(2,1)} %param.12) | copy-start | bytes 393220
  0.6 25.6 %copy-start.8 = (bf16[1,2,64,384]{3,2,1,0:T(8,128)(2,1)S(1)}, bf16[1,2,64,384]{3,2,1,0:T(8,128)(2,1)}, u32[]{:S(2)}) copy-start(bf16[1,2,64,384]{3,2,1,0:T(8,128)(2,1)} %param.16) | copy-start | bytes 294916
  4.5 23.2 %collective-permute-start = (bf16[24,128]{1,0:T(8,128)(2,1)S(1)}, bf16[24,128]{1,0:T(8,128)(2,1)S(1)}, u32[]{:S(2)}, u32[]{:S(2)}) collective-permute-start(bf16[24,128]{1,0:T(8,128)(2,1)S(1)} %fusion.66), channel_id=1, source_target_pairs={{0,4},{4,0},{1,5},{5,1},{2,6},{6,2},{3,7},{7,3},{8,12},{12,8},{9,1... | collective-permute-start | bytes 18440 | tf_op jit(solution)/shard_map/ppermute | solution.py:158
  13.9 13.0 %copy-start.14 = (f32[384]{0:T(512)S(1)}, f32[384]{0:T(512)}, u32[]{:S(2)}) copy-start(f32[384]{0:T(512)} %param.18) | copy-start | bytes 4612
  14.1 12.9 %copy-start.11 = (bf16[2,2,64,384]{3,2,1,0:T(8,128)(2,1)S(1)}, bf16[2,2,64,384]{3,2,1,0:T(8,128)(2,1)}, u32[]{:S(2)}) copy-start(bf16[2,2,64,384]{3,2,1,0:T(8,128)(2,1)} %param.17) | copy-start | bytes 589828
  14.9 26.1 %all-to-all-start.1 = ((bf16[16,72,128]{2,1,0:T(8,128)(2,1)}), bf16[16,72,128]{2,1,0:T(8,128)(2,1)S(1)}, u32[]{:S(2)}, u32[]{:S(2)}) async-start(bf16[16,72,128]{2,1,0:T(8,128)(2,1)} %bitcast.18), calls=%async_computation.1 | async-start | bytes 589824 | tf_op jit(solution)/shard_map/all_to_all | solution.py:171
  29.3 8.4 %collective-permute-start.5 = (bf16[2,400,128]{2,0,1:T(2,128)(2,1)S(1)}, bf16[2,400,128]{2,0,1:T(2,128)(2,1)S(1)}, u32[]{:S(2)}, u32[]{:S(2)}) collective-permute-start(bf16[2,400,128]{2,0,1:T(2,128)(2,1)S(1)} %fusion.15), channel_id=1, source_target_pairs={{0,1},{1,0},{2,3},{3,2},{4,5},{5,4},{6,7},{7,6},{8,9},{9,8},{10,11... | collective-permute-start | bytes 614408 | tf_op jit(solution)/shard_map/ppermute | solution.py:162
  38.6 15.4 %collective-permute-start.6 = (bf16[2,400,128]{2,0,1:T(2,128)(2,1)S(1)}, bf16[2,400,128]{2,0,1:T(2,128)(2,1)S(1)}, u32[]{:S(2)}, u32[]{:S(2)}) collective-permute-start(bf16[2,400,128]{2,0,1:T(2,128)(2,1)S(1)} %fusion.18), channel_id=1, source_target_pairs={{0,2},{1,3},{2,0},{3,1},{4,6},{5,7},{6,4},{7,5},{8,10},{9,11},{10,... | collective-permute-start | bytes 614408 | tf_op jit(solution)/shard_map/ppermute | solution.py:162
  41.1 21.0 %all-to-all-start = ((bf16[16,104,128]{2,1,0:T(8,128)(2,1)}), bf16[16,104,128]{2,1,0:T(8,128)(2,1)S(1)}, u32[]{:S(2)}, u32[]{:S(2)}) async-start(bf16[16,104,128]{2,1,0:T(8,128)(2,1)} %pad_maximum_fusion), calls=%async_computation | async-start | bytes 851968 | tf_op jit(solution)/shard_map/all_to_all | solution.py:171
  50.7 11.4 %collective-permute-start.1 = (bf16[1152,128]{1,0:T(8,128)(2,1)S(1)}, bf16[1152,128]{1,0:T(8,128)(2,1)S(1)}, u32[]{:S(2)}, u32[]{:S(2)}) collective-permute-start(bf16[1152,128]{1,0:T(8,128)(2,1)S(1)} %maximum_maximum_fusion.refs_0_), channel_id=1, source_target_pairs={{0,128},{128,256},{256,384},{384,0},{1,129},{129,257},{257,385},{3... | collective-permute-start | bytes 884744 | tf_op jit(solution)/shard_map/ppermute | solution.py:158
  55.7 17.9 %collective-permute-start.3 = (bf16[1152,128]{1,0:T(8,128)(2,1)S(1)}, bf16[1152,128]{1,0:T(8,128)(2,1)S(1)}, u32[]{:S(2)}, u32[]{:S(2)}) collective-permute-start(bf16[1152,128]{1,0:T(8,128)(2,1)S(1)} %maximum_maximum_fusion.refs_0_), channel_id=1, source_target_pairs={{0,384},{128,0},{256,128},{384,256},{1,385},{129,1},{257,129},{385... | collective-permute-start | bytes 884744 | tf_op jit(solution)/shard_map/ppermute | solution.py:158
  58.9 14.7 %collective-permute-start.4 = (bf16[1152,128]{1,0:T(8,128)(2,1)S(1)}, bf16[1152,128]{1,0:T(8,128)(2,1)S(1)}, u32[]{:S(2)}, u32[]{:S(2)}) collective-permute-start(bf16[1152,128]{1,0:T(8,128)(2,1)S(1)} %maximum_maximum_fusion.refs_0_), channel_id=1, source_target_pairs={{0,256},{128,384},{256,0},{384,128},{1,257},{129,385},{257,1},{385... | collective-permute-start | bytes 884744 | tf_op jit(solution)/shard_map/ppermute | solution.py:158
  62.8 4.0 %copy-start.7 = (bf16[4,384,128]{2,0,1:T(4,128)(2,1)S(1)}, bf16[4,384,128]{2,0,1:T(4,128)(2,1)}, u32[]{:S(2)}) copy-start(bf16[4,384,128]{2,0,1:T(4,128)(2,1)} %slice.213) | copy-start | bytes 1179652
  62.9 14.2 %collective-permute-start.2 = (bf16[1040,128]{1,0:T(8,128)(2,1)S(1)}, bf16[1040,128]{1,0:T(8,128)(2,1)S(1)}, u32[]{:S(2)}, u32[]{:S(2)}) collective-permute-start(bf16[1040,128]{1,0:T(8,128)(2,1)S(1)} %pad_maximum_fusion.3), channel_id=1, source_target_pairs={{0,256},{256,0},{1,257},{257,1},{2,258},{258,2},{3,259},{259,3},{4... | collective-permute-start | bytes 798728 | tf_op jit(solution)/shard_map/ppermute | solution.py:158
  67.0 10.4 %collective-permute-start.7 = (bf16[4,208,128]{2,1,0:T(8,128)(2,1)S(1)}, bf16[4,208,128]{2,1,0:T(8,128)(2,1)S(1)}, u32[]{:S(2)}, u32[]{:S(2)}) collective-permute-start(bf16[4,208,128]{2,1,0:T(8,128)(2,1)S(1)} %fusion.14), channel_id=1, source_target_pairs={{8,16},{16,8},{24,32},{32,24},{40,48},{48,40},{56,64},{64,56},{72,... | collective-permute-start | bytes 638984 | tf_op jit(solution)/shard_map/ppermute | solution.py:303
  73.6 3.8 %copy-start.3 = (bf16[1152,128]{1,0:T(8,128)(2,1)}, bf16[1152,128]{1,0:T(8,128)(2,1)S(1)}, u32[]{:S(2)}) copy-start(bf16[1152,128]{1,0:T(8,128)(2,1)S(1)} %collective-permute-done.3.refs_2_) | copy-start | bytes 884740
  77.4 5.9 %collective-permute-start.8 = (bf16[4512,128]{1,0:T(8,128)(2,1)S(1)}, bf16[4512,128]{1,0:T(8,128)(2,1)S(1)}, u32[]{:S(2)}, u32[]{:S(2)}) collective-permute-start(bf16[4512,128]{1,0:T(8,128)(2,1)S(1)} %constant_dynamic-update-slice_fusion.mine_ref), channel_id=1, source_target_pairs={{0,8},{8,0},{1,9},{9,1},{2,10},{10,2},{3,11},{11,3},{4,12},{12,4},... | collective-permute-start | bytes 3465224 | tf_op jit(solution)/shard_map/ppermute | solution.py:158
  81.6 4.6 %copy-start.2 = (bf16[1152,128]{1,0:T(8,128)(2,1)S(1)}, bf16[1152,128]{1,0:T(8,128)(2,1)}, u32[]{:S(2)}) copy-start(bf16[1152,128]{1,0:T(8,128)(2,1)} %copy-done.1) | copy-start | bytes 884740
  81.6 4.6 %copy-start.4 = (bf16[1152,128]{1,0:T(8,128)(2,1)S(1)}, bf16[1152,128]{1,0:T(8,128)(2,1)}, u32[]{:S(2)}) copy-start(bf16[1152,128]{1,0:T(8,128)(2,1)} %copy-done.3) | copy-start | bytes 884740
  81.6 4.6 %copy-start.6 = (bf16[1152,128]{1,0:T(8,128)(2,1)S(1)}, bf16[1152,128]{1,0:T(8,128)(2,1)}, u32[]{:S(2)}) copy-start(bf16[1152,128]{1,0:T(8,128)(2,1)} %copy-done.5) | copy-start | bytes 884740
  90.3 13.7 %collective-permute-start.9 = (bf16[2,384,128]{2,1,0:T(8,128)(2,1)S(1)}, bf16[2,384,128]{2,1,0:T(8,128)(2,1)S(1)}, u32[]{:S(2)}, u32[]{:S(2)}) collective-permute-start(bf16[2,384,128]{2,1,0:T(8,128)(2,1)S(1)} %slice.220), channel_id=1, source_target_pairs={{0,2},{1,3},{2,0},{3,1},{4,6},{5,7},{6,4},{7,5},{8,10},{9,11},{10,... | collective-permute-start | bytes 589832 | tf_op jit(solution)/shard_map/ppermute | solution.py:162
  94.0 15.7 %all-to-all-start.2 = ((bf16[16,32,128]{2,1,0:T(8,128)(2,1)}), bf16[16,32,128]{2,1,0:T(8,128)(2,1)S(1)}, u32[]{:S(2)}, u32[]{:S(2)}) async-start(bf16[16,32,128]{2,1,0:T(8,128)(2,1)} %bitcast.32), calls=%async_computation.2 | async-start | bytes 262144 | tf_op jit(solution)/shard_map/all_to_all | solution.py:171
  104.1 6.4 %collective-permute-start.10 = (bf16[384,128]{1,0:T(8,128)(2,1)S(1)}, bf16[384,128]{1,0:T(8,128)(2,1)S(1)}, u32[]{:S(2)}, u32[]{:S(2)}) collective-permute-start(bf16[384,128]{1,0:T(8,128)(2,1)S(1)} %fusion.34), channel_id=1, source_target_pairs={{0,1},{1,0},{2,3},{3,2},{4,5},{5,4},{6,7},{7,6},{8,9},{9,8},{10,11... | collective-permute-start | bytes 294920 | tf_op jit(solution)/shard_map/ppermute | solution.py:162
  110.7 4.9 %collective-permute-start.11 = (bf16[128,192]{1,0:T(8,128)(2,1)S(1)}, bf16[128,192]{1,0:T(8,128)(2,1)S(1)}, u32[]{:S(2)}, u32[]{:S(2)}) collective-permute-start(bf16[128,192]{1,0:T(8,128)(2,1)S(1)} %fusion.37), channel_id=1, source_target_pairs={{0,8},{8,0},{1,9},{9,1},{2,10},{10,2},{3,11},{11,3},{4,12},{12,4},... | collective-permute-start | bytes 147464 | tf_op jit(solution)/shard_map/ppermute | solution.py:158
  (7 other events, 9.4 us)

commit v6 on v4

--- a/solution.py
+++ b/solution.py
@@ -273,8 +273,8 @@
     )
     weights = (my_weight,) + planes_of(my_weight)
     taps = (27 * order) // planes
-    got, before = lax.optimization_barrier((got, weights[1]))
-    weights = (weights[0], before) + weights[2:]
+    got, after = lax.optimization_barrier((got, weights[2]))
+    weights = weights[:2] + (after, weights[3])
 
     feat_f = features.astype(F32)
     stacked = jnp.concatenate([frame_cache, activate(features, feat_gain)], axis=0)

time: 113 us -> 117 us (1.035)
  waiting for transfers between devices: 13 us -> 19.5 us
  starting transfers between devices: 75.7 us -> 72.5 us
    ppermute x10, waiting for transfers between devices: 6.69 us -> 11.8 us  [ring(): lax.ppermute(data, axis, [(i, (i + by) % count) for i in range(count)])]
    ppermute x2, waiting for transfers between devices: 1.79 us -> 6.06 us  [swap(): lax.ppermute(data, axis, [(i, i ^ bit) for i in range(lax.axis_size(axis))])]
    all_to_all x3, starting transfers between devices: 25.2 us -> 22.6 us  [exchange(): return lax.all_to_all(data, axes, split_axis=0, concat_axis=0, tiled=True)]
    all_to_all x3, waiting for transfers between devices: 4.21 us -> 1.65 us  [exchange(): return lax.all_to_all(data, axes, split_axis=0, concat_axis=0, tiled=True)]
  transfers between devices with their start and end apart: 16 -> 16, of which waited for: 8 -> 8; matrix products, arithmetic and copies ran while one was open for 9% -> 8% of each run, Pallas kernels for 0% -> 0%
where the time goes in v6:
time: 117 us; the launch traced here: 116 us
  starting transfers between devices  72.5 us (62%)
  waiting for transfers between devices  19.5 us (17%)
  Pallas kernels  6.88 us (6%)
  other arithmetic  6.52 us (6%)
  local copies, waits for them, and re-layouts  4.98 us (4%)
  matrix products  3.78 us (3%)
  between operations  1.5 us (1%)
    ppermute x10, starting transfers between devices, ring(): lax.ppermute(data, axis, [(i, (i + by) % count) for i in range(count)])  38.1 us
    all_to_all x3, starting transfers between devices, exchange(): return lax.all_to_all(data, axes, split_axis=0, concat_axis=0, tiled=True)  22.6 us
    ppermute x10, waiting for transfers between devices, ring(): lax.ppermute(data, axis, [(i, (i + by) % count) for i in range(count)])  11.8 us
    ppermute x2, starting transfers between devices, swap(): lax.ppermute(data, axis, [(i, i ^ bit) for i in range(lax.axis_size(axis))])  6.34 us
    ppermute x2, waiting for transfers between devices, swap(): lax.ppermute(data, axis, [(i, i ^ bit) for i in range(lax.axis_size(axis))])  6.06 us
    ppermute x1, starting transfers between devices, shards(): beyond = lax.ppermute(outer, SEQ, steps)  5.41 us
    pallas_call x1, Pallas kernels, shards(): pl.pallas_call(functools.partial(conv_kernel, share, sizes), out_shape=ja...  4.02 us
    pallas_call x1, Pallas kernels, shards(): pl.pallas_call(functools.partial(attention_kernel, tok, sizes[0]), out_sh...  2.86 us
  transfers between devices with their start and end apart: 16, of which 8 were waited for; matrix products, arithmetic and copies ran while one was open for 8% of the time, Pallas kernels for 0%

profile of v6, /device:TPU:1, one launch (start us, length us, event | category | flops | bytes accessed | tf_op | source)
XLA Modules:
  0.0 115.6 jit_solution(13707551874862123902)
XLA Ops:
  4.4 8.3 %collective-permute-start = (bf16[24,128]{1,0:T(8,128)(2,1)S(1)}, bf16[24,128]{1,0:T(8,128)(2,1)S(1)}, u32[]{:S(2)}, u32[]{:S(2)}) collective-permute-start(bf16[24,128]{1,0:T(8,128)(2,1)S(1)} %fusion.68), channel_id=1, source_target_pairs={{0,4},{4,0},{1,5},{5,1},{2,6},{6,2},{3,7},{7,3},{8,12},{12,8},{9,1... | collective-permute-start | bytes 18440 | tf_op jit(solution)/shard_map/ppermute | solution.py:158
  14.9 11.3 %all-to-all-start.1 = ((bf16[16,72,128]{2,1,0:T(8,128)(2,1)}), bf16[16,72,128]{2,1,0:T(8,128)(2,1)S(1)}, u32[]{:S(2)}, u32[]{:S(2)}) async-start(bf16[16,72,128]{2,1,0:T(8,128)(2,1)} %bitcast.18), calls=%async_computation.1 | async-start | bytes 589824 | tf_op jit(solution)/shard_map/all_to_all | solution.py:171
  28.8 2.5 %collective-permute-start.7 = (bf16[400,128]{1,0:T(8,128)(2,1)S(1)}, bf16[400,128]{1,0:T(8,128)(2,1)S(1)}, u32[]{:S(2)}, u32[]{:S(2)}) collective-permute-start(bf16[400,128]{1,0:T(8,128)(2,1)S(1)} %get-tuple-element.22), channel_id=1, source_target_pairs={{0,3},{1,0},{2,1},{3,2},{4,7},{5,4},{6,5},{7,6},{8,11},{9,8},{10,9... | collective-permute-start | bytes 307208 | tf_op jit(solution)/shard_map/ppermute | solution.py:158
  31.4 2.9 %collective-permute-start.6 = (bf16[400,128]{1,0:T(8,128)(2,1)S(1)}, bf16[400,128]{1,0:T(8,128)(2,1)S(1)}, u32[]{:S(2)}, u32[]{:S(2)}) collective-permute-start(bf16[400,128]{1,0:T(8,128)(2,1)S(1)} %get-tuple-element.23), channel_id=1, source_target_pairs={{0,2},{1,3},{2,0},{3,1},{4,6},{5,7},{6,4},{7,5},{8,10},{9,11},{10,... | collective-permute-start | bytes 307208 | tf_op jit(solution)/shard_map/ppermute | solution.py:158
  34.2 2.3 %collective-permute-start.5 = (bf16[400,128]{1,0:T(8,128)(2,1)S(1)}, bf16[400,128]{1,0:T(8,128)(2,1)S(1)}, u32[]{:S(2)}, u32[]{:S(2)}) collective-permute-start(bf16[400,128]{1,0:T(8,128)(2,1)S(1)} %get-tuple-element.21), channel_id=1, source_target_pairs={{0,1},{1,2},{2,3},{3,0},{4,5},{5,6},{6,7},{7,4},{8,9},{9,10},{10,1... | collective-permute-start | bytes 307208 | tf_op jit(solution)/shard_map/ppermute | solution.py:158
  37.3 1.2 %all-to-all-done.1 = bf16[16,72,128]{2,1,0:T(8,128)(2,1)S(1)} async-done(((bf16[16,72,128]{2,1,0:T(8,128)(2,1)}), bf16[16,72,128]{2,1,0:T(8,128)(2,1)S(1)}, u32[]{:S(2)}, u32[]{:S(2)}) %all-to-all-start.1) | async-done | bytes 294944 | tf_op jit(solution)/shard_map/all_to_all | solution.py:171
  38.6 6.4 %all-to-all-start = ((bf16[16,104,128]{2,1,0:T(8,128)(2,1)}), bf16[16,104,128]{2,1,0:T(8,128)(2,1)S(1)}, u32[]{:S(2)}, u32[]{:S(2)}) async-start(bf16[16,104,128]{2,1,0:T(8,128)(2,1)} %pad_maximum_fusion), calls=%async_computation | async-start | bytes 851968 | tf_op jit(solution)/shard_map/all_to_all | solution.py:171
  47.2 4.5 %collective-permute-start.1 = (bf16[1152,128]{1,0:T(8,128)(2,1)S(1)}, bf16[1152,128]{1,0:T(8,128)(2,1)S(1)}, u32[]{:S(2)}, u32[]{:S(2)}) collective-permute-start(bf16[1152,128]{1,0:T(8,128)(2,1)S(1)} %maximum_maximum_fusion.refs_0_), channel_id=1, source_target_pairs={{0,384},{128,0},{256,128},{384,256},{1,385},{129,1},{257,129},{385... | collective-permute-start | bytes 884744 | tf_op jit(solution)/shard_map/ppermute | solution.py:158
  52.7 1.9 %collective-permute-start.3 = (bf16[1152,128]{1,0:T(8,128)(2,1)S(1)}, bf16[1152,128]{1,0:T(8,128)(2,1)S(1)}, u32[]{:S(2)}, u32[]{:S(2)}) collective-permute-start(bf16[1152,128]{1,0:T(8,128)(2,1)S(1)} %maximum_maximum_fusion.refs_0_), channel_id=1, source_target_pairs={{0,128},{128,256},{256,384},{384,0},{1,129},{129,257},{257,385},{3... | collective-permute-start | bytes 884744 | tf_op jit(solution)/shard_map/ppermute | solution.py:158
  54.6 3.2 %collective-permute-start.4 = (bf16[1152,128]{1,0:T(8,128)(2,1)S(1)}, bf16[1152,128]{1,0:T(8,128)(2,1)S(1)}, u32[]{:S(2)}, u32[]{:S(2)}) collective-permute-start(bf16[1152,128]{1,0:T(8,128)(2,1)S(1)} %maximum_maximum_fusion.refs_0_), channel_id=1, source_target_pairs={{0,256},{128,384},{256,0},{384,128},{1,257},{129,385},{257,1},{385... | collective-permute-start | bytes 884744 | tf_op jit(solution)/shard_map/ppermute | solution.py:158
  57.8 2.9 %collective-permute-done.1.refs_2_ = bf16[1152,128]{1,0:T(8,128)(2,1)S(1)} collective-permute-done((bf16[1152,128]{1,0:T(8,128)(2,1)S(1)}, bf16[1152,128]{1,0:T(8,128)(2,1)S(1)}, u32[]{:S(2)}, u32[]{:S(2)}) %collective-permute-start.1) | collective-permute-done | bytes 294944 | tf_op jit(solution)/shard_map/ppermute | solution.py:158
  61.5 4.5 %collective-permute-start.2 = (bf16[1040,128]{1,0:T(8,128)(2,1)S(1)}, bf16[1040,128]{1,0:T(8,128)(2,1)S(1)}, u32[]{:S(2)}, u32[]{:S(2)}) collective-permute-start(bf16[1040,128]{1,0:T(8,128)(2,1)S(1)} %pad_maximum_fusion.3), channel_id=1, source_target_pairs={{0,256},{256,0},{1,257},{257,1},{2,258},{258,2},{3,259},{259,3},{4... | collective-permute-start | bytes 798728 | tf_op jit(solution)/shard_map/ppermute | solution.py:158
  66.0 5.4 %collective-permute-start.8 = (bf16[4,208,128]{2,1,0:T(8,128)(2,1)S(1)}, bf16[4,208,128]{2,1,0:T(8,128)(2,1)S(1)}, u32[]{:S(2)}, u32[]{:S(2)}) collective-permute-start(bf16[4,208,128]{2,1,0:T(8,128)(2,1)S(1)} %fusion.14), channel_id=1, source_target_pairs={{8,16},{16,8},{24,32},{32,24},{40,48},{48,40},{56,64},{64,56},{72,... | collective-permute-start | bytes 638984 | tf_op jit(solution)/shard_map/ppermute | solution.py:301
  71.5 6.2 %collective-permute-done.2 = bf16[1040,128]{1,0:T(8,128)(2,1)S(1)} collective-permute-done((bf16[1040,128]{1,0:T(8,128)(2,1)S(1)}, bf16[1040,128]{1,0:T(8,128)(2,1)S(1)}, u32[]{:S(2)}, u32[]{:S(2)}) %collective-permute-start.2) | collective-permute-done | bytes 266272 | tf_op jit(solution)/shard_map/ppermute | solution.py:158
  77.8 3.7 %collective-permute-start.9 = (bf16[4512,128]{1,0:T(8,128)(2,1)S(1)}, bf16[4512,128]{1,0:T(8,128)(2,1)S(1)}, u32[]{:S(2)}, u32[]{:S(2)}) collective-permute-start(bf16[4512,128]{1,0:T(8,128)(2,1)S(1)} %constant_dynamic-update-slice_fusion.mine_ref), channel_id=1, source_target_pairs={{0,8},{8,0},{1,9},{9,1},{2,10},{10,2},{3,11},{11,3},{4,12},{12,4},... | collective-permute-start | bytes 3465224 | tf_op jit(solution)/shard_map/ppermute | solution.py:158
  82.0 1.9 %collective-permute-done.9.theirs_ref = bf16[4512,128]{1,0:T(8,128)(2,1)S(1)} collective-permute-done((bf16[4512,128]{1,0:T(8,128)(2,1)S(1)}, bf16[4512,128]{1,0:T(8,128)(2,1)S(1)}, u32[]{:S(2)}, u32[]{:S(2)}) %collective-permute-start.9) | collective-permute-done | bytes 1155104 | tf_op jit(solution)/shard_map/ppermute | solution.py:158
  83.9 2.9 %attention.1 = bf16[512,128]{1,0:T(8,128)(2,1)} custom-call(bf16[16,104,128]{2,1,0:T(8,128)(2,1)S(1)} %all-to-all-done.q_ref, bf16[4512,128]{1,0:T(8,128)(2,1)S(1)} %constant_dynamic-update-slice_fusion.mine_ref, bf16[4512,128]{1,0:T(8,128)(2,1)S(1)} %collective-permute-done.9.theirs_ref, f32[512,1]{1,0:T(8,128)S(1)} %reshape.472.qid_ref), custom_call_target="tpu_custom_call" | custom-call | flops 536870912 | bytes 1048576 | tf_op jit(solution)/shard_map/attention/pallas_call | solution.py:318
  86.8 4.0 %convolution.19 = bf16[4,384,128]{2,1,0:T(8,128)(2,1)S(1)} custom-call(s32[10]{0:T(128)S(1)} %pad_add_fusion.place_ref, bf16[4512,128]{1,0:T(8,128)(2,1)S(1)} %constant_dynamic-update-slice_fusion.mine_ref, bf16[4512,128]{1,0:T(8,128)(2,1)S(1)} %collective-permute-done.9.theirs_ref, bf16[1152,128]{1,0:T(8,128)(2,1)S(1)} %maximum_maximum_fusion.refs_0_, ...), custom_call_target="tpu_custom_call" | custom-call | flops 2147483648 | bytes 1327104 | tf_op jit(solution)/shard_map/convolution/pallas_call | solution.py:332
  90.9 3.8 %collective-permute-start.10 = (bf16[2,384,128]{2,1,0:T(8,128)(2,1)S(1)}, bf16[2,384,128]{2,1,0:T(8,128)(2,1)S(1)}, u32[]{:S(2)}, u32[]{:S(2)}) collective-permute-start(bf16[2,384,128]{2,1,0:T(8,128)(2,1)S(1)} %slice.216), channel_id=1, source_target_pairs={{0,2},{1,3},{2,0},{3,1},{4,6},{5,7},{6,4},{7,5},{8,10},{9,11},{10,... | collective-permute-start | bytes 589832 | tf_op jit(solution)/shard_map/ppermute | solution.py:162
  94.6 5.0 %all-to-all-start.2 = ((bf16[16,32,128]{2,1,0:T(8,128)(2,1)}), bf16[16,32,128]{2,1,0:T(8,128)(2,1)S(1)}, u32[]{:S(2)}, u32[]{:S(2)}) async-start(bf16[16,32,128]{2,1,0:T(8,128)(2,1)} %bitcast.38), calls=%async_computation.2 | async-start | bytes 262144 | tf_op jit(solution)/shard_map/all_to_all | solution.py:171
  99.6 4.4 %collective-permute-done.10 = bf16[2,384,128]{2,1,0:T(8,128)(2,1)S(1)} collective-permute-done((bf16[2,384,128]{2,1,0:T(8,128)(2,1)S(1)}, bf16[2,384,128]{2,1,0:T(8,128)(2,1)S(1)}, u32[]{:S(2)}, u32[]{:S(2)}) %collective-permute-start.10) | collective-permute-done | bytes 196640 | tf_op jit(solution)/shard_map/ppermute | solution.py:162
  104.0 2.6 %collective-permute-start.11 = (bf16[384,128]{1,0:T(8,128)(2,1)S(1)}, bf16[384,128]{1,0:T(8,128)(2,1)S(1)}, u32[]{:S(2)}, u32[]{:S(2)}) collective-permute-start(bf16[384,128]{1,0:T(8,128)(2,1)S(1)} %fusion.36), channel_id=1, source_target_pairs={{0,1},{1,0},{2,3},{3,2},{4,5},{5,4},{6,7},{7,6},{8,9},{9,8},{10,11... | collective-permute-start | bytes 294920 | tf_op jit(solution)/shard_map/ppermute | solution.py:162
  107.7 1.7 %collective-permute-done.11 = bf16[384,128]{1,0:T(8,128)(2,1)S(1)} collective-permute-done((bf16[384,128]{1,0:T(8,128)(2,1)S(1)}, bf16[384,128]{1,0:T(8,128)(2,1)S(1)}, u32[]{:S(2)}, u32[]{:S(2)}) %collective-permute-start.11) | collective-permute-done | bytes 98336 | tf_op jit(solution)/shard_map/ppermute | solution.py:162
  109.7 4.3 %collective-permute-start.12 = (bf16[128,192]{1,0:T(8,128)(2,1)S(1)}, bf16[128,192]{1,0:T(8,128)(2,1)S(1)}, u32[]{:S(2)}, u32[]{:S(2)}) collective-permute-start(bf16[128,192]{1,0:T(8,128)(2,1)S(1)} %fusion.39), channel_id=1, source_target_pairs={{0,8},{8,0},{1,9},{9,1},{2,10},{10,2},{3,11},{11,3},{4,12},{12,4},... | collective-permute-start | bytes 147464 | tf_op jit(solution)/shard_map/ppermute | solution.py:158
  (134 shorter events, 16.6 us)
Async XLA Ops:
  0.6 25.7 %copy-start = (bf16[32,2048]{1,0:T(8,128)(2,1)S(1)}, bf16[32,2048]{1,0:T(8,128)(2,1)}, u32[]{:S(2)}) copy-start(bf16[32,2048]{1,0:T(8,128)(2,1)} %param.12) | copy-start | bytes 393220
  0.6 25.6 %copy-start.8 = (bf16[1,2,64,384]{3,2,1,0:T(8,128)(2,1)S(1)}, bf16[1,2,64,384]{3,2,1,0:T(8,128)(2,1)}, u32[]{:S(2)}) copy-start(bf16[1,2,64,384]{3,2,1,0:T(8,128)(2,1)} %param.16) | copy-start | bytes 294916
  0.7 25.7 %copy-start.15 = (s32[32]{0:T(128)S(1)}, s32[32]{0:T(128)}, u32[]{:S(2)}) copy-start(s32[32]{0:T(128)} %param.15) | copy-start | bytes 388
  4.4 23.2 %collective-permute-start = (bf16[24,128]{1,0:T(8,128)(2,1)S(1)}, bf16[24,128]{1,0:T(8,128)(2,1)S(1)}, u32[]{:S(2)}, u32[]{:S(2)}) collective-permute-start(bf16[24,128]{1,0:T(8,128)(2,1)S(1)} %fusion.68), channel_id=1, source_target_pairs={{0,4},{4,0},{1,5},{5,1},{2,6},{6,2},{3,7},{7,3},{8,12},{12,8},{9,1... | collective-permute-start | bytes 18440 | tf_op jit(solution)/shard_map/ppermute | solution.py:158
  13.9 13.0 %copy-start.14 = (f32[384]{0:T(512)S(1)}, f32[384]{0:T(512)}, u32[]{:S(2)}) copy-start(f32[384]{0:T(512)} %param.18) | copy-start | bytes 4612
  14.1 13.0 %copy-start.11 = (bf16[2,2,64,384]{3,2,1,0:T(8,128)(2,1)S(1)}, bf16[2,2,64,384]{3,2,1,0:T(8,128)(2,1)}, u32[]{:S(2)}) copy-start(bf16[2,2,64,384]{3,2,1,0:T(8,128)(2,1)} %param.17) | copy-start | bytes 589828
  14.9 23.6 %all-to-all-start.1 = ((bf16[16,72,128]{2,1,0:T(8,128)(2,1)}), bf16[16,72,128]{2,1,0:T(8,128)(2,1)S(1)}, u32[]{:S(2)}, u32[]{:S(2)}) async-start(bf16[16,72,128]{2,1,0:T(8,128)(2,1)} %bitcast.18), calls=%async_computation.1 | async-start | bytes 589824 | tf_op jit(solution)/shard_map/all_to_all | solution.py:171
  28.8 23.0 %collective-permute-start.7 = (bf16[400,128]{1,0:T(8,128)(2,1)S(1)}, bf16[400,128]{1,0:T(8,128)(2,1)S(1)}, u32[]{:S(2)}, u32[]{:S(2)}) collective-permute-start(bf16[400,128]{1,0:T(8,128)(2,1)S(1)} %get-tuple-element.22), channel_id=1, source_target_pairs={{0,3},{1,0},{2,1},{3,2},{4,7},{5,4},{6,5},{7,6},{8,11},{9,8},{10,9... | collective-permute-start | bytes 307208 | tf_op jit(solution)/shard_map/ppermute | solution.py:158
  31.4 20.5 %collective-permute-start.6 = (bf16[400,128]{1,0:T(8,128)(2,1)S(1)}, bf16[400,128]{1,0:T(8,128)(2,1)S(1)}, u32[]{:S(2)}, u32[]{:S(2)}) collective-permute-start(bf16[400,128]{1,0:T(8,128)(2,1)S(1)} %get-tuple-element.23), channel_id=1, source_target_pairs={{0,2},{1,3},{2,0},{3,1},{4,6},{5,7},{6,4},{7,5},{8,10},{9,11},{10,... | collective-permute-start | bytes 307208 | tf_op jit(solution)/shard_map/ppermute | solution.py:158
  34.2 17.6 %collective-permute-start.5 = (bf16[400,128]{1,0:T(8,128)(2,1)S(1)}, bf16[400,128]{1,0:T(8,128)(2,1)S(1)}, u32[]{:S(2)}, u32[]{:S(2)}) collective-permute-start(bf16[400,128]{1,0:T(8,128)(2,1)S(1)} %get-tuple-element.21), channel_id=1, source_target_pairs={{0,1},{1,2},{2,3},{3,0},{4,5},{5,6},{6,7},{7,4},{8,9},{9,10},{10,1... | collective-permute-start | bytes 307208 | tf_op jit(solution)/shard_map/ppermute | solution.py:158
  38.6 19.2 %all-to-all-start = ((bf16[16,104,128]{2,1,0:T(8,128)(2,1)}), bf16[16,104,128]{2,1,0:T(8,128)(2,1)S(1)}, u32[]{:S(2)}, u32[]{:S(2)}) async-start(bf16[16,104,128]{2,1,0:T(8,128)(2,1)} %pad_maximum_fusion), calls=%async_computation | async-start | bytes 851968 | tf_op jit(solution)/shard_map/all_to_all | solution.py:171
  47.2 13.4 %collective-permute-start.1 = (bf16[1152,128]{1,0:T(8,128)(2,1)S(1)}, bf16[1152,128]{1,0:T(8,128)(2,1)S(1)}, u32[]{:S(2)}, u32[]{:S(2)}) collective-permute-start(bf16[1152,128]{1,0:T(8,128)(2,1)S(1)} %maximum_maximum_fusion.refs_0_), channel_id=1, source_target_pairs={{0,384},{128,0},{256,128},{384,256},{1,385},{129,1},{257,129},{385... | collective-permute-start | bytes 884744 | tf_op jit(solution)/shard_map/ppermute | solution.py:158
  52.7 18.7 %collective-permute-start.3 = (bf16[1152,128]{1,0:T(8,128)(2,1)S(1)}, bf16[1152,128]{1,0:T(8,128)(2,1)S(1)}, u32[]{:S(2)}, u32[]{:S(2)}) collective-permute-start(bf16[1152,128]{1,0:T(8,128)(2,1)S(1)} %maximum_maximum_fusion.refs_0_), channel_id=1, source_target_pairs={{0,128},{128,256},{256,384},{384,0},{1,129},{129,257},{257,385},{3... | collective-permute-start | bytes 884744 | tf_op jit(solution)/shard_map/ppermute | solution.py:158
  54.6 16.8 %collective-permute-start.4 = (bf16[1152,128]{1,0:T(8,128)(2,1)S(1)}, bf16[1152,128]{1,0:T(8,128)(2,1)S(1)}, u32[]{:S(2)}, u32[]{:S(2)}) collective-permute-start(bf16[1152,128]{1,0:T(8,128)(2,1)S(1)} %maximum_maximum_fusion.refs_0_), channel_id=1, source_target_pairs={{0,256},{128,384},{256,0},{384,128},{1,257},{129,385},{257,1},{385... | collective-permute-start | bytes 884744 | tf_op jit(solution)/shard_map/ppermute | solution.py:158
  61.5 16.2 %collective-permute-start.2 = (bf16[1040,128]{1,0:T(8,128)(2,1)S(1)}, bf16[1040,128]{1,0:T(8,128)(2,1)S(1)}, u32[]{:S(2)}, u32[]{:S(2)}) collective-permute-start(bf16[1040,128]{1,0:T(8,128)(2,1)S(1)} %pad_maximum_fusion.3), channel_id=1, source_target_pairs={{0,256},{256,0},{1,257},{257,1},{2,258},{258,2},{3,259},{259,3},{4... | collective-permute-start | bytes 798728 | tf_op jit(solution)/shard_map/ppermute | solution.py:158
  66.0 11.7 %collective-permute-start.8 = (bf16[4,208,128]{2,1,0:T(8,128)(2,1)S(1)}, bf16[4,208,128]{2,1,0:T(8,128)(2,1)S(1)}, u32[]{:S(2)}, u32[]{:S(2)}) collective-permute-start(bf16[4,208,128]{2,1,0:T(8,128)(2,1)S(1)} %fusion.14), channel_id=1, source_target_pairs={{8,16},{16,8},{24,32},{32,24},{40,48},{48,40},{56,64},{64,56},{72,... | collective-permute-start | bytes 638984 | tf_op jit(solution)/shard_map/ppermute | solution.py:301
  71.5 6.3 %copy-start.3 = (bf16[1152,128]{1,0:T(8,128)(2,1)}, bf16[1152,128]{1,0:T(8,128)(2,1)S(1)}, u32[]{:S(2)}) copy-start(bf16[1152,128]{1,0:T(8,128)(2,1)S(1)} %collective-permute-done.3.refs_1_) | copy-start | bytes 884740
  71.5 6.3 %copy-start.5 = (bf16[1152,128]{1,0:T(8,128)(2,1)}, bf16[1152,128]{1,0:T(8,128)(2,1)S(1)}, u32[]{:S(2)}) copy-start(bf16[1152,128]{1,0:T(8,128)(2,1)S(1)} %collective-permute-done.4.refs_3_) | copy-start | bytes 884740
  77.8 6.1 %collective-permute-start.9 = (bf16[4512,128]{1,0:T(8,128)(2,1)S(1)}, bf16[4512,128]{1,0:T(8,128)(2,1)S(1)}, u32[]{:S(2)}, u32[]{:S(2)}) collective-permute-start(bf16[4512,128]{1,0:T(8,128)(2,1)S(1)} %constant_dynamic-update-slice_fusion.mine_ref), channel_id=1, source_target_pairs={{0,8},{8,0},{1,9},{9,1},{2,10},{10,2},{3,11},{11,3},{4,12},{12,4},... | collective-permute-start | bytes 3465224 | tf_op jit(solution)/shard_map/ppermute | solution.py:158
  82.0 4.8 %copy-start.2 = (bf16[1152,128]{1,0:T(8,128)(2,1)S(1)}, bf16[1152,128]{1,0:T(8,128)(2,1)}, u32[]{:S(2)}) copy-start(bf16[1152,128]{1,0:T(8,128)(2,1)} %copy-done.1) | copy-start | bytes 884740
  90.9 13.1 %collective-permute-start.10 = (bf16[2,384,128]{2,1,0:T(8,128)(2,1)S(1)}, bf16[2,384,128]{2,1,0:T(8,128)(2,1)S(1)}, u32[]{:S(2)}, u32[]{:S(2)}) collective-permute-start(bf16[2,384,128]{2,1,0:T(8,128)(2,1)S(1)} %slice.216), channel_id=1, source_target_pairs={{0,2},{1,3},{2,0},{3,1},{4,6},{5,7},{6,4},{7,5},{8,10},{9,11},{10,... | collective-permute-start | bytes 589832 | tf_op jit(solution)/shard_map/ppermute | solution.py:162
  94.6 12.4 %all-to-all-start.2 = ((bf16[16,32,128]{2,1,0:T(8,128)(2,1)}), bf16[16,32,128]{2,1,0:T(8,128)(2,1)S(1)}, u32[]{:S(2)}, u32[]{:S(2)}) async-start(bf16[16,32,128]{2,1,0:T(8,128)(2,1)} %bitcast.38), calls=%async_computation.2 | async-start | bytes 262144 | tf_op jit(solution)/shard_map/all_to_all | solution.py:171
  104.0 5.4 %collective-permute-start.11 = (bf16[384,128]{1,0:T(8,128)(2,1)S(1)}, bf16[384,128]{1,0:T(8,128)(2,1)S(1)}, u32[]{:S(2)}, u32[]{:S(2)}) collective-permute-start(bf16[384,128]{1,0:T(8,128)(2,1)S(1)} %fusion.36), channel_id=1, source_target_pairs={{0,1},{1,0},{2,3},{3,2},{4,5},{5,4},{6,7},{7,6},{8,9},{9,8},{10,11... | collective-permute-start | bytes 294920 | tf_op jit(solution)/shard_map/ppermute | solution.py:162
  109.7 5.2 %collective-permute-start.12 = (bf16[128,192]{1,0:T(8,128)(2,1)S(1)}, bf16[128,192]{1,0:T(8,128)(2,1)S(1)}, u32[]{:S(2)}, u32[]{:S(2)}) collective-permute-start(bf16[128,192]{1,0:T(8,128)(2,1)S(1)} %fusion.39), channel_id=1, source_target_pairs={{0,8},{8,0},{1,9},{9,1},{2,10},{10,2},{3,11},{11,3},{4,12},{12,4},... | collective-permute-start | bytes 147464 | tf_op jit(solution)/shard_map/ppermute | solution.py:158
  (8 other events, 18.6 us)
